TPU v7x, 32 devices: a whole 2x2x4 slice. The times are simulated.
32 devices in a mesh: dp: 4 (over z), seq: 2 (over y), tensor: 4 (over x, core).
Axes of the slice: x: 2, y: 2, z: 4, core: 2. Of those that a mesh axis runs over, the one named last changes fastest.
Arguments:
- hidden_in: bfloat16 [8192, 2048], P(('dp', 'seq', 'tensor')), may hold values from -6 to 6
- norm1_gain: bfloat16 [2048], replicated, may hold values from 0.5 to 1.5
- norm1_bias: bfloat16 [2048], replicated, may hold values from -3 to 3
- query_weight: bfloat16 [2048, 2048], P(None, 'tensor'), may hold values from -0.125 to 0.125
- query_bias: bfloat16 [2048], P('tensor'), may hold values from -3 to 3
- key_weight: bfloat16 [2048, 2048], P(None, 'tensor'), may hold values from -0.125 to 0.125
- value_weight: bfloat16 [2048, 2048], P(None, 'tensor'), may hold values from -0.125 to 0.125
- value_bias: bfloat16 [2048], P('tensor'), may hold values from -3 to 3
- out_weight: bfloat16 [2048, 2048], P('tensor'), may hold values from -0.375 to 0.375
- out_bias: bfloat16 [2048], replicated, may hold values from -3 to 3
- norm2_gain: bfloat16 [2048], replicated, may hold values from 0.5 to 1.5
- norm2_bias: bfloat16 [2048], replicated, may hold values from -3 to 3
- up_weight: bfloat16 [2048, 8192], P(None, 'tensor'), may hold values from -0.125 to 0.125
- up_bias: bfloat16 [8192], P('tensor'), may hold values from -3 to 3
- down_weight: bfloat16 [8192, 2048], P('tensor'), may hold values from -0.09375 to 0.09375
- down_bias: bfloat16 [2048], replicated, may hold values from -3 to 3
- seg_lengths: int32 [4, 13], P('dp'), may hold values from 64 to 576, as said below
- parents: int32 [4, 13], P('dp'), may hold values from 0 to 4, as said below
- out_grad: bfloat16 [8192, 2048], P(('dp', 'seq', 'tensor')), may hold values from -6 to 6
Outputs:
- layer_out: bfloat16 [8192, 2048], P(('dp', 'seq', 'tensor'))
- grad_in: bfloat16 [8192, 2048], P(('dp', 'seq', 'tensor'))
- grad_norm1_gain: float32 [2048], replicated
- grad_norm1_bias: float32 [2048], replicated
- grad_query_weight: float32 [2048, 2048], P(None, 'tensor')
- grad_query_bias: float32 [2048], P('tensor')
- grad_key_weight: float32 [2048, 2048], P(None, 'tensor')
- grad_value_weight: float32 [2048, 2048], P(None, 'tensor')
- grad_value_bias: float32 [2048], P('tensor')
- grad_out_weight: float32 [2048, 2048], P('tensor')
- grad_out_bias: float32 [2048], replicated
- grad_norm2_gain: float32 [2048], replicated
- grad_norm2_bias: float32 [2048], replicated
- grad_up_weight: float32 [2048, 8192], P(None, 'tensor')
- grad_up_bias: float32 [8192], P('tensor')
- grad_down_weight: float32 [8192, 2048], P('tensor')
- grad_down_bias: float32 [2048], replicated
Inputs may be any that keep to these rules, and one draw needn't show every extreme that they name: `seg_lengths`: in every slot the 13 lengths sum to 2048; segment 0 (the trunk) comes first and is the longest, then the 4 branches, then the leaves. `parents`: entry 0 is 0 and unused; segments 1 to 4 have parent 0; every later segment has a parent among 1 to 4.
All inputs are finite; a program needn't handle non-finite values.
Results may differ from a plain program's by a relative error of at most 0.02.
Values may be sent and summed in bfloat16 or wider, within the bound.
No kernel may reach another device: no remote copies, remote signals or barrier semaphores. Data moves between devices by JAX's collectives and lax.ppermute only.
A program may use at most 384 MiB of HBM per device.

v0:
```python
from functools import partial

import jax
import jax.numpy as jnp
from jax import lax
from jax.sharding import PartitionSpec as P

HEADS = 32
HD = 64


EPS = 1e-05
NEG = -1e30


def tree_tables(lengths, parent_ids, whole):
    nseg = lengths.shape[0]
    seg_ids = jnp.arange(nseg, dtype=jnp.int32)
    ends = jnp.cumsum(lengths, dtype=jnp.int32)
    starts = ends - lengths
    token = jnp.arange(whole, dtype=jnp.int32)
    segment = jnp.sum((token[:, None] >= ends[None, :]).astype(jnp.int32), axis=1, dtype=jnp.int32)
    link = ((parent_ids[:, None] == seg_ids[None, :]) & (seg_ids[:, None] > 0)).astype(jnp.int32)
    identity = (seg_ids[:, None] == seg_ids[None, :]).astype(jnp.int32)
    ancestor = identity
    for _ in range(nseg):
        ancestor = jnp.minimum(
            identity + jnp.sum(link[:, :, None] * ancestor[None, :, :], axis=1, dtype=jnp.int32), 1
        )
    path_start = jnp.sum((ancestor - identity) * lengths[None, :], axis=1, dtype=jnp.int32)
    onehot = (segment[:, None] == seg_ids[None, :]).astype(jnp.int32)
    depth = token + jnp.sum(onehot * (path_start - starts)[None, :], axis=1, dtype=jnp.int32)
    return (onehot.astype(jnp.float32), ancestor.astype(jnp.float32), depth.astype(jnp.float32))


def norm_forward(values, gain, shift):
    center = values - jnp.mean(values, axis=-1, keepdims=True)
    variance = jnp.mean(center * center, axis=-1, keepdims=True)
    inverse = lax.rsqrt(variance + EPS)
    normed = center * inverse
    return (normed * gain + shift, normed, inverse)


def norm_backward(incoming, normed, inverse, gain):
    scaled = incoming * gain
    inner = (
        scaled
        - jnp.mean(scaled, axis=-1, keepdims=True)
        - normed * jnp.mean(scaled * normed, axis=-1, keepdims=True)
    )
    return (inner * inverse, jnp.sum(incoming * normed, axis=0), jnp.sum(incoming, axis=0))


def dot_first(left, right):
    return lax.dot_general(
        left, right, (((0,), (0,)), ((), ())), preferred_element_type=jnp.float32
    )


def dot_second(left, right):
    return lax.dot_general(
        left, right, (((1,), (1,)), ((), ())), preferred_element_type=jnp.float32
    )


def local(
    hidden_in,
    norm1_gain,
    norm1_bias,
    query_weight,
    query_bias,
    key_weight,
    value_weight,
    value_bias,
    out_weight,
    out_bias,
    norm2_gain,
    norm2_bias,
    up_weight,
    up_bias,
    down_weight,
    down_bias,
    seg_lengths,
    parents,
    out_grad,
):
    local_rows = hidden_in.shape[0]
    tensor_count = lax.axis_size("tensor")
    seq_count = lax.axis_size("seq")
    group = local_rows * tensor_count
    whole = group * seq_count
    columns = query_weight.shape[1]
    local_heads = columns // HD
    scale = HD ** (-0.5)
    block = min(512, group)
    count = group // block
    onehot, ancestor, depth = tree_tables(seg_lengths[0], parents[0], whole)
    reach = jnp.dot(ancestor, onehot.T, precision=lax.Precision.HIGHEST)
    query_base = lax.axis_index("seq") * group
    key_index = jnp.arange(whole, dtype=jnp.int32)
    head_ids = (
        lax.axis_index("tensor") * local_heads + jnp.arange(local_heads, dtype=jnp.int32)
    ).astype(jnp.float32)
    slopes = jnp.exp2(-8.0 * (head_ids + 1.0) / HEADS)
    gain_one = norm1_gain.astype(jnp.float32)
    gain_two = norm2_gain.astype(jnp.float32)
    inputs = hidden_in.astype(jnp.float32)
    first, normed_one, inverse_one = norm_forward(inputs, gain_one, norm1_bias.astype(jnp.float32))
    rows_one = lax.all_gather(first.astype(jnp.bfloat16), "tensor", axis=0, tiled=True)
    queries = (
        jnp.dot(rows_one, query_weight, preferred_element_type=jnp.float32)
        + query_bias.astype(jnp.float32)
    ).astype(jnp.bfloat16)
    keys_own = jnp.dot(rows_one, key_weight, preferred_element_type=jnp.float32).astype(
        jnp.bfloat16
    )
    values_own = (
        jnp.dot(rows_one, value_weight, preferred_element_type=jnp.float32)
        + value_bias.astype(jnp.float32)
    ).astype(jnp.bfloat16)
    keys_all, values_all = (
        lax.all_gather(keys_own, "seq", axis=0, tiled=True),
        lax.all_gather(values_own, "seq", axis=0, tiled=True),
    )
    queries3 = queries.reshape(group, local_heads, HD)

    def block_scores(index, keys3):
        start = index * block
        query_block = lax.dynamic_slice_in_dim(queries3, start, block, 0)
        query_hot = lax.dynamic_slice_in_dim(onehot, query_base + start, block, 0)
        query_depth = lax.dynamic_slice_in_dim(depth, query_base + start, block, 0)
        rows_index = query_base + start + jnp.arange(block, dtype=jnp.int32)
        allowed = (jnp.dot(query_hot, reach, precision=lax.Precision.HIGHEST) > 0.5) & (
            key_index[None, :] <= rows_index[:, None]
        )
        raw = (
            jnp.einsum("bhd,khd->hbk", query_block, keys3, preferred_element_type=jnp.float32)
            * scale
        )
        raw = raw - slopes[:, None, None] * (query_depth[:, None] - depth[None, :])[None]
        return (jnp.where(allowed[None], raw, NEG), query_block)

    keys3 = keys_all.reshape(whole, local_heads, HD)
    values3 = values_all.reshape(whole, local_heads, HD)

    def forward_block(index):
        scores, query_block = block_scores(index, keys3)
        log_total = jax.nn.logsumexp(scores, axis=-1)
        weights = jnp.exp(scores - log_total[..., None]).astype(jnp.bfloat16)
        mixed = jnp.einsum("hbk,khd->bhd", weights, values3, preferred_element_type=jnp.float32)
        return (mixed.reshape(block, columns), log_total)

    mixed_blocks, log_totals = lax.map(forward_block, jnp.arange(count, dtype=jnp.int32))
    heads_out = mixed_blocks.reshape(group, columns).astype(jnp.bfloat16)
    branch = lax.psum_scatter(
        jnp.dot(heads_out, out_weight, preferred_element_type=jnp.float32),
        "tensor",
        scatter_dimension=0,
        tiled=True,
    ) + out_bias.astype(jnp.float32)
    middle = inputs + branch
    second, normed_two, inverse_two = norm_forward(middle, gain_two, norm2_bias.astype(jnp.float32))
    rows_two = lax.all_gather(second.astype(jnp.bfloat16), "tensor", axis=0, tiled=True)
    pre_act = jnp.dot(rows_two, up_weight, preferred_element_type=jnp.float32) + up_bias.astype(
        jnp.float32
    )
    act_full, gelu_pull = jax.vjp(partial(jax.nn.gelu, approximate=False), pre_act)
    activated = act_full.astype(jnp.bfloat16)
    ffn_out = lax.psum_scatter(
        jnp.dot(
            lax.slice_in_dim(activated, 0, lax.axis_size("tensor") * local_rows, axis=0),
            down_weight,
            preferred_element_type=jnp.float32,
        ).astype(jnp.bfloat16),
        "tensor",
        scatter_dimension=0,
        tiled=True,
    ).astype(jnp.float32) + down_bias.astype(jnp.float32)
    layer_out = (middle + ffn_out).astype(jnp.bfloat16)
    cotangent = out_grad.astype(jnp.float32)
    grad_down_bias = jnp.sum(cotangent, axis=0)
    grad_rows = lax.all_gather(out_grad, "tensor", axis=0, tiled=True)
    act_grad = dot_second(grad_rows, down_weight)
    up_grad = gelu_pull(act_grad)[0].astype(jnp.bfloat16)
    grad_down_weight = dot_first(activated, grad_rows)
    grad_up_weight = dot_first(rows_two, up_grad)
    grad_up_bias = jnp.sum(up_grad.astype(jnp.float32), axis=0)
    second_grad = lax.psum_scatter(
        dot_second(up_grad, up_weight).astype(jnp.bfloat16),
        "tensor",
        scatter_dimension=0,
        tiled=True,
    ).astype(jnp.float32)
    middle_part, grad_norm2_gain, grad_norm2_bias = norm_backward(
        second_grad, normed_two, inverse_two, gain_two
    )
    middle_grad = cotangent + middle_part
    branch_grad = middle_grad.astype(jnp.bfloat16)
    grad_out_bias = jnp.sum(branch_grad.astype(jnp.float32), axis=0)
    branch_rows = lax.all_gather(branch_grad, "tensor", axis=0, tiled=True)
    grad_out_weight = dot_first(heads_out, branch_rows)
    heads_grad = (
        dot_second(branch_rows, out_weight).astype(jnp.bfloat16).reshape(group, local_heads, HD)
    )
    keys_use = keys3

    def backward_block(carry, index):
        key_total, value_total = carry
        scores, query_block = block_scores(index, keys_use)
        probs = jnp.exp(scores - log_totals[index][..., None])
        grad_block = lax.dynamic_slice_in_dim(heads_grad, index * block, block, 0)
        prob_grad = jnp.einsum(
            "bhd,khd->hbk", grad_block, values3, preferred_element_type=jnp.float32
        )
        score_grad = (
            probs * (prob_grad - jnp.sum(probs * prob_grad, axis=-1, keepdims=True))
        ).astype(jnp.bfloat16)
        query_part = (
            jnp.einsum("hbk,khd->bhd", score_grad, keys_use, preferred_element_type=jnp.float32)
            * scale
        )
        key_part = (
            jnp.einsum("hbk,bhd->khd", score_grad, query_block, preferred_element_type=jnp.float32)
            * scale
        )
        value_part = jnp.einsum(
            "hbk,bhd->khd",
            probs.astype(jnp.bfloat16),
            grad_block,
            preferred_element_type=jnp.float32,
        )
        key_total = key_total + key_part.reshape(whole, columns)
        value_total = value_total + value_part.reshape(whole, columns)
        return ((key_total, value_total), query_part.reshape(block, columns))

    empty = jnp.zeros((whole, columns), jnp.float32)
    (key_total, value_total), query_parts = lax.scan(
        backward_block, (empty, empty), jnp.arange(count, dtype=jnp.int32)
    )
    query_grad = query_parts.reshape(group, columns).astype(jnp.bfloat16)
    key_sum, value_sum = (
        lax.psum_scatter(
            key_total.astype(jnp.bfloat16), "seq", scatter_dimension=0, tiled=True
        ).astype(jnp.float32),
        lax.psum_scatter(
            value_total.astype(jnp.bfloat16), "seq", scatter_dimension=0, tiled=True
        ).astype(jnp.float32),
    )
    key_grad = key_sum.astype(jnp.bfloat16)
    value_grad = value_sum.astype(jnp.bfloat16)
    grad_query_weight = dot_first(rows_one, query_grad)
    grad_key_weight = dot_first(rows_one, key_grad)
    grad_value_weight = dot_first(rows_one, value_grad)
    grad_query_bias = jnp.sum(query_grad.astype(jnp.float32), axis=0)
    grad_value_bias = jnp.sum(value_grad.astype(jnp.float32), axis=0)
    total = dot_second(query_grad, query_weight)
    total = total + dot_second(key_grad, key_weight)
    first_grad = lax.psum_scatter(
        (total + dot_second(value_grad, value_weight)).astype(jnp.bfloat16),
        "tensor",
        scatter_dimension=0,
        tiled=True,
    ).astype(jnp.float32)
    input_part, grad_norm1_gain, grad_norm1_bias = norm_backward(
        first_grad, normed_one, inverse_one, gain_one
    )
    grad_in = (middle_grad + input_part).astype(jnp.bfloat16)
    (
        grad_query_weight,
        grad_query_bias,
        grad_key_weight,
        grad_value_weight,
        grad_value_bias,
        grad_out_weight,
        grad_up_weight,
        grad_up_bias,
        grad_down_weight,
    ) = (
        lax.psum(grad_query_weight.astype(jnp.bfloat16), ("dp", "seq")).astype(jnp.float32),
        lax.psum(grad_query_bias.astype(jnp.bfloat16), ("dp", "seq")).astype(jnp.float32),
        lax.psum(grad_key_weight.astype(jnp.bfloat16), ("dp", "seq")).astype(jnp.float32),
        lax.psum(grad_value_weight.astype(jnp.bfloat16), ("dp", "seq")).astype(jnp.float32),
        lax.psum(grad_value_bias.astype(jnp.bfloat16), ("dp", "seq")).astype(jnp.float32),
        lax.psum(grad_out_weight.astype(jnp.bfloat16), ("dp", "seq")).astype(jnp.float32),
        lax.psum(grad_up_weight.astype(jnp.bfloat16), ("dp", "seq")).astype(jnp.float32),
        lax.psum(grad_up_bias.astype(jnp.bfloat16), ("dp", "seq")).astype(jnp.float32),
        lax.psum(grad_down_weight.astype(jnp.bfloat16), ("dp", "seq")).astype(jnp.float32),
    )
    (
        grad_norm1_gain,
        grad_norm1_bias,
        grad_out_bias,
        grad_norm2_gain,
        grad_norm2_bias,
        grad_down_bias,
    ) = lax.psum(
        (
            grad_norm1_gain,
            grad_norm1_bias,
            grad_out_bias,
            grad_norm2_gain,
            grad_norm2_bias,
            grad_down_bias,
        ),
        ("dp", "seq", "tensor"),
    )
    return (
        layer_out,
        grad_in,
        grad_norm1_gain,
        grad_norm1_bias,
        grad_query_weight,
        grad_query_bias,
        grad_key_weight,
        grad_value_weight,
        grad_value_bias,
        grad_out_weight,
        grad_out_bias,
        grad_norm2_gain,
        grad_norm2_bias,
        grad_up_weight,
        grad_up_bias,
        grad_down_weight,
        grad_down_bias,
    )


def solution(mesh):
    placed = (
        P(("dp", "seq", "tensor"), None),
        P(),
        P(),
        P(None, "tensor"),
        P("tensor"),
        P(None, "tensor"),
        P(None, "tensor"),
        P("tensor"),
        P("tensor", None),
        P(),
        P(),
        P(),
        P(None, "tensor"),
        P("tensor"),
        P("tensor", None),
        P(),
        P("dp", None),
        P("dp", None),
        P(("dp", "seq", "tensor"), None),
    )
    return jax.shard_map(
        local,
        mesh=mesh,
        in_specs=placed,
        out_specs=(
            P(("dp", "seq", "tensor"), None),
            P(("dp", "seq", "tensor"), None),
            P(),
            P(),
            P(None, "tensor"),
            P("tensor"),
            P(None, "tensor"),
            P(None, "tensor"),
            P("tensor"),
            P("tensor", None),
            P(),
            P(),
            P(),
            P(None, "tensor"),
            P("tensor"),
            P("tensor", None),
            P(),
        ),
        check_vma=False,
    )
```

profile of v0, /device:TPU:0, one launch (start us, length us, event | category | flops | bytes accessed | tf_op | source)
XLA Modules:
  0.0 1756.7 jit_solution(7682176037835182039)
XLA Ops:
  16.0 35.9 %all-gather.7.cloned.1.call-done = bf16[1024,2048]{1,0:T(8,128)(2,1)} async-done(((bf16[256,2048]{1,0:T(8,128)(2,1)}), bf16[1024,2048]{1,0:T(8,128)(2,1)}) %all-gather.7.cloned.1.call-update) | async-done | bytes 4194320 | tf_op jit(solution)/shard_map/all_gather | solution.py:109
  72.3 19.1 %all-gather.11.cloned.1.call-done = bf16[2048,512]{1,0:T(8,128)(2,1)} async-done(((bf16[1024,512]{1,0:T(8,128)(2,1)}), bf16[2048,512]{1,0:T(8,128)(2,1)}) %all-gather.11.cloned.1.call-update) | async-done | bytes 2097168 | tf_op jit(solution)/shard_map/all_gather | solution.py:123
  95.6 31.1 %all-gather.9.cloned.1.call-done = bf16[2048,512]{1,0:T(8,128)(2,1)} async-done(((bf16[1024,512]{1,0:T(8,128)(2,1)}), bf16[2048,512]{1,0:T(8,128)(2,1)}) %all-gather.9.cloned.1.call-update) | async-done | bytes 2097168 | tf_op jit(solution)/shard_map/all_gather | solution.py:122
  131.7 106.0 %while.28 = (s32[]{:T(128)}, bf16[2,512,512]{2,1,0:T(8,128)(2,1)}, f32[2,8,512]{2,1,0:T(8,128)S(1)}, s32[2]{0:T(128)S(1)}, s32[]{:T(128)}, /*index=5*/f32[2048,1...) while((s32[]{:T(128)}, bf16[2,512,512]{2,1,0:T(8,128)(2,1)}, ...), condition=%wide.region_22.23_spmd.clone, body=%wide.region_19.22_spmd.clone.sunk | while | flops 2390786560 | bytes 118868320 | solution.py:153
  138.6 17.3 fusion.167
  191.4 17.3 fusion.167
  245.6 71.2 %reduce-scatter.7.cloned.1.call-done = f32[256,2048]{1,0:T(8,128)} async-done(((f32[1024,2048]{1,0:T(8,128)}), f32[256,2048]{1,0:T(8,128)}) %reduce-scatter.7.cloned.1.call-update) | async-done | bytes 2097168 | tf_op jit(solution)/shard_map/reduce_scatter | solution.py:155
  322.9 34.0 %all-gather.13.cloned.1.call-done = bf16[1024,2048]{1,0:T(8,128)(2,1)} async-done(((bf16[256,2048]{1,0:T(8,128)(2,1)}), bf16[1024,2048]{1,0:T(8,128)(2,1)}) %all-gather.13.cloned.1.call-update) | async-done | bytes 4194320 | tf_op jit(solution)/shard_map/all_gather | solution.py:163
  371.3 21.5 %all-gather.15.cloned.1.call-done = bf16[1024,2048]{1,0:T(8,128)(2,1)} async-done(((bf16[256,2048]{1,0:T(8,128)(2,1)}), bf16[1024,2048]{1,0:T(8,128)(2,1)}) %all-gather.15.cloned.1.call-update) | async-done | bytes 4194320 | tf_op jit(solution)/shard_map/all_gather | solution.py:182
  392.9 33.5 %fusion.86 = (bf16[2048]{0:T(1024)(128)(2,1)}, bf16[1024,2048]{1,0:T(8,128)(2,1)S(1)}, f32[1024,2048]{1,0:T(8,128)}) fusion(f32[1024,2048]{1,0:T(8,128)} %fusion.91, f32[2048]{0:T(1024)S(1)} %convert_element_type.289, bf16[1024,2048]{1,0:T(8,128)(2,1)} %all-gather.15.cloned.1.call-done, bf16[2048,2048]{1,0:T(8,128)(2,1)} %param.37), kind=kOutput, calls=%fused_computation.190 | convolution fusion | flops 8745121792 | bytes 33566720 | tf_op jit(solution)/shard_map/dot_general | solution.py:61
  464.8 20.9 %reduce-scatter.11.cloned.1.call-done = bf16[256,2048]{1,0:T(8,128)(2,1)} async-done(((bf16[1024,2048]{1,0:T(8,128)(2,1)}), bf16[256,2048]{1,0:T(8,128)(2,1)}) %reduce-scatter.11.cloned.1.call-update) | async-done | bytes 1048592 | tf_op jit(solution)/shard_map/reduce_scatter | solution.py:188
  489.2 44.2 %reduce-scatter.9.cloned.1.call-done = bf16[256,2048]{1,0:T(8,128)(2,1)} async-done(((bf16[1024,2048]{1,0:T(8,128)(2,1)}), bf16[256,2048]{1,0:T(8,128)(2,1)}) %reduce-scatter.9.cloned.1.call-update) | async-done | bytes 1048592 | tf_op jit(solution)/shard_map/reduce_scatter | solution.py:169
  540.0 34.5 %all-gather.17.cloned.1.call-done = bf16[1024,2048]{1,0:T(8,128)(2,1)} async-done(((bf16[256,2048]{1,0:T(8,128)(2,1)}), bf16[1024,2048]{1,0:T(8,128)(2,1)}) %all-gather.17.cloned.1.call-update) | async-done | bytes 4194320 | tf_op jit(solution)/shard_map/all_gather | solution.py:200
  580.2 245.7 %while.29 = (s32[]{:T(128)}, f32[2048,512]{0,1:T(8,128)}, f32[2048,512]{0,1:T(8,128)}, bf16[2,512,512]{2,1,0:T(8,128)(2,1)}, s32[2]{0:T(128)S(1)}, /*index=5*/bf...) while((s32[]{:T(128)}, f32[2048,512]{0,1:T(8,128)}, ...), condition=%wide.region_32.33_spmd.clone, body=%wide.region_30.32_spmd.clone.sunk | while | flops 5634519552 | bytes 422292672 | solution.py:237
  603.9 27.0 %multiply_reduce_fusion.16 = (f32[8,512]{1,0:T(8,128)S(1)}, f32[8,512,2048]{2,1,0:T(8,128)}) fusion(f32[8,512,2048]{2,1,0:T(8,128)} %fusion.182, f32[8,512]{1,0:T(8,128)S(1)} %dynamic-slice_bitcast_fusion.2, f32[512,2048]{1,0:T(8,128)S(1)} %broadcast_subtract_fusion.5, f32[8]{0:T(128)S(1)} %multiply_exponential_fusion.5, ...), kind=kOutput, calls=%fused_computation.26.clone.1 | convolution fusion | flops 1132457984 | bytes 75006464 | tf_op jit(solution)/shard_map/while/body/eval_jaxpr/bhd,khd->hbk/dot_general | solution.py:137
  630.9 27.4 %multiply_convert_fusion.3 = bf16[8,512,2048]{2,1,0:T(8,128)(2,1)} fusion(f32[8,512,2048]{2,1,0:T(8,128)} %get-tuple-element.549, f32[8,512,2048]{2,1,0:T(8,128)} %fusion.182, f32[8,512]{1,0:T(8,128)S(1)} %get-tuple-element.550), kind=kLoop, calls=%fused_computation.25.clone.1 | loop fusion | flops 25165824 | bytes 83902464 | tf_op jit(solution)/shard_map/while/body/eval_jaxpr/convert_element_type | solution.py:217
  725.3 27.0 %multiply_reduce_fusion.16 = (f32[8,512]{1,0:T(8,128)S(1)}, f32[8,512,2048]{2,1,0:T(8,128)}) fusion(f32[8,512,2048]{2,1,0:T(8,128)} %fusion.182, f32[8,512]{1,0:T(8,128)S(1)} %dynamic-slice_bitcast_fusion.2, f32[512,2048]{1,0:T(8,128)S(1)} %broadcast_subtract_fusion.5, f32[8]{0:T(128)S(1)} %multiply_exponential_fusion.5, ...), kind=kOutput, calls=%fused_computation.26.clone.1 | convolution fusion | flops 1132457984 | bytes 75006464 | tf_op jit(solution)/shard_map/while/body/eval_jaxpr/bhd,khd->hbk/dot_general | solution.py:137
  752.3 27.4 %multiply_convert_fusion.3 = bf16[8,512,2048]{2,1,0:T(8,128)(2,1)} fusion(f32[8,512,2048]{2,1,0:T(8,128)} %get-tuple-element.549, f32[8,512,2048]{2,1,0:T(8,128)} %fusion.182, f32[8,512]{1,0:T(8,128)S(1)} %get-tuple-element.550), kind=kLoop, calls=%fused_computation.25.clone.1 | loop fusion | flops 25165824 | bytes 83902464 | tf_op jit(solution)/shard_map/while/body/eval_jaxpr/convert_element_type | solution.py:217
  779.7 15.8 fusion.184
  839.7 22.1 %reduce-scatter.13.cloned.1.call-done = bf16[1024,512]{0,1:T(8,128)(2,1)} async-done(((bf16[2048,512]{0,1:T(8,128)(2,1)}), bf16[1024,512]{0,1:T(8,128)(2,1)}) %reduce-scatter.13.cloned.1.call-update) | async-done | bytes 1048592 | tf_op jit(solution)/shard_map/reduce_scatter | solution.py:242
  869.5 27.0 %reduce-scatter.15.cloned.1.call-done = bf16[1024,512]{0,1:T(8,128)(2,1)} async-done(((bf16[2048,512]{0,1:T(8,128)(2,1)}), bf16[1024,512]{0,1:T(8,128)(2,1)}) %reduce-scatter.15.cloned.1.call-update) | async-done | bytes 1048592 | tf_op jit(solution)/shard_map/reduce_scatter | solution.py:245
  948.8 20.8 %all-reduce.1 = (bf16[512]{0:T(512)(128)(2,1)S(1)}, bf16[512]{0:T(512)(128)(2,1)S(1)}, bf16[2048]{0:T(1024)(128)(2,1)S(1)}) all-reduce(bf16[512]{0:T(512)(128)(2,1)S(1)} %reduce_sum.353, bf16[512]{0:T(512)(128)(2,1)S(1)} %reduce_sum.354, bf16[2048]{0:T(1024)(128)(2,1)S(1)} %copy-done.52), channel_id=1, replica_groups=mesh['dp'=4,'seq'=2,'tensor'=4] {'dp','seq'}, use_global_device_ids=true, to_apply=%region_44.45 | all-reduce | flops 3072 | bytes 12288 | tf_op jit(solution)/shard_map/psum | solution.py:280
  973.7 43.5 %all-reduce = (f32[2048]{0:T(1024)}, f32[2048]{0:T(1024)}, f32[2048]{0:T(1024)}, f32[2048]{0:T(1024)}, f32[2048]{0:T(1024)}, /*index=5*/f32[2048]{0:T(1024)}) all-reduce(f32[2048]{0:T(1024)S(1)} %get-tuple-element.284, f32[2048]{0:T(1024)S(1)} %get-tuple-element.289, ...), channel_id=1, replica_groups=mesh['dp'=4,'seq'=2,'tensor'=4] {'dp','seq','tensor'}, use_global_device_ids=true, to_apply=%region_39.40 | all-reduce | flops 12288 | bytes 98304 | tf_op jit(solution)/shard_map/psum | solution.py:296
  1020.9 693.2 %all-reduce.5.cloned.1.call-done = (bf16[2048,512]{1,0:T(8,128)(2,1)}, bf16[2048,512]{1,0:T(8,128)(2,1)}, bf16[2048,512]{1,0:T(8,128)(2,1)}, bf16[512,2048]{1,0:...) async-done(((bf16[2048,512]{1,0:T(8,128)(2,1)}, bf16[2048,512]{1,0:T(8,128)(2,1)}, bf16[2048,512]{1,0:T(8,128)(2,1)}, bf16[512,2048]{1,0:T(8,128)(2,1)}, ...) | async-done | bytes 25165840 | tf_op jit(solution)/shard_map/psum | solution.py:279
  (330 shorter events, 422.0 us)
Async XLA Ops:
  7.2 230.6 %copy-start = (bf16[512,2048]{1,0:T(8,128)(2,1)S(1)}, bf16[512,2048]{1,0:T(8,128)(2,1)}, u32[]{:S(2)}) copy-start(bf16[512,2048]{1,0:T(8,128)(2,1)} %param.31) | copy-start | bytes 6291460
  7.2 44.7 %all-gather.7.cloned.1.call-start = ((), (), s32[]{:S(2)}) async-start(), calls=%async_computation.6 | async-start | bytes 5242880 | tf_op jit(solution)/shard_map/all_gather | solution.py:109
  14.6 76.8 %all-gather.11.cloned.1.call-start = ((), (), s32[]{:S(2)}) async-start(), calls=%async_computation.8 | async-start | bytes 3145728 | tf_op jit(solution)/shard_map/all_gather | solution.py:123
  58.2 68.6 %all-gather.9.cloned.1.call-start = ((), (), s32[]{:S(2)}) async-start(), calls=%async_computation.7 | async-start | bytes 3145728 | tf_op jit(solution)/shard_map/all_gather | solution.py:122
  65.0 251.8 %reduce-scatter.7.cloned.1.call-start = ((), (), s32[]{:S(2)}) async-start(), calls=%async_computation.9 | async-start | bytes 10485760 | tf_op jit(solution)/shard_map/reduce_scatter | solution.py:155
  244.9 71.9 %copy-start.7 = (bf16[256,2048]{1,0:T(8,128)(2,1)S(1)}, bf16[256,2048]{1,0:T(8,128)(2,1)}, u32[]{:S(2)}) copy-start(bf16[256,2048]{1,0:T(8,128)(2,1)} %param.23) | copy-start | bytes 3145732
  245.0 111.9 %all-gather.13.cloned.1.call-start = ((), (), s32[]{:S(2)}) async-start(), calls=%async_computation.10 | async-start | bytes 5242880 | tf_op jit(solution)/shard_map/all_gather | solution.py:163
  245.6 76.6 %copy-start.33 = (f32[2048]{0:T(1024)}, f32[2048]{0:T(1024)S(1)}, u32[]{:S(2)}) copy-start(f32[2048]{0:T(1024)S(1)} %convert_element_type.286) | copy-start | bytes 24580
  322.2 70.6 %all-gather.15.cloned.1.call-start = ((), (), s32[]{:S(2)}) async-start(), calls=%async_computation.12 | async-start | bytes 5242880 | tf_op jit(solution)/shard_map/all_gather | solution.py:182
  322.8 162.9 %reduce-scatter.11.cloned.1.call-start = ((), (), s32[]{:S(2)}) async-start(), calls=%async_computation.13 | async-start | bytes 5242880 | tf_op jit(solution)/shard_map/reduce_scatter | solution.py:188
  441.1 92.3 %reduce-scatter.9.cloned.1.call-start = ((), (), s32[]{:S(2)}) async-start(), calls=%async_computation.11 | async-start | bytes 5242880 | tf_op jit(solution)/shard_map/reduce_scatter | solution.py:169
  464.2 69.2 %copy-start.14 = (bf16[256,2048]{1,0:T(8,128)(2,1)S(1)}, bf16[256,2048]{1,0:T(8,128)(2,1)}, u32[]{:S(2)}) copy-start(bf16[256,2048]{1,0:T(8,128)(2,1)} %param.41) | copy-start | bytes 3145732
  464.2 110.3 %all-gather.17.cloned.1.call-start = ((), (), s32[]{:S(2)}) async-start(), calls=%async_computation.14 | async-start | bytes 5242880 | tf_op jit(solution)/shard_map/all_gather | solution.py:200
  539.9 321.9 %reduce-scatter.13.cloned.1.call-start = ((), (), s32[]{:S(2)}) async-start(), calls=%async_computation.15 | async-start | bytes 3145728 | tf_op jit(solution)/shard_map/reduce_scatter | solution.py:242
  539.9 40.2 %copy-start.24 = (f32[2048]{0:T(1024)S(1)}, f32[2048]{0:T(1024)}, u32[]{:S(2)}) copy-start(f32[2048]{0:T(1024)} %copy-done.23) | copy-start | bytes 24580
  540.0 40.2 %copy-start.27 = (f32[2,8,512]{2,1,0:T(8,128)S(1)}, f32[2,8,512]{2,1,0:T(8,128)}, u32[]{:S(2)}) copy-start(f32[2,8,512]{2,1,0:T(8,128)} %copy-done.26) | copy-start | bytes 98308
  540.0 40.2 %copy-start.31 = (f32[13,2048]{1,0:T(8,128)S(1)}, f32[13,2048]{1,0:T(8,128)}, u32[]{:S(2)}) copy-start(f32[13,2048]{1,0:T(8,128)} %copy-done.30) | copy-start | bytes 319492
  580.6 77.7 %copy-start.9 = (bf16[1024,8,64]{0,2,1:T(8,128)(2,1)}, bf16[1024,8,64]{0,2,1:T(8,128)(2,1)S(1)}, u32[]{:S(2)}) copy-start(bf16[1024,8,64]{0,2,1:T(8,128)(2,1)S(1)} %get-tuple-element.658) | copy-start | bytes 3145732 | tf_op jit(solution)/shard_map/while
  702.0 77.7 %copy-start.9 = (bf16[1024,8,64]{0,2,1:T(8,128)(2,1)}, bf16[1024,8,64]{0,2,1:T(8,128)(2,1)S(1)}, u32[]{:S(2)}) copy-start(bf16[1024,8,64]{0,2,1:T(8,128)(2,1)S(1)} %get-tuple-element.658) | copy-start | bytes 3145732 | tf_op jit(solution)/shard_map/while
  829.8 66.7 %reduce-scatter.15.cloned.1.call-start = ((), (), s32[]{:S(2)}) async-start(), calls=%async_computation.16 | async-start | bytes 3145728 | tf_op jit(solution)/shard_map/reduce_scatter | solution.py:245
  833.9 137.5 %reduce-scatter.17.cloned.1.call-start = ((), (), s32[]{:S(2)}) async-start(), calls=%async_computation.17 | async-start | bytes 5242880 | tf_op jit(solution)/shard_map/reduce_scatter | solution.py:258
  839.7 56.8 %copy-start.19 = (bf16[2048,512]{1,0:T(8,128)(2,1)S(1)}, bf16[2048,512]{1,0:T(8,128)(2,1)}, u32[]{:S(2)}) copy-start(bf16[2048,512]{1,0:T(8,128)(2,1)} %param.29) | copy-start | bytes 6291460
  907.0 807.1 %all-reduce.5.cloned.1.call-start = ((), (), s32[]{:S(2)}) async-start(), calls=%async_computation.18 | async-start | bytes 50331648 | tf_op jit(solution)/shard_map/psum | solution.py:279
  948.2 25.5 %copy-start.35 = (f32[2048]{0:T(1024)S(1)}, f32[2048]{0:T(1024)}, u32[]{:S(2)}) copy-start(f32[2048]{0:T(1024)} %get-tuple-element.282) | copy-start | bytes 24580
  (63 other events, 585.6 us)
Sparse Core Ops, SparseCore 0:
  14.8 37.1 all-gather.6
  58.3 33.1 all-gather.10
  93.6 33.1 all-gather.8
  245.1 71.7 reduce-scatter.6
  322.3 34.4 all-gather.12
  358.3 34.4 all-gather.14
  441.2 44.4 reduce-scatter.10
  488.8 44.5 reduce-scatter.8
  540.0 34.4 all-gather.16
  829.9 31.8 reduce-scatter.12
  864.6 31.8 reduce-scatter.14
  907.1 44.5 reduce-scatter.16
  958.4 755.6 all-reduce.4
where the time goes:
time: 1760 us
  waiting for transfers between devices  1060 us (60%)
  matrix products  396 us (22%)
  other arithmetic  188 us (11%)
  blocking collectives  64.3 us (4%)
  local copies, waits for them, and re-layouts  29.5 us (2%)
    psum x1, waiting for transfers between devices, local(): lax.psum(grad_query_weight.astype(jnp.bfloat16), ('dp', 'seq'))  693 us
    dot_general x4, matrix products, block_scores(): jnp.einsum('bhd,khd->hbk', query_block, keys3, preferred_element_type=jnp...  88.6 us
    dot_general x6, matrix products, dot_second(): lax.dot_general(left, right, (((1,), (1,)), ((), ())), preferred_element_...  74.7 us
    reduce_scatter x1, waiting for transfers between devices, local(): lax.psum_scatter(jnp.dot(heads_out, out_weight, preferred_element_type=jn...  71.2 us
    convert_element_type x2, other arithmetic, backward_block(): score_grad = (probs * (prob_grad - jnp.sum(probs * prob_grad, axis=-1, ke...  54.8 us
    reduce_scatter x1, waiting for transfers between devices, local(): lax.psum_scatter(jnp.dot(lax.slice_in_dim(activated, 0, lax.axis_size('te...  44.2 us
    psum x1, blocking collectives, local(): lax.psum((grad_norm1_gain, grad_norm1_bias, grad_out_bias, grad_norm2_gai...  43.5 us
    dot_general x6, matrix products, dot_first(): lax.dot_general(left, right, (((0,), (0,)), ((), ())), preferred_element_...  41 us
  transfers between devices with their start and end apart: 13, of which 12 were waited for; matrix products, arithmetic and copies ran while one was open for 7% of the time, Pallas kernels for 0%

commit v1 on v0

v1 whole, which is shorter than its diff:
```python
from functools import partial

import jax
import jax.numpy as jnp
from jax import lax
from jax.experimental import pallas as pl
from jax.experimental.pallas import tpu as pltpu
from jax.sharding import PartitionSpec as P

HEADS = 32
EPS = 1e-05
HD = 64
LANES = 128
BIG = 2.0 ** 100
SLOPE_COL = 16
LSE_COL = 24
VMEM_LIMIT = 60 * 1024 * 1024


def dot_nt(left, right):
    return lax.dot_general(left, right, (((1,), (1,)), ((), ())), preferred_element_type=jnp.float32)


def dot_tn(left, right):
    return lax.dot_general(left, right, (((0,), (0,)), ((), ())), preferred_element_type=jnp.float32)


def dot_nn(left, right):
    return lax.dot_general(left, right, (((1,), (0,)), ((), ())), preferred_element_type=jnp.float32)


def three_parts(value):
    high = value.astype(jnp.bfloat16).astype(jnp.float32)
    rest = value - high
    middle = rest.astype(jnp.bfloat16).astype(jnp.float32)
    return high, middle, rest - middle


def tree_features(lengths, parent_ids, first_head, heads, block, whole):
    nseg = lengths.shape[0]
    seg_ids = jnp.arange(nseg, dtype=jnp.int32)
    ends = jnp.cumsum(lengths, dtype=jnp.int32)
    starts = ends - lengths
    parents = jnp.where(seg_ids > 0, parent_ids, 0)
    own = seg_ids[:, None] == seg_ids[None, :]
    ancestor = own | (parents[:, None] == seg_ids[None, :]) | (seg_ids[None, :] == 0)
    above = (ancestor & ~own).astype(jnp.int32)
    path_start = jnp.sum(above * lengths[None, :], axis=1, dtype=jnp.int32)
    token = jnp.arange(whole, dtype=jnp.int32)[:, None]
    hot = (token >= starts[None, :]) & (token < ends[None, :])
    depth = token + jnp.sum(jnp.where(hot, (path_start - starts)[None, :], 0), axis=1, keepdims=True)
    reach = jnp.sum(jnp.where(hot[:, None, :] & ancestor[None, :, :], 1, 0), axis=2)
    lane = jnp.arange(LANES, dtype=jnp.int32)[None, :]
    pad = ((0, 0), (0, LANES - nseg))
    query_side = jnp.pad(hot.astype(jnp.float32), pad)
    key_side = jnp.pad(jnp.where(reach > 0, 0.0, -BIG), pad)
    digit = lane - SLOPE_COL
    coarse = (depth // 256) * 256
    fine = depth - coarse
    in_slope = (digit >= 0) & (digit < 6)
    key_side = jnp.where(in_slope, jnp.where(digit % 2 == 0, coarse, fine).astype(jnp.float32), key_side)
    key_side = jnp.where((lane >= LSE_COL) & (lane < LSE_COL + 3), 1.0, key_side)
    head_ids = (first_head + jnp.arange(heads, dtype=jnp.int32)).astype(jnp.float32)
    slopes = jnp.exp2(-8.0 * (head_ids + 1.0) / 32)
    parts = jnp.stack(three_parts(slopes), axis=1)
    slope_rows = jnp.pad(jnp.repeat(parts, 2, axis=1), ((0, 0), (SLOPE_COL, LANES - SLOPE_COL - 6)))
    count = whole // block
    held = jnp.max(hot.reshape(count, block, nseg).astype(jnp.float32), axis=1)
    reached = jnp.max(reach.reshape(count, block, nseg).astype(jnp.float32), axis=1)
    ids = jnp.arange(count, dtype=jnp.int32)
    active = (jnp.sum(held[:, None, :] * reached[None, :, :], axis=2) > 0.5) & (ids[None, :] < ids[:, None])

    def packed(flags):
        rank = jnp.cumsum(flags.astype(jnp.int32), axis=1) - 1
        slot = flags[:, :, None] & (rank[:, :, None] == ids[None, None, :])
        listed = jnp.sum(jnp.where(slot, ids[None, :, None], 0), axis=1, dtype=jnp.int32)
        total = jnp.sum(flags.astype(jnp.int32), axis=1, keepdims=True, dtype=jnp.int32)
        return jnp.concatenate([total, listed], axis=1)

    return (
        query_side.astype(jnp.bfloat16),
        key_side.astype(jnp.bfloat16),
        slope_rows.astype(jnp.bfloat16),
        packed(active),
        packed(active.T),
    )


def _masks(block):
    lane = lax.broadcasted_iota(jnp.int32, (block, LANES), 1)
    return [lane < HD, lane >= HD], lane


def forward_kernel(place, lists, qkv, fq, fk, srow, o, lse, qa, vt, top, acc, *, block, pairs):
    count = qkv.shape[0] // block
    width = pairs * LANES
    heads = 2 * pairs
    halves, lane = _masks(block)
    zero = jnp.zeros((block, LANES), jnp.bfloat16)
    ones = jnp.ones((16, block), jnp.bfloat16)
    row = lax.broadcasted_iota(jnp.int32, (block, block), 0)
    col = lax.broadcasted_iota(jnp.int32, (block, block), 1)
    diagonal = row <= col

    def spot(index):
        return pl.ds(pl.multiple_of(place[index] * block, block), block)

    def canon(index):
        return pl.ds(pl.multiple_of(index * block, block), block)

    def turn(j, _):
        for pair in range(pairs):
            cols = slice(pair * LANES, (pair + 1) * LANES)
            turned = qkv[spot(j), 2 * width + pair * LANES : 2 * width + (pair + 1) * LANES].astype(jnp.float32).T.astype(jnp.bfloat16)
            for side in range(2):
                vt[j, 2 * pair + side] = jnp.concatenate([turned[side * HD : (side + 1) * HD], ones], axis=0)
        return 0

    lax.fori_loop(0, count, turn, 0)

    def step(j, first):
        key_features = fk[canon(j), :]
        keys = [
            jnp.concatenate([qkv[spot(j), width + pair * LANES : width + (pair + 1) * LANES], key_features], axis=1) for pair in range(pairs)
        ]
        scores = [dot_nt(keys[h // 2], qa[h]) for h in range(heads)]
        if first:
            scores = [jnp.where(diagonal, score, -BIG) for score in scores]
        bests = [jnp.max(score, axis=0, keepdims=True) for score in scores]
        if not first:
            olds = [top[h : h + 1, :] for h in range(heads)]
            bests = [jnp.maximum(old, best) for old, best in zip(olds, bests)]
            scales = [jnp.exp(old - best) for old, best in zip(olds, bests)]
        weights = [jnp.exp(score - best).astype(jnp.bfloat16) for score, best in zip(scores, bests)]
        mixed = [dot_nn(vt[j, h], weights[h]) for h in range(heads)]
        for h in range(heads):
            acc[h] = mixed[h] if first else acc[h] * scales[h] + mixed[h]
            top[h : h + 1, :] = bests[h]

    def rows(i, _):
        query_features = fq[canon(i), :]
        for pair in range(pairs):
            cols = slice(pair * LANES, (pair + 1) * LANES)
            queries = qkv[spot(i), cols] * jnp.bfloat16(HD ** -0.5)
            for side in range(2):
                h = 2 * pair + side
                qa[h] = jnp.concatenate(
                    [jnp.where(halves[side], queries, zero), query_features + srow[h : h + 1, :]], axis=1
                )
        step(i, True)

        def other(n, _):
            step(lists[i, n + 1], False)
            return 0

        lax.fori_loop(0, lists[i, 0], other, 0)
        logs = []
        for pair in range(pairs):
            cols = slice(pair * LANES, (pair + 1) * LANES)
            mixed = []
            for h in (2 * pair, 2 * pair + 1):
                total = acc[h, HD : HD + 1, :]
                mixed.append(acc[h, :HD, :] / total)
                logs.append(top[h : h + 1, :] + jnp.log(total))
            o[spot(i), cols] = jnp.concatenate(mixed, axis=0).T.astype(o.dtype)
        logs.append(jnp.zeros((LANES - heads, block), jnp.float32))
        lse[canon(i), :] = jnp.concatenate(logs, axis=0).T
        return 0

    lax.fori_loop(0, count, rows, 0)


def backward_kernel(place, lists, qkv, do, o, fq, fk, srow, lse, dqkv, qa, da, dqa, dka, dva, *, block, pairs):
    count = qkv.shape[0] // block
    width = pairs * LANES
    heads = 2 * pairs
    halves, lane = _masks(block)
    zero = jnp.zeros((block, LANES), jnp.bfloat16)
    row = lax.broadcasted_iota(jnp.int32, (block, block), 0)
    col = lax.broadcasted_iota(jnp.int32, (block, block), 1)
    diagonal = row <= col
    ones = jnp.where(lane < 3, 1.0, 0.0).astype(jnp.bfloat16)

    def spot(index):
        return pl.ds(pl.multiple_of(place[index] * block, block), block)

    def canon(index):
        return pl.ds(pl.multiple_of(index * block, block), block)

    def spread(value, first):
        high, middle, low = three_parts(value)
        spread_out = jnp.where(lane == first, high, 0.0)
        spread_out = jnp.where(lane == first + 1, middle, spread_out)
        return jnp.where(lane == first + 2, low, spread_out).astype(jnp.bfloat16)

    def prepare(i, _):
        query_features = fq[canon(i), :]
        logs = lse[canon(i), :]
        for pair in range(pairs):
            cols = slice(pair * LANES, (pair + 1) * LANES)
            queries = qkv[spot(i), cols] * jnp.bfloat16(HD ** -0.5)
            grads = do[spot(i), cols]
            product = grads.astype(jnp.float32) * o[spot(i), cols].astype(jnp.float32)
            for side in range(2):
                h = 2 * pair + side
                delta = jnp.sum(jnp.where(halves[side], product, 0.0), axis=1, keepdims=True)
                log_total = jnp.sum(jnp.where(lane == h, logs, 0.0), axis=1, keepdims=True)
                features = query_features + srow[h : h + 1, :] + spread(-log_total, LSE_COL)
                qa[h, canon(i), :] = jnp.concatenate([jnp.where(halves[side], queries, zero), features], axis=1)
                da[h, canon(i), :] = jnp.concatenate([jnp.where(halves[side], grads, zero), spread(-delta, 0)], axis=1)
        dqa[i] = jnp.zeros((pairs * LANES, block), jnp.float32)
        return 0

    lax.fori_loop(0, count, prepare, 0)

    def columns(j, _):
        key_features = fk[canon(j), :]
        key_blocks = [qkv[spot(j), width + pair * LANES : width + (pair + 1) * LANES] for pair in range(pairs)]
        keys = [jnp.concatenate([key_block, key_features], axis=1) for key_block in key_blocks]
        values = [
            jnp.concatenate([qkv[spot(j), 2 * width + pair * LANES : 2 * width + (pair + 1) * LANES], ones], axis=1) for pair in range(pairs)
        ]
        turned = [key_block.astype(jnp.float32).T.astype(jnp.bfloat16) for key_block in key_blocks]

        def step(i, first):
            query_rows = [qa[h, canon(i), :] for h in range(heads)]
            grad_rows = [da[h, canon(i), :] for h in range(heads)]
            scores = [dot_nt(keys[h // 2], query_rows[h]) for h in range(heads)]
            slopes = [dot_nt(values[h // 2], grad_rows[h]) for h in range(heads)]
            if first:
                scores = [jnp.where(diagonal, score, -BIG) for score in scores]
            probs = [jnp.exp(score) for score in scores]
            changes = [(prob * slope).astype(jnp.bfloat16) for prob, slope in zip(probs, slopes)]
            probs = [prob.astype(jnp.bfloat16) for prob in probs]
            for pair in range(pairs):
                cols = slice(pair * LANES, (pair + 1) * LANES)
                a, b = 2 * pair, 2 * pair + 1
                value_part = dot_nn(probs[a], grad_rows[a][:, :LANES]) + dot_nn(probs[b], grad_rows[b][:, :LANES])
                key_part = dot_nn(changes[a], query_rows[a][:, :LANES]) + dot_nn(changes[b], query_rows[b][:, :LANES])
                if first:
                    dva[:, cols] = value_part
                    dka[:, cols] = key_part
                else:
                    dva[:, cols] += value_part
                    dka[:, cols] += key_part
                for side in range(2):
                    h = 2 * pair + side
                    part = slice(h * HD, (h + 1) * HD)
                    dqa[i, part, :] += dot_nn(turned[pair][side * HD : (side + 1) * HD], changes[h])

        step(j, True)

        def other(n, _):
            step(lists[j, n + 1], False)
            return 0

        lax.fori_loop(0, lists[j, 0], other, 0)
        dqkv[spot(j), width : 2 * width] = dka[...].astype(dqkv.dtype)
        dqkv[spot(j), 2 * width :] = dva[...].astype(dqkv.dtype)
        return 0

    lax.fori_loop(0, count, columns, 0)

    def finish(i, _):
        dqkv[spot(i), :width] = (dqa[i] * HD ** -0.5).T.astype(dqkv.dtype)
        return 0

    lax.fori_loop(0, count, finish, 0)


def _specs(number):
    return [pl.BlockSpec(memory_space=pltpu.SMEM)] * 2 + [pl.BlockSpec(memory_space=pltpu.VMEM)] * number


def attention_forward(place, lists, qkv, fq, fk, srow, block):
    whole, width = qkv.shape[0], qkv.shape[1] // 3
    pairs = width // LANES
    return pl.pallas_call(
        partial(forward_kernel, block=block, pairs=pairs),
        out_shape=(jax.ShapeDtypeStruct((whole, width), jnp.bfloat16), jax.ShapeDtypeStruct((whole, LANES), jnp.float32)),
        in_specs=_specs(4),
        out_specs=(pl.BlockSpec(memory_space=pltpu.VMEM),) * 2,
        scratch_shapes=[
            pltpu.VMEM((2 * pairs, block, 2 * LANES), jnp.bfloat16),
            pltpu.VMEM((whole // block, 2 * pairs, HD + 16, block), jnp.bfloat16),
            pltpu.VMEM((8, block), jnp.float32),
            pltpu.VMEM((2 * pairs, HD + 16, block), jnp.float32),
        ],
        compiler_params=pltpu.CompilerParams(vmem_limit_bytes=VMEM_LIMIT),
        name="attention_forward",
    )(place, lists, qkv, fq, fk, srow)


def attention_backward(place, lists, qkv, do, o, fq, fk, srow, lse, block):
    whole, width = do.shape
    pairs = width // LANES
    return pl.pallas_call(
        partial(backward_kernel, block=block, pairs=pairs),
        out_shape=jax.ShapeDtypeStruct((whole, 3 * width), jnp.bfloat16),
        in_specs=_specs(7),
        out_specs=pl.BlockSpec(memory_space=pltpu.VMEM),
        scratch_shapes=[
            pltpu.VMEM((2 * pairs, whole, 2 * LANES), jnp.bfloat16),
            pltpu.VMEM((2 * pairs, whole, 2 * LANES), jnp.bfloat16),
            pltpu.VMEM((whole // block, width, block), jnp.float32),
            pltpu.VMEM((block, width), jnp.float32),
            pltpu.VMEM((block, width), jnp.float32),
        ],
        compiler_params=pltpu.CompilerParams(vmem_limit_bytes=VMEM_LIMIT),
        name="attention_backward",
    )(place, lists, qkv, do, o, fq, fk, srow, lse)


CORE = [(0, 1), (1, 0), (2, 3), (3, 2)]
ACROSS = [(0, 2), (2, 0), (1, 3), (3, 1)]
SWAP = [(0, 1), (1, 0)]
INWARD = [(0, 1), (3, 2)]
MIDDLE = [(1, 2), (2, 1)]
OUTWARD = [(1, 0), (2, 3)]


def low(value):
    return lax.optimization_barrier(value.astype(jnp.bfloat16))


def wide(value):
    return value.astype(jnp.float32)


def core(value):
    return lax.ppermute(value, "tensor", CORE)


def across(value):
    return lax.ppermute(value, "tensor", ACROSS)


def over(value):
    return lax.ppermute(value, "seq", SWAP)


def norm_forward(values, gain, shift):
    center = values - jnp.mean(values, axis=-1, keepdims=True)
    variance = jnp.mean(center * center, axis=-1, keepdims=True)
    inverse = lax.rsqrt(variance + EPS)
    normed = center * inverse
    return (normed * gain + shift, normed, inverse)


def norm_backward(incoming, normed, inverse, gain):
    scaled = incoming * gain
    inner = (
        scaled
        - jnp.mean(scaled, axis=-1, keepdims=True)
        - normed * jnp.mean(scaled * normed, axis=-1, keepdims=True)
    )
    return (inner * inverse, jnp.sum(incoming * normed, axis=0), jnp.sum(incoming, axis=0))


def halves_of(value, axis, which):
    size = value.shape[axis] // 2
    return (
        lax.dynamic_slice_in_dim(value, which * size, size, axis),
        lax.dynamic_slice_in_dim(value, (1 - which) * size, size, axis),
    )


def in_order(own, other, axis, which):
    first = which == 0
    return jnp.concatenate([jnp.where(first, own, other), jnp.where(first, other, own)], axis=axis)


def gather_group(value):
    if lax.axis_size("tensor") == 4:
        beside = core(value)
        far = across(value)
        return (jnp.concatenate([value, beside]), jnp.concatenate([far, core(far)]))
    rows = lax.all_gather(value, "tensor", axis=0, tiled=True)
    return tuple(jnp.split(rows, 2))


def scatter_group(far, near):
    if lax.axis_size("tensor") == 4:
        away = far()
        size = away.shape[0] // 2
        sent = across(low(wide(away[:size]) + wide(core(away[size:]))))
        here = near()
        return wide(here[:size]) + wide(core(here[size:])) + wide(sent)
    away = far()
    here = near()
    return wide(lax.psum_scatter(jnp.concatenate([here, away]), "tensor", scatter_dimension=0, tiled=True))


def gather_slot(value):
    if lax.axis_size("tensor") == 4:
        half = value.shape[0] // 2
        beside = core(value)
        far = across(value)
        past = over(value)
        both = jnp.concatenate([over(far[:half]), across(past[half:])])
        return [jnp.concatenate([piece, other]) for piece, other in
                ((value, beside), (far, core(far)), (past, core(past)), (both, core(both)))]
    own = lax.all_gather(value, "tensor", axis=0, tiled=True)
    return jnp.split(own, 2) + jnp.split(over(own), 2)


def scatter_slot(parts):
    if lax.axis_size("tensor") == 4:
        def chip(part):
            rows = part()
            size = rows.shape[0] // 2
            return wide(rows[:size]) + wide(core(rows[size:]))

        both = low(chip(parts[3]))
        half = both.shape[0] // 2
        both_far = across(both[:half])
        both_past = over(both[half:])
        far = chip(parts[1])
        far_first = across(low(far[:half]))
        past = chip(parts[2])
        past_last = over(low(past[half:]))
        far_last = across(low(far[half:] + wide(both_past)))
        past_first = over(low(past[:half] + wide(both_far)))
        here = chip(parts[0])
        return here + wide(jnp.concatenate([far_first, far_last])) + wide(jnp.concatenate([past_first, past_last]))
    own = lax.psum_scatter(jnp.concatenate([parts[0](), parts[1]()]), "tensor", scatter_dimension=0, tiled=True)
    other = lax.psum_scatter(jnp.concatenate([parts[2](), parts[3]()]), "tensor", scatter_dimension=0, tiled=True)
    return wide(own) + wide(over(other))


def tie(values, after):
    count = len(values)
    return pl.pallas_call(
        lambda *refs: None,
        out_shape=[jax.ShapeDtypeStruct(v.shape, v.dtype) for v in values],
        in_specs=[pl.BlockSpec(memory_space=pl.ANY)] * (count + len(after)),
        out_specs=[pl.BlockSpec(memory_space=pl.ANY)] * count,
        input_output_aliases={i: i for i in range(count)},
        name="tie",
    )(*values, *after)


class Hops:
    def __init__(self, steps):
        self.steps = steps
        self.pending, self.sent = next(steps)
        self.result = None

    def arrived(self, values):
        try:
            self.pending, self.sent = self.steps.send(values)
        except StopIteration as stop:
            self.pending, self.sent, self.result = [], [], stop.value


class Order:
    def __init__(self, after):
        self.after = [after]

    def enter(self, *values):
        out = tie(list(values), self.after)
        self.after = [out[0]]
        return out

    def done(self, *values):
        self.after.extend(values)

    def wait(self, *hops):
        values = [v for h in hops for v in h.pending]
        out = self.enter(*values)
        self.after = []
        for h in hops:
            count = len(h.pending)
            h.arrived(out[:count])
            self.after.extend(h.sent if h.sent else h.result)
            out = out[count:]


def on_line(value, pairs):
    return lax.ppermute(value, "dp", pairs)


def at_end():
    place = lax.axis_index("dp")
    return (place == 0) | (place == 3)


def line_hops(mine):
    (arrived,) = yield [on_line(mine, INWARD)], [mine]
    inner = low(wide(mine) + wide(arrived))
    (arrived,) = yield [on_line(inner, MIDDLE)], [inner]
    total = low(wide(inner) + wide(arrived))
    (arrived,) = yield [on_line(total, OUTWARD)], [total]
    total = low(jnp.where(at_end(), arrived, total))
    (arrived,) = yield [over(total)], [total]
    return [total, arrived]


def pair_hops(own, other):
    (arrived,) = yield [over(other)], [other, own]
    return (yield from line_hops(low(wide(own) + wide(arrived))))


def middle_hops(both):
    (arrived,) = yield [on_line(both, INWARD)], [both]
    inner = low(wide(both) + wide(arrived))
    size = both.shape[1] // 2
    upper = lax.axis_index("dp") // 2
    keep = lax.dynamic_slice_in_dim(inner, upper * size, size, 1)
    give = low(lax.dynamic_slice_in_dim(inner, (1 - upper) * size, size, 1))
    (arrived,) = yield [on_line(give, MIDDLE)], [give]
    kept = low(wide(keep) + wide(arrived))
    (arrived,) = yield [over(kept)], [kept]
    total = low(wide(kept) + wide(jnp.concatenate([arrived[1:], arrived[:1]])))
    first, second = yield [on_line(total, MIDDLE), on_line(total, OUTWARD)], [total]
    total = low(jnp.where(at_end(), second, total))
    (arrived,) = yield [on_line(first, OUTWARD)], [first, total]
    return [total, low(jnp.where(at_end(), arrived, first))]


def vector_sum(group, pair):
    if lax.axis_size("tensor") == 4 and lax.axis_size("dp") == 4:
        group = group + core(group)
        group = group + across(group)
        rows = jnp.concatenate([group, pair])
        rows = rows + over(rows)
        rows = rows + lax.ppermute(rows, "dp", CORE)
        rows = rows + lax.ppermute(rows, "dp", ACROSS)
        return rows[: group.shape[0]], rows[group.shape[0] :]
    return lax.psum(group, ("dp", "seq", "tensor")), lax.psum(pair, ("dp", "seq"))


def local(
    hidden_in, norm1_gain, norm1_bias, query_weight, query_bias, key_weight, value_weight, value_bias, out_weight,
    out_bias, norm2_gain, norm2_bias, up_weight, up_bias, down_weight, down_bias, seg_lengths, parents, out_grad,
):
    local_rows, model = hidden_in.shape
    tensor_count = lax.axis_size("tensor")
    group = local_rows * tensor_count
    whole = 2 * group
    columns = query_weight.shape[1]
    width = columns // 2
    heads = width // HD
    units = up_weight.shape[1]
    seq = lax.axis_index("seq")
    tensor = lax.axis_index("tensor")
    block = 256
    f32 = jnp.float32
    gain_one, gain_two = wide(norm1_gain), wide(norm2_gain)

    quick = tensor_count == 4 and lax.axis_size("dp") == 4

    inputs = wide(hidden_in)
    first, normed_one, inverse_one = norm_forward(inputs, gain_one, wide(norm1_bias))
    chunks_one = gather_slot(low(first))

    qkv_weight = jnp.concatenate([halves_of(w, 1, seq)[0] for w in (query_weight, key_weight, value_weight)], axis=1)
    qkv_bias = jnp.concatenate(
        [halves_of(query_bias, 0, seq)[0], jnp.zeros((width,), jnp.bfloat16), halves_of(value_bias, 0, seq)[0]]
    )
    out_rel = jnp.concatenate(halves_of(out_weight, 0, seq))
    up_rel = jnp.concatenate(halves_of(up_weight, 1, seq), axis=1)
    up_bias_rel = wide(jnp.concatenate(halves_of(up_bias, 0, seq)))
    down_rel = jnp.concatenate(halves_of(down_weight, 0, seq))

    blocks = jnp.arange(whole // block, dtype=jnp.int32)
    if tensor_count == 4:
        place = blocks ^ (seq * 4 + tensor)
    else:
        side = group // block
        place = ((blocks // side) ^ seq) * side + blocks % side
    fq, fk, slope_rows, key_lists, query_lists = tree_features(
        seg_lengths[0], parents[0], tensor * (columns // HD) + seq * heads, heads, block, whole
    )

    qkv = jnp.concatenate(
        [(jnp.dot(rows, qkv_weight, preferred_element_type=f32) + wide(qkv_bias)).astype(jnp.bfloat16) for rows in chunks_one]
    )
    order = Order(qkv)
    (out_grad_late,) = order.enter(out_grad)
    grad_near, grad_far = gather_group(out_grad_late)
    mixed, log_totals = attention_forward(place, key_lists, qkv, fq, fk, slope_rows, block)
    heads_out = jnp.concatenate([mixed[:group], over(mixed[group:])], axis=1)
    half = group // 2

    def product(left, right):
        return lambda: jnp.dot(left, right, preferred_element_type=f32).astype(jnp.bfloat16)

    def product_nt(left, right):
        return lambda: dot_nt(left, right).astype(jnp.bfloat16)

    def low_dot(left, right):
        return dot_tn(left, right).astype(jnp.bfloat16)

    branch = scatter_group(product(heads_out[half:], out_rel), product(heads_out[:half], out_rel)) + wide(out_bias)
    act_grad_near = low(dot_nt(grad_near, down_rel))
    order = Order(act_grad_near)
    (branch,) = order.enter(branch)
    middle = inputs + branch
    second, normed_two, inverse_two = norm_forward(middle, gain_two, wide(norm2_bias))
    two_near, two_far = gather_group(low(second))
    act_grad_far = low(dot_nt(grad_far, down_rel))
    order = Order(act_grad_far)
    (two_far,) = order.enter(two_far)
    activated, up_grad = [], []
    for rows, grads in ((two_near, act_grad_near), (two_far, act_grad_far)):
        pre = jnp.dot(rows, up_rel, preferred_element_type=f32) + up_bias_rel
        cdf = 0.5 * (1.0 + lax.erf(pre * (0.5 ** 0.5)))
        activated.append((pre * cdf).astype(jnp.bfloat16))
        slope = cdf + pre * (jnp.exp(-0.5 * pre * pre) * 0.3989422804014327)
        up_grad.append((wide(grads) * slope).astype(jnp.bfloat16))
    act_all = jnp.concatenate(activated)
    up_grad_all = jnp.concatenate(up_grad)
    rows_two = jnp.concatenate([two_near, two_far])
    grad_rows = jnp.concatenate([grad_near, grad_far])
    rows_one = jnp.concatenate(chunks_one)
    part = units // 2
    cotangent = wide(out_grad)

    def down_parts(index):
        cols = slice(index * (model // 2), (index + 1) * (model // 2))
        return low_dot(act_all[:, :part], grad_rows[:, cols]), low_dot(act_all[:, part:], grad_rows[:, cols])

    quarter = model // 4

    def up_parts(index):
        rows = rows_two[:, index * quarter : (index + 1) * quarter]
        return jnp.stack([low_dot(rows, up_grad_all[:, :part]), low_dot(rows, up_grad_all[:, part:])])

    def ffn_sum():
        return scatter_group(product(act_all[half:], down_rel), product(act_all[:half], down_rel)) + wide(down_bias)

    def norm_two(second_grad):
        middle_part, gain_grad, bias_grad = norm_backward(second_grad, normed_two, inverse_two, gain_two)
        return cotangent + middle_part, gain_grad, bias_grad

    def heads_grads(rows):
        return dot_nt(rows, out_rel).astype(jnp.bfloat16)

    def attention_grads(arrived, near_grads):
        return attention_backward(
            place, query_lists, qkv, jnp.concatenate([near_grads, arrived]), mixed, fq, fk, slope_rows, log_totals, block
        )

    def first_grads(grads):
        return scatter_slot([product_nt(grads[i * half : (i + 1) * half], qkv_weight) for i in range(4)])

    def qkv_part(grads, index):
        return low_dot(rows_one, grads[:, index * width : (index + 1) * width])

    if quick:
        order = Order(up_grad_all)
        (act_all,) = order.enter(act_all)
        down0 = Hops(pair_hops(*down_parts(0)))
        order.done(*down0.sent)
        (up_grad_all,) = order.enter(up_grad_all)
        up0 = Hops(middle_hops(up_parts(0)))
        order.done(*up0.sent)
        (up_grad_all,) = order.enter(up_grad_all)
        second_far = product_nt(up_grad_all[half:], up_rel)()
        second_size = half // 2
        second_sent = low(wide(second_far[:second_size]) + wide(core(second_far[second_size:])))
        second_back = across(second_sent)
        order.done(second_sent)
        (act_all,) = order.enter(act_all)
        down1 = Hops(pair_hops(*down_parts(1)))
        order.done(*down1.sent)
        (up_grad_all,) = order.enter(up_grad_all)
        second_near = product_nt(up_grad_all[:half], up_rel)()
        second_own = wide(second_near[:second_size]) + wide(core(second_near[second_size:]))
        order.done(second_own)
        (second_back,) = order.enter(second_back)
        middle_grad, grad_norm2_gain, grad_norm2_bias = norm_two(second_own + wide(second_back))
        branch_grad = low(middle_grad)
        branch_near, branch_far = gather_group(branch_grad)
        order.done(branch_grad)
        (act_all,) = order.enter(act_all)
        ffn_out = ffn_sum()
        grad_up_bias = jnp.sum(wide(up_grad_all), axis=0)
        order.wait(down0)
        order.wait(up0)
        (branch_far,) = order.enter(branch_far)
        heads_grad = jnp.concatenate([heads_grads(branch_near), heads_grads(branch_far)])
        heads_grad_sent = low(heads_grad[:, width:])
        heads_grad_back = over(heads_grad_sent)
        order.done(heads_grad, heads_grad_sent)
        (up_grad_all,) = order.enter(up_grad_all)
        up1 = Hops(middle_hops(up_parts(1)))
        order.done(*up1.sent)
        order.wait(up0)
        branch_rows = jnp.concatenate([branch_near, branch_far])
        order.wait(down1)
        order.wait(down0)
        (heads_grad_back,) = order.enter(heads_grad_back)
        grads = attention_grads(heads_grad_back, heads_grad[:, :width])
        order.done(grads)
        (up_grad_all,) = order.enter(up_grad_all)
        up2 = Hops(middle_hops(up_parts(2)))
        order.done(*up2.sent)
        order.wait(up0)
        order.wait(up1)
        order.wait(down0)
        (grads,) = order.enter(grads)
        first_grad = first_grads(grads)
        out0 = Hops(pair_hops(low_dot(heads_out[:, :width], branch_rows), low_dot(heads_out[:, width:], branch_rows)))
        order.done(*out0.sent)
        order.wait(up1)
        (up_grad_all,) = order.enter(up_grad_all)
        up3 = Hops(middle_hops(up_parts(3)))
        order.done(*up3.sent)
        qkv0 = Hops(line_hops(qkv_part(grads, 0)))
        order.wait(down0)
        order.wait(down1)
        order.wait(up0)
        order.wait(up2)
        order.wait(out0)
        order.wait(up1)
        qkv1 = Hops(line_hops(qkv_part(grads, 1)))
        qkv2 = Hops(line_hops(qkv_part(grads, 2)))
        order.wait(down0)
        order.wait(up2)
        order.wait(down1)
        order.wait(up1)
        order.wait(up3)
        order.wait(up2)
        order.wait(qkv0)
        order.wait(out0)
        order.wait(up0)
        order.wait(up3)
        order.wait(down1)
        order.wait(qkv0, qkv1)
        order.wait(out0)
        order.wait(up2)
        order.wait(up3)
        order.wait(qkv0, qkv1, qkv2)
        order.wait(out0)
        order.wait(up1)
        order.wait(qkv1, qkv2)
        order.wait(up3)
        order.wait(down1)
        order.wait(out0)
        order.wait(up2)
        order.wait(qkv0, qkv2)
        order.wait(up3)
        order.wait(qkv1)
        order.wait(qkv2)
        for h in (down0, down1, up0, up1, up2, up3, out0, qkv0, qkv1, qkv2):
            assert h.result is not None
    else:
        second_grad = scatter_group(product_nt(up_grad[1], up_rel), product_nt(up_grad[0], up_rel))
        middle_grad, grad_norm2_gain, grad_norm2_bias = norm_two(second_grad)
        branch_grad = low(middle_grad)
        branch_near, branch_far = gather_group(branch_grad)
        ffn_out = ffn_sum()
        grad_up_bias = jnp.sum(wide(up_grad_all), axis=0)
        heads_grad = jnp.concatenate([heads_grads(branch_near), heads_grads(branch_far)])
        grads = attention_grads(over(heads_grad[:, width:]), heads_grad[:, :width])
        branch_rows = jnp.concatenate([branch_near, branch_far])
        first_grad = first_grads(grads)
        sums = [[*down_parts(0)], [*down_parts(1)], *[[up[0], up[1]] for up in map(up_parts, range(4))]]
        sums.append([low_dot(heads_out[:, :width], branch_rows), low_dot(heads_out[:, width:], branch_rows)])
        axes = [0, 0, 1, 1, 1, 1, 0, 1, 1, 1]
        for i in range(3):
            sums.append([qkv_part(grads, i), jnp.zeros((model, width), jnp.bfloat16)])
        sums = [lax.psum(in_order(own, other, axis, seq), ("dp", "seq")) for (own, other), axis in zip(sums, axes)]

    layer_out = (middle + ffn_out).astype(jnp.bfloat16)
    grad_down_bias = jnp.sum(cotangent, axis=0)
    grad_out_bias = jnp.sum(wide(branch_grad), axis=0)
    bias_sum = jnp.sum(wide(grads), axis=0)
    input_part, grad_norm1_gain, grad_norm1_bias = norm_backward(first_grad, normed_one, inverse_one, gain_one)
    grad_in = (middle_grad + input_part).astype(jnp.bfloat16)

    nothing = jnp.zeros((width,), f32)
    query_bias_row = in_order(bias_sum[:width], nothing, 0, seq)
    value_bias_row = in_order(bias_sum[2 * width :], nothing, 0, seq)
    up_bias_row = in_order(grad_up_bias[:part], grad_up_bias[part:], 0, seq)
    pairs = jnp.concatenate([query_bias_row, value_bias_row, up_bias_row])
    group_rows, pair_rows = vector_sum(
        jnp.stack([grad_norm1_gain, grad_norm1_bias, grad_out_bias, grad_norm2_gain, grad_norm2_bias, grad_down_bias]),
        jnp.pad(pairs, (0, -pairs.shape[0] % model)).reshape(-1, model),
    )
    pair_rows = pair_rows.reshape(-1)

    def put(out, value, row, column):
        return lax.dynamic_update_slice(out, wide(value), (row, column))

    if quick:
        down = jnp.zeros((units, model), f32)
        for i, (own, other) in enumerate((down0.result, down1.result)):
            down = put(down, own, seq * part, i * (model // 2))
            down = put(down, other, (1 - seq) * part, i * (model // 2))
        up = jnp.zeros((model, units), f32)
        upper = lax.axis_index("dp") // 2
        for i, h in enumerate((up0, up1, up2, up3)):
            for value, side in zip(h.result, (upper, 1 - upper)):
                row = i * quarter + side * (quarter // 2)
                up = put(up, value[0], row, seq * part)
                up = put(up, value[1], row, (1 - seq) * part)
        out = jnp.zeros((columns, model), f32)
        out = put(put(out, out0.result[0], seq * width, 0), out0.result[1], (1 - seq) * width, 0)
        qkv_out = []
        for h in (qkv0, qkv1, qkv2):
            empty = jnp.zeros((model, columns), f32)
            qkv_out.append(put(put(empty, h.result[0], 0, seq * width), h.result[1], 0, (1 - seq) * width))
    else:
        down = wide(jnp.concatenate(sums[:2], axis=1))
        up = wide(jnp.concatenate(sums[2:6], axis=0))
        out = wide(sums[6])
        qkv_out = [wide(v) for v in sums[7:]]

    return (
        layer_out,
        grad_in,
        group_rows[0],
        group_rows[1],
        qkv_out[0],
        pair_rows[:columns],
        qkv_out[1],
        qkv_out[2],
        pair_rows[columns : 2 * columns],
        out,
        group_rows[2],
        group_rows[3],
        group_rows[4],
        up,
        pair_rows[2 * columns : 2 * columns + units],
        down,
        group_rows[5],
    )


def solution(mesh):
    placed = (
        P(("dp", "seq", "tensor"), None),
        P(),
        P(),
        P(None, "tensor"),
        P("tensor"),
        P(None, "tensor"),
        P(None, "tensor"),
        P("tensor"),
        P("tensor", None),
        P(),
        P(),
        P(),
        P(None, "tensor"),
        P("tensor"),
        P("tensor", None),
        P(),
        P("dp", None),
        P("dp", None),
        P(("dp", "seq", "tensor"), None),
    )
    return jax.shard_map(
        local,
        mesh=mesh,
        in_specs=placed,
        out_specs=(
            P(("dp", "seq", "tensor"), None),
            P(("dp", "seq", "tensor"), None),
            P(),
            P(),
            P(None, "tensor"),
            P("tensor"),
            P(None, "tensor"),
            P(None, "tensor"),
            P("tensor"),
            P("tensor", None),
            P(),
            P(),
            P(),
            P(None, "tensor"),
            P("tensor"),
            P("tensor", None),
            P(),
        ),
        check_vma=False,
    )
```

time: 1760 us -> 1080 us (0.61)
  waiting for transfers between devices: 1060 us -> 343 us
  matrix products: 396 us -> 167 us
  starting transfers between devices: 0.54 us -> 128 us
  local copies, waits for them, and re-layouts: 29.5 us -> 118 us
  Pallas kernels: 0 us -> 65.6 us
  blocking collectives: 64.3 us -> 0 us
  other arithmetic: 188 us -> 244 us
    psum x1 -> x0, waiting for transfers between devices: 693 us -> none  [local(): lax.psum(grad_query_weight.astype(jnp.bfloat16), ('dp', 'seq'))]
    ppermute x0 -> x94, waiting for transfers between devices: none -> 343 us  [the longest x38 186 us: on_line(): return lax.ppermute(value, 'dp', pairs)]
    dot_general x37, matrix products: 396 us -> 167 us  [the longest x17 62.7 us: dot_tn(): lax.dot_general(left, right, (((0,), (0,)), ((), ())), preferred_element_...]
    reduce_scatter x6 -> x0, waiting for transfers between devices: 185 us -> none  [the longest x1 71.2 us: local(): lax.psum_scatter(jnp.dot(heads_out, out_weight, preferred_element_type=jn...]
    all_gather x6 -> x0, waiting for transfers between devices: 176 us -> none  [the longest x1 35.9 us: local(): lax.all_gather(first.astype(jnp.bfloat16), 'tensor', axis=0, tiled=True)]
    ppermute x0 -> x94, starting transfers between devices: none -> 128 us  [the longest x38 86.3 us: on_line(): return lax.ppermute(value, 'dp', pairs)]
    pallas_call x0 -> x60, Pallas kernels: none -> 65.6 us  [the longest x1 38.3 us: attention_backward(): pl.pallas_call(partial(backward_kernel, block=block, pairs=pairs), out_sh...]
    psum x2 -> x0, blocking collectives: 64.3 us -> none  [the longest x1 43.5 us: local(): lax.psum((grad_norm1_gain, grad_norm1_bias, grad_out_bias, grad_norm2_gai...]
  transfers between devices with their start and end apart: 13 -> 94, of which waited for: 12 -> 30; matrix products, arithmetic and copies ran while one was open for 7% -> 39% of each run, Pallas kernels for 0% -> 4%
where the time goes in v1:
time: 1080 us; the launch traced here: 1070 us
  waiting for transfers between devices  343 us (32%)
  other arithmetic  244 us (23%)
  matrix products  167 us (15%)
  starting transfers between devices  128 us (12%)
  local copies, waits for them, and re-layouts  118 us (11%)
  Pallas kernels  65.6 us (6%)
    ppermute x38, waiting for transfers between devices, on_line(): return lax.ppermute(value, 'dp', pairs)  186 us
    convert_element_type x36, other arithmetic, low(): return lax.optimization_barrier(value.astype(jnp.bfloat16))  98.5 us
    ppermute x38, starting transfers between devices, on_line(): return lax.ppermute(value, 'dp', pairs)  86.3 us
    ppermute x12, waiting for transfers between devices, across(): return lax.ppermute(value, 'tensor', ACROSS)  73.6 us
    ppermute x21, waiting for transfers between devices, over(): return lax.ppermute(value, 'seq', SWAP)  66.7 us
    dot_general x17, matrix products, dot_tn(): lax.dot_general(left, right, (((0,), (0,)), ((), ())), preferred_element_...  62.7 us
    dot_general x10, matrix products, dot_nt(): lax.dot_general(left, right, (((1,), (1,)), ((), ())), preferred_element_...  54 us
    unnamed x325, local copies, waits for them, and re-layouts  48.5 us
  transfers between devices with their start and end apart: 94, of which 30 were waited for; matrix products, arithmetic and copies ran while one was open for 39% of the time, Pallas kernels for 4%

profile of v1, /device:TPU:0, one launch (start us, length us, event | category | flops | bytes accessed | tf_op | source)
XLA Modules:
  0.0 1067.7 jit_solution(17916442895688881927)
XLA Ops:
  64.0 27.3 %attention_forward.1 = (bf16[2048,256]{1,0:T(8,128)(2,1)}, f32[2048,128]{1,0:T(8,128)}) custom-call(s32[8]{0:T(128)} %iota_xor_fusion.place, s32[8,9]{1,0:T(8,128)} %pad_add_fusion.lists, bf16[2048,768]{1,0:T(8,128)(2,1)} %pad_maximum_fusion.8.qkv.refs_1_, bf16[2048,128]{1,0:T(8,128)(2,1)} %convert_convert_fusion.fq, ...), custom_call_target="tpu_custom_call" | custom-call | tf_op jit(solution)/shard_map/attention_forward/pallas_call | solution.py:278
  97.6 10.1 collective-permute-done.8
  111.1 9.7 constant_dynamic-slice_fusion.7
  135.3 9.8 convolution_convert_fusion.9.refs_1_
  152.0 21.8 %collective-permute-done.11 = bf16[256,2048]{1,0:T(8,128)(2,1)S(1)} collective-permute-done((bf16[256,2048]{1,0:T(8,128)(2,1)}, bf16[256,2048]{1,0:T(8,128)(2,1)S(1)}, u32[]{:S(2)}, u32[]{:S(2)}) %collective-permute-start.11) | collective-permute-done | bytes 1048608 | tf_op jit(solution)/shard_map/ppermute | solution.py:335
  182.0 10.5 convolution_convert_fusion.8.refs_1_
  192.5 12.9 %collective-permute-done.14 = bf16[256,2048]{1,0:T(8,128)(2,1)} collective-permute-done((bf16[256,2048]{1,0:T(8,128)(2,1)}, bf16[256,2048]{1,0:T(8,128)(2,1)}, u32[]{:S(2)}, u32[]{:S(2)}) %collective-permute-start.14) | collective-permute-done | bytes 1048608 | tf_op jit(solution)/shard_map/ppermute | solution.py:335
  219.5 12.2 %fusion.5 = (bf16[512,2048]{1,0:T(8,128)(2,1)S(1)}, bf16[512,2048]{1,0:T(8,128)(2,1)S(1)}, bf16[512,2048]{1,0:T(8,128)(2,1)S(1)}, bf16[512,2048]{1,0:T(8,128)(2,1)S(1)}) fusion(bf16[512,2048]{1,0:T(8,128)(2,1)} %convolution_convert_fusion.9.refs_1_, f32[512,2048]{1,0:T(8,128)} %fusion.76, f32[2048]{0:T(1024)S(1)} %maximum_convert_fusion, ...), kind=kOutput, calls=%fused_computation.11 | convolution fusion | flops 4341104640 | bytes 27271168 | tf_op jit(solution)/shard_map/dot_general | solution.py:607
  259.5 8.6 convolution_convert_fusion.7
  291.0 8.8 convolution_convert_fusion.6
  316.7 13.9 %collective-permute-done.19.refs_0_ = bf16[256,2048]{1,0:T(8,128)(2,1)S(1)} collective-permute-done((bf16[256,2048]{1,0:T(8,128)(2,1)S(1)}, bf16[256,2048]{1,0:T(8,128)(2,1)S(1)}, u32[]{:S(2)}, u32[]{:S(2)}) %collective-permute-start.19) | collective-permute-done | bytes 1048608 | tf_op jit(solution)/shard_map/ppermute | solution.py:335
  341.0 8.7 convolution_convert_fusion.4
  438.2 38.3 %attention_backward.1.refs_2_.refs_0_ = bf16[2048,768]{1,0:T(8,128)(2,1)} custom-call(s32[8]{0:T(128)} %iota_xor_fusion.place, s32[8,9]{1,0:T(8,128)} %pad_add_fusion.1.lists, bf16[2048,768]{1,0:T(8,128)(2,1)} %pad_maximum_fusion.8.qkv.refs_1_, bf16[2048,256]{1,0:T(8,128)(2,1)} %pad_maximum_fusion.20.do, bf16[2048,256]{1,0:T(8,128)(2,1)} %get-tuple-element.36.o, ...), custom_call_target="tpu_custom_call" | custom-call | tf_op jit(solution)/shard_map/attention_backward/pallas_call | solution.py:297
  577.4 17.3 %collective-permute-done.54.refs_1_ = bf16[2,256,1024]{2,1,0:T(8,128)(2,1)} collective-permute-done((bf16[2,256,1024]{2,1,0:T(8,128)(2,1)S(1)}, bf16[2,256,1024]{2,1,0:T(8,128)(2,1)}, u32[]{:S(2)}, u32[]{:S(2)}) %collective-permute-start.54) | collective-permute-done | bytes 1048608 | tf_op jit(solution)/shard_map/ppermute | solution.py:480
  631.6 9.8 collective-permute-start.63
  658.7 28.8 %collective-permute-done.48 = f32[8,2048]{1,0:T(8,128)S(1)} collective-permute-done((f32[8,2048]{1,0:T(8,128)S(1)}, f32[8,2048]{1,0:T(8,128)S(1)}, u32[]{:S(2)}, u32[]{:S(2)}) %collective-permute-start.48) | collective-permute-done | bytes 65568 | tf_op jit(solution)/shard_map/ppermute | solution.py:339
  697.6 14.6 %collective-permute-done.50 = f32[8,2048]{1,0:T(8,128)S(1)} collective-permute-done((f32[8,2048]{1,0:T(8,128)S(1)}, f32[8,2048]{1,0:T(8,128)S(1)}, u32[]{:S(2)}, u32[]{:S(2)}) %collective-permute-start.50) | collective-permute-done | bytes 65568 | tf_op jit(solution)/shard_map/ppermute | solution.py:528
  765.6 37.4 %collective-permute-done.72.refs_0_ = bf16[256,2048]{1,0:T(8,128)(2,1)} collective-permute-done((bf16[256,2048]{1,0:T(8,128)(2,1)S(1)}, bf16[256,2048]{1,0:T(8,128)(2,1)}, u32[]{:S(2)}, u32[]{:S(2)}) %collective-permute-start.72) | collective-permute-done | bytes 1048608 | tf_op jit(solution)/shard_map/ppermute | solution.py:480
  819.7 23.4 %collective-permute-done.69.refs_0_ = bf16[1024,1024]{1,0:T(8,128)(2,1)} collective-permute-done((bf16[1024,1024]{1,0:T(8,128)(2,1)S(1)}, bf16[1024,1024]{1,0:T(8,128)(2,1)}, u32[]{:S(2)}, u32[]{:S(2)}) %collective-permute-start.69) | collective-permute-done | bytes 2097184 | tf_op jit(solution)/shard_map/ppermute | solution.py:480
  876.1 24.8 %collective-permute-done.73.refs_0_ = bf16[2048,256]{1,0:T(8,128)(2,1)} collective-permute-done((bf16[2048,256]{1,0:T(8,128)(2,1)}, bf16[2048,256]{1,0:T(8,128)(2,1)}, u32[]{:S(2)}, u32[]{:S(2)}) %collective-permute-start.73) | collective-permute-done | bytes 1048608 | tf_op jit(solution)/shard_map/ppermute | solution.py:480
  911.9 34.0 %collective-permute-done.84.refs_0_ = bf16[256,2048]{1,0:T(8,128)(2,1)} collective-permute-done((bf16[256,2048]{1,0:T(8,128)(2,1)S(1)}, bf16[256,2048]{1,0:T(8,128)(2,1)}, u32[]{:S(2)}, u32[]{:S(2)}) %collective-permute-start.84) | collective-permute-done | bytes 1048608 | tf_op jit(solution)/shard_map/ppermute | solution.py:480
  966.5 19.3 %collective-permute-done.81.refs_0_ = bf16[2048,256]{1,0:T(8,128)(2,1)} collective-permute-done((bf16[2048,256]{1,0:T(8,128)(2,1)}, bf16[2048,256]{1,0:T(8,128)(2,1)}, u32[]{:S(2)}, u32[]{:S(2)}) %collective-permute-start.81) | collective-permute-done | bytes 1048608 | tf_op jit(solution)/shard_map/ppermute | solution.py:480
  994.4 16.2 %collective-permute-done.90.refs_1_ = bf16[2,256,1024]{2,1,0:T(8,128)(2,1)} collective-permute-done((bf16[2,256,1024]{2,1,0:T(8,128)(2,1)}, bf16[2,256,1024]{2,1,0:T(8,128)(2,1)}, u32[]{:S(2)}, u32[]{:S(2)}) %collective-permute-start.90) | collective-permute-done | bytes 1048608 | tf_op jit(solution)/shard_map/ppermute | solution.py:480
  1039.1 8.6 collective-permute-done.92.refs_0_
  (823 shorter events, 638.0 us)
Async XLA Ops:
  306.4 58.3 %collective-permute-start.27 = (bf16[2,512,1024]{2,1,0:T(8,128)(2,1)}, bf16[2,512,1024]{2,1,0:T(8,128)(2,1)}, u32[]{:S(2)}, u32[]{:S(2)}) collective-permute-start(bf16[2,512,1024]{2,1,0:T(8,128)(2,1)} %pad_maximum_fusion.11.refs_2_), channel_id=1, source_target_pairs={{0,8},{24,16},{1,9},{25,17},{2,10},{26,18},{3,11},{27,19},{4,12},{... | collective-permute-start | bytes 6291464 | tf_op jit(solution)/shard_map/ppermute | solution.py:480
  312.9 92.3 %collective-permute-start.31 = (bf16[1024,1024]{1,0:T(8,128)(2,1)}, bf16[1024,1024]{1,0:T(8,128)(2,1)}, u32[]{:S(2)}, u32[]{:S(2)}) collective-permute-start(bf16[1024,1024]{1,0:T(8,128)(2,1)} %fusion.93.refs_2_), channel_id=1, source_target_pairs={{0,4},{4,0},{1,5},{5,1},{2,6},{6,2},{3,7},{7,3},{8,12},{12,8},{9,1... | collective-permute-start | bytes 6291464 | tf_op jit(solution)/shard_map/ppermute | solution.py:339
  364.7 54.7 %collective-permute-start.21 = (bf16[256,2048]{1,0:T(8,128)(2,1)}, bf16[256,2048]{1,0:T(8,128)(2,1)}, u32[]{:S(2)}, u32[]{:S(2)}) collective-permute-start(bf16[256,2048]{1,0:T(8,128)(2,1)} %slice.440), channel_id=1, source_target_pairs={{0,1},{1,0},{2,3},{3,2},{4,5},{5,4},{6,7},{7,6},{8,9},{9,8},{10,11... | collective-permute-start | bytes 3145736 | tf_op jit(solution)/shard_map/ppermute | solution.py:331
  370.1 59.4 %collective-permute-start.30 = (bf16[1024,1024]{1,0:T(8,128)(2,1)}, bf16[1024,1024]{1,0:T(8,128)(2,1)}, u32[]{:S(2)}, u32[]{:S(2)}) collective-permute-start(bf16[1024,1024]{1,0:T(8,128)(2,1)} %add_convert_fusion.9.refs_1_), channel_id=1, source_target_pairs={{0,8},{24,16},{1,9},{25,17},{2,10},{26,18},{3,11},{27,19},{4,12},{... | collective-permute-start | bytes 6291464 | tf_op jit(solution)/shard_map/ppermute | solution.py:480
  405.1 85.8 %collective-permute-start.34 = (bf16[2,512,1024]{2,1,0:T(8,128)(2,1)}, bf16[2,512,1024]{2,1,0:T(8,128)(2,1)}, u32[]{:S(2)}, u32[]{:S(2)}) collective-permute-start(bf16[2,512,1024]{2,1,0:T(8,128)(2,1)} %pad_maximum_fusion.13.refs_2_), channel_id=1, source_target_pairs={{0,8},{24,16},{1,9},{25,17},{2,10},{26,18},{3,11},{27,19},{4,12},{... | collective-permute-start | bytes 6291464 | tf_op jit(solution)/shard_map/ppermute | solution.py:480
  419.4 67.6 %collective-permute-start.35 = (bf16[2,256,1024]{2,1,0:T(8,128)(2,1)}, bf16[2,256,1024]{2,1,0:T(8,128)(2,1)}, u32[]{:S(2)}, u32[]{:S(2)}) collective-permute-start(bf16[2,256,1024]{2,1,0:T(8,128)(2,1)} %add_convert_fusion.27.refs_1_), channel_id=1, source_target_pairs={{0,4},{4,0},{1,5},{5,1},{2,6},{6,2},{3,7},{7,3},{8,12},{12,8},{9,1... | collective-permute-start | bytes 3145736 | tf_op jit(solution)/shard_map/ppermute | solution.py:339
  420.0 152.2 %collective-permute-start.55 = (bf16[1024,1024]{1,0:T(8,128)(2,1)}, bf16[1024,1024]{1,0:T(8,128)(2,1)}, u32[]{:S(2)}, u32[]{:S(2)}) collective-permute-start(bf16[1024,1024]{1,0:T(8,128)(2,1)} %add_convert_fusion.7.refs_1_), channel_id=1, source_target_pairs={{0,8},{24,16},{1,9},{25,17},{2,10},{26,18},{3,11},{27,19},{4,12},{... | collective-permute-start | bytes 6291464 | tf_op jit(solution)/shard_map/ppermute | solution.py:480
  434.0 63.0 %collective-permute-start.33 = (bf16[1024,1024]{1,0:T(8,128)(2,1)}, bf16[1024,1024]{1,0:T(8,128)(2,1)}, u32[]{:S(2)}, u32[]{:S(2)}) collective-permute-start(bf16[1024,1024]{1,0:T(8,128)(2,1)} %add_convert_fusion.6.refs_1_), channel_id=1, source_target_pairs={{8,16},{16,8},{9,17},{17,9},{10,18},{18,10},{11,19},{19,11},{12,20... | collective-permute-start | bytes 6291464 | tf_op jit(solution)/shard_map/ppermute | solution.py:480
  484.4 114.2 %collective-permute-start.52 = (bf16[2,512,1024]{2,1,0:T(8,128)(2,1)}, bf16[2,512,1024]{2,1,0:T(8,128)(2,1)}, u32[]{:S(2)}, u32[]{:S(2)}) collective-permute-start(bf16[2,512,1024]{2,1,0:T(8,128)(2,1)} %pad_maximum_fusion.14.refs_2_), channel_id=1, source_target_pairs={{0,8},{24,16},{1,9},{25,17},{2,10},{26,18},{3,11},{27,19},{4,12},{... | collective-permute-start | bytes 6291464 | tf_op jit(solution)/shard_map/ppermute | solution.py:480
  515.2 52.5 %collective-permute-start.56 = (bf16[1024,1024]{1,0:T(8,128)(2,1)S(1)}, bf16[1024,1024]{1,0:T(8,128)(2,1)}, u32[]{:S(2)}, u32[]{:S(2)}) collective-permute-start(bf16[1024,1024]{1,0:T(8,128)(2,1)S(1)} %copy-done.16), channel_id=1, source_target_pairs={{8,0},{16,24},{9,1},{17,25},{10,2},{18,26},{11,3},{19,27},{12,4},{... | collective-permute-start | bytes 6291464 | tf_op jit(solution)/shard_map/ppermute | solution.py:480
  572.2 59.4 %collective-permute-start.36 = (bf16[256,2048]{1,0:T(8,128)(2,1)}, bf16[256,2048]{1,0:T(8,128)(2,1)}, u32[]{:S(2)}, u32[]{:S(2)}) collective-permute-start(bf16[256,2048]{1,0:T(8,128)(2,1)} %slice.458), channel_id=1, source_target_pairs={{0,1},{1,0},{2,3},{3,2},{4,5},{5,4},{6,7},{7,6},{8,9},{9,8},{10,11... | collective-permute-start | bytes 3145736 | tf_op jit(solution)/shard_map/ppermute | solution.py:331
  631.6 107.7 %collective-permute-start.63 = (bf16[2,512,1024]{2,1,0:T(8,128)(2,1)}, bf16[2,512,1024]{2,1,0:T(8,128)(2,1)}, u32[]{:S(2)}, u32[]{:S(2)}) collective-permute-start(bf16[2,512,1024]{2,1,0:T(8,128)(2,1)} %pad_maximum_fusion.15.refs_2_), channel_id=1, source_target_pairs={{0,8},{24,16},{1,9},{25,17},{2,10},{26,18},{3,11},{27,19},{4,12},{... | collective-permute-start | bytes 6291464 | tf_op jit(solution)/shard_map/ppermute | solution.py:480
  641.4 74.7 %collective-permute-start.58 = (bf16[2,256,1024]{2,1,0:T(8,128)(2,1)}, bf16[2,256,1024]{2,1,0:T(8,128)(2,1)}, u32[]{:S(2)}, u32[]{:S(2)}) collective-permute-start(bf16[2,256,1024]{2,1,0:T(8,128)(2,1)} %constant_dynamic-slice_fusion.1.refs_1_), channel_id=1, source_target_pairs={{8,16},{16,8},{9,17},{17,9},{10,18},{18,10},{11,19},{19,11},{12,20... | collective-permute-start | bytes 3145736 | tf_op jit(solution)/shard_map/ppermute | solution.py:480
  643.1 71.1 %collective-permute-start.59 = (bf16[1024,1024]{1,0:T(8,128)(2,1)}, bf16[1024,1024]{1,0:T(8,128)(2,1)}, u32[]{:S(2)}, u32[]{:S(2)}) collective-permute-start(bf16[1024,1024]{1,0:T(8,128)(2,1)} %broadcast_select_fusion.1.refs_1_), channel_id=1, source_target_pairs={{0,4},{4,0},{1,5},{5,1},{2,6},{6,2},{3,7},{7,3},{8,12},{12,8},{9,1... | collective-permute-start | bytes 6291464 | tf_op jit(solution)/shard_map/ppermute | solution.py:339
  644.6 80.9 %collective-permute-start.66 = (bf16[1024,1024]{1,0:T(8,128)(2,1)}, bf16[1024,1024]{1,0:T(8,128)(2,1)}, u32[]{:S(2)}, u32[]{:S(2)}) collective-permute-start(bf16[1024,1024]{1,0:T(8,128)(2,1)} %add_convert_fusion.3.refs_2_), channel_id=1, source_target_pairs={{8,16},{16,8},{9,17},{17,9},{10,18},{18,10},{11,19},{19,11},{12,20... | collective-permute-start | bytes 6291464 | tf_op jit(solution)/shard_map/ppermute | solution.py:480
  725.5 124.1 %collective-permute-start.68 = (bf16[2048,256]{1,0:T(8,128)(2,1)}, bf16[2048,256]{1,0:T(8,128)(2,1)}, u32[]{:S(2)}, u32[]{:S(2)}) collective-permute-start(bf16[2048,256]{1,0:T(8,128)(2,1)} %convolution_convert_fusion.15), channel_id=1, source_target_pairs={{0,8},{24,16},{1,9},{25,17},{2,10},{26,18},{3,11},{27,19},{4,12},{... | collective-permute-start | bytes 3145736 | tf_op jit(solution)/shard_map/ppermute | solution.py:480
  732.5 142.3 %collective-permute-start.75 = (bf16[2048,256]{1,0:T(8,128)(2,1)}, bf16[2048,256]{1,0:T(8,128)(2,1)}, u32[]{:S(2)}, u32[]{:S(2)}) collective-permute-start(bf16[2048,256]{1,0:T(8,128)(2,1)} %convolution_convert_fusion.14), channel_id=1, source_target_pairs={{0,8},{24,16},{1,9},{25,17},{2,10},{26,18},{3,11},{27,19},{4,12},{... | collective-permute-start | bytes 3145736 | tf_op jit(solution)/shard_map/ppermute | solution.py:480
  739.3 67.6 %collective-permute-start.71 = (bf16[2,256,1024]{2,1,0:T(8,128)(2,1)}, bf16[2,256,1024]{2,1,0:T(8,128)(2,1)}, u32[]{:S(2)}, u32[]{:S(2)}) collective-permute-start(bf16[2,256,1024]{2,1,0:T(8,128)(2,1)} %get-tuple-element.38.refs_1_), channel_id=1, source_target_pairs={{8,0},{16,24},{9,1},{17,25},{10,2},{18,26},{11,3},{19,27},{12,4},{... | collective-permute-start | bytes 3145736 | tf_op jit(solution)/shard_map/ppermute | solution.py:480
  761.0 49.9 %collective-permute-start.70 = (bf16[2,256,1024]{2,1,0:T(8,128)(2,1)}, bf16[2,256,1024]{2,1,0:T(8,128)(2,1)}, u32[]{:S(2)}, u32[]{:S(2)}) collective-permute-start(bf16[2,256,1024]{2,1,0:T(8,128)(2,1)} %constant_dynamic-slice_fusion.refs_1_), channel_id=1, source_target_pairs={{8,16},{16,8},{9,17},{17,9},{10,18},{18,10},{11,19},{19,11},{12,20... | collective-permute-start | bytes 3145736 | tf_op jit(solution)/shard_map/ppermute | solution.py:480
  867.2 86.5 %collective-permute-start.83 = (bf16[2,256,1024]{2,1,0:T(8,128)(2,1)}, bf16[2,256,1024]{2,1,0:T(8,128)(2,1)}, u32[]{:S(2)}, u32[]{:S(2)}) collective-permute-start(bf16[2,256,1024]{2,1,0:T(8,128)(2,1)} %get-tuple-element.40.refs_1_), channel_id=1, source_target_pairs={{8,0},{16,24},{9,1},{17,25},{10,2},{18,26},{11,3},{19,27},{12,4},{... | collective-permute-start | bytes 3145736 | tf_op jit(solution)/shard_map/ppermute | solution.py:480
  870.8 143.6 %collective-permute-start.88 = (bf16[1024,1024]{1,0:T(8,128)(2,1)S(1)}, bf16[1024,1024]{1,0:T(8,128)(2,1)}, u32[]{:S(2)}, u32[]{:S(2)}) collective-permute-start(bf16[1024,1024]{1,0:T(8,128)(2,1)S(1)} %copy-done.14), channel_id=1, source_target_pairs={{0,4},{4,0},{1,5},{5,1},{2,6},{6,2},{3,7},{7,3},{8,12},{12,8},{9,1... | collective-permute-start | bytes 6291464 | tf_op jit(solution)/shard_map/ppermute | solution.py:339
  874.8 71.1 %collective-permute-start.84 = (bf16[256,2048]{1,0:T(8,128)(2,1)S(1)}, bf16[256,2048]{1,0:T(8,128)(2,1)}, u32[]{:S(2)}, u32[]{:S(2)}) collective-permute-start(bf16[256,2048]{1,0:T(8,128)(2,1)S(1)} %copy-done.35), channel_id=1, source_target_pairs={{8,0},{16,24},{9,1},{17,25},{10,2},{18,26},{11,3},{19,27},{12,4},{... | collective-permute-start | bytes 3145736 | tf_op jit(solution)/shard_map/ppermute | solution.py:480
  900.9 114.8 %collective-permute-start.86 = (bf16[2,256,1024]{2,1,0:T(8,128)(2,1)}, bf16[2,256,1024]{2,1,0:T(8,128)(2,1)}, u32[]{:S(2)}, u32[]{:S(2)}) collective-permute-start(bf16[2,256,1024]{2,1,0:T(8,128)(2,1)} %get-tuple-element.44.refs_1_), channel_id=1, source_target_pairs={{8,0},{16,24},{9,1},{17,25},{10,2},{18,26},{11,3},{19,27},{12,4},{... | collective-permute-start | bytes 3145736 | tf_op jit(solution)/shard_map/ppermute | solution.py:480
  902.2 90.4 %collective-permute-start.89 = (bf16[2,256,1024]{2,1,0:T(8,128)(2,1)}, bf16[2,256,1024]{2,1,0:T(8,128)(2,1)}, u32[]{:S(2)}, u32[]{:S(2)}) collective-permute-start(bf16[2,256,1024]{2,1,0:T(8,128)(2,1)} %add_convert_fusion.13.refs_3_), channel_id=1, source_target_pairs={{8,16},{16,8},{9,17},{17,9},{10,18},{18,10},{11,19},{19,11},{12,20... | collective-permute-start | bytes 3145736 | tf_op jit(solution)/shard_map/ppermute | solution.py:480
  (226 other events, 3149.4 us)

commit v2 on v1

--- a/solution.py
+++ b/solution.py
@@ -14,7 +14,8 @@
 BIG = 2.0 ** 100
 SLOPE_COL = 16
 LSE_COL = 24
-VMEM_LIMIT = 60 * 1024 * 1024
+VMEM_LIMIT = 36 * 1024 * 1024
+MATMUL_LIMIT = 26 * 1024 * 1024
 
 
 def dot_nt(left, right):
@@ -91,7 +92,7 @@
     return [lane < HD, lane >= HD], lane
 
 
-def forward_kernel(place, lists, qkv, fq, fk, srow, o, lse, qa, vt, top, acc, *, block, pairs):
+def forward_kernel(first_block, place, lists, qkv, fq, fk, srow, o, lse, qa, vt, top, acc, *, block, pairs):
     count = qkv.shape[0] // block
     width = pairs * LANES
     heads = 2 * pairs
@@ -101,6 +102,7 @@
     row = lax.broadcasted_iota(jnp.int32, (block, block), 0)
     col = lax.broadcasted_iota(jnp.int32, (block, block), 1)
     diagonal = row <= col
+    side_blocks = count // 2
 
     def spot(index):
         return pl.ds(pl.multiple_of(place[index] * block, block), block)
@@ -137,7 +139,8 @@
             acc[h] = mixed[h] if first else acc[h] * scales[h] + mixed[h]
             top[h : h + 1, :] = bests[h]
 
-    def rows(i, _):
+    def rows(n, _):
+        i = place[first_block[0] + n]
         query_features = fq[canon(i), :]
         for pair in range(pairs):
             cols = slice(pair * LANES, (pair + 1) * LANES)
@@ -149,8 +152,8 @@
                 )
         step(i, True)
 
-        def other(n, _):
-            step(lists[i, n + 1], False)
+        def other(m, _):
+            step(lists[i, m + 1], False)
             return 0
 
         lax.fori_loop(0, lists[i, 0], other, 0)
@@ -162,15 +165,17 @@
                 total = acc[h, HD : HD + 1, :]
                 mixed.append(acc[h, :HD, :] / total)
                 logs.append(top[h : h + 1, :] + jnp.log(total))
-            o[spot(i), cols] = jnp.concatenate(mixed, axis=0).T.astype(o.dtype)
+            o[canon(n), cols] = jnp.concatenate(mixed, axis=0).T.astype(o.dtype)
         logs.append(jnp.zeros((LANES - heads, block), jnp.float32))
-        lse[canon(i), :] = jnp.concatenate(logs, axis=0).T
+        lse[canon(n), :] = jnp.concatenate(logs, axis=0).T
         return 0
 
-    lax.fori_loop(0, count, rows, 0)
-
-
-def backward_kernel(place, lists, qkv, do, o, fq, fk, srow, lse, dqkv, qa, da, dqa, dka, dva, *, block, pairs):
+    lax.fori_loop(0, o.shape[0] // block, rows, 0)
+
+
+def backward_kernel(
+    place, lists, qkv, do, o_own, o_other, fq, fk, srow, lse_own, lse_other, dqkv, qa, da, dqa, dka, dva, *, block, pairs
+):
     count = qkv.shape[0] // block
     width = pairs * LANES
     heads = 2 * pairs
@@ -180,6 +185,7 @@
     col = lax.broadcasted_iota(jnp.int32, (block, block), 1)
     diagonal = row <= col
     ones = jnp.where(lane < 3, 1.0, 0.0).astype(jnp.bfloat16)
+    side_blocks = count // 2
 
     def spot(index):
         return pl.ds(pl.multiple_of(place[index] * block, block), block)
@@ -195,12 +201,15 @@
 
     def prepare(i, _):
         query_features = fq[canon(i), :]
-        logs = lse[canon(i), :]
+        own = place[i] < side_blocks
+        mixed_rows = canon(place[i] % side_blocks)
+        logs = jnp.where(own, lse_own[mixed_rows, :], lse_other[mixed_rows, :])
         for pair in range(pairs):
             cols = slice(pair * LANES, (pair + 1) * LANES)
             queries = qkv[spot(i), cols] * jnp.bfloat16(HD ** -0.5)
             grads = do[spot(i), cols]
-            product = grads.astype(jnp.float32) * o[spot(i), cols].astype(jnp.float32)
+            mixed = jnp.where(own, o_own[mixed_rows, cols], o_other[mixed_rows, cols])
+            product = grads.astype(jnp.float32) * mixed.astype(jnp.float32)
             for side in range(2):
                 h = 2 * pair + side
                 delta = jnp.sum(jnp.where(halves[side], product, 0.0), axis=1, keepdims=True)
@@ -268,47 +277,61 @@
     lax.fori_loop(0, count, finish, 0)
 
 
-def _specs(number):
-    return [pl.BlockSpec(memory_space=pltpu.SMEM)] * 2 + [pl.BlockSpec(memory_space=pltpu.VMEM)] * number
-
-
-def attention_forward(place, lists, qkv, fq, fk, srow, block):
+def cost(microseconds):
+    return pl.CostEstimate(flops=int(microseconds * 1.15e9), bytes_accessed=0, transcendentals=0)
+
+
+def _attention_call(name, kernel, scalars, arrays, outs, scratch, microseconds):
+    vmem = pl.BlockSpec(memory_space=pltpu.VMEM)
+    return pl.pallas_call(
+        kernel,
+        out_shape=outs,
+        in_specs=[pl.BlockSpec(memory_space=pltpu.SMEM)] * len(scalars) + [vmem] * len(arrays),
+        out_specs=[vmem] * len(outs),
+        scratch_shapes=scratch,
+        compiler_params=pltpu.CompilerParams(vmem_limit_bytes=VMEM_LIMIT),
+        cost_estimate=cost(microseconds),
+        name=name,
+    )(*scalars, *arrays)
+
+
+def attention_forward(first_block, count, place, lists, qkv, fq, fk, srow, block):
     whole, width = qkv.shape[0], qkv.shape[1] // 3
     pairs = width // LANES
-    return pl.pallas_call(
+    return _attention_call(
+        "attention_forward",
         partial(forward_kernel, block=block, pairs=pairs),
-        out_shape=(jax.ShapeDtypeStruct((whole, width), jnp.bfloat16), jax.ShapeDtypeStruct((whole, LANES), jnp.float32)),
-        in_specs=_specs(4),
-        out_specs=(pl.BlockSpec(memory_space=pltpu.VMEM),) * 2,
-        scratch_shapes=[
+        (first_block.reshape(1), place, lists),
+        (qkv, fq, fk, srow),
+        [jax.ShapeDtypeStruct((count * block, width), jnp.bfloat16), jax.ShapeDtypeStruct((count * block, LANES), jnp.float32)],
+        [
             pltpu.VMEM((2 * pairs, block, 2 * LANES), jnp.bfloat16),
             pltpu.VMEM((whole // block, 2 * pairs, HD + 16, block), jnp.bfloat16),
             pltpu.VMEM((8, block), jnp.float32),
             pltpu.VMEM((2 * pairs, HD + 16, block), jnp.float32),
         ],
-        compiler_params=pltpu.CompilerParams(vmem_limit_bytes=VMEM_LIMIT),
-        name="attention_forward",
-    )(place, lists, qkv, fq, fk, srow)
+        0,
+    )
 
 
 def attention_backward(place, lists, qkv, do, o, fq, fk, srow, lse, block):
     whole, width = do.shape
     pairs = width // LANES
-    return pl.pallas_call(
+    return _attention_call(
+        "attention_backward",
         partial(backward_kernel, block=block, pairs=pairs),
-        out_shape=jax.ShapeDtypeStruct((whole, 3 * width), jnp.bfloat16),
-        in_specs=_specs(7),
-        out_specs=pl.BlockSpec(memory_space=pltpu.VMEM),
-        scratch_shapes=[
+        (place, lists),
+        (qkv, do, *o, fq, fk, srow, *lse),
+        [jax.ShapeDtypeStruct((whole, 3 * width), jnp.bfloat16)],
+        [
             pltpu.VMEM((2 * pairs, whole, 2 * LANES), jnp.bfloat16),
             pltpu.VMEM((2 * pairs, whole, 2 * LANES), jnp.bfloat16),
             pltpu.VMEM((whole // block, width, block), jnp.float32),
             pltpu.VMEM((block, width), jnp.float32),
             pltpu.VMEM((block, width), jnp.float32),
         ],
-        compiler_params=pltpu.CompilerParams(vmem_limit_bytes=VMEM_LIMIT),
-        name="attention_backward",
-    )(place, lists, qkv, do, o, fq, fk, srow, lse)
+        0,
+    )[0]
 
 
 CORE = [(0, 1), (1, 0), (2, 3), (3, 2)]
@@ -428,94 +451,8 @@
     return wide(own) + wide(over(other))
 
 
-def tie(values, after):
-    count = len(values)
-    return pl.pallas_call(
-        lambda *refs: None,
-        out_shape=[jax.ShapeDtypeStruct(v.shape, v.dtype) for v in values],
-        in_specs=[pl.BlockSpec(memory_space=pl.ANY)] * (count + len(after)),
-        out_specs=[pl.BlockSpec(memory_space=pl.ANY)] * count,
-        input_output_aliases={i: i for i in range(count)},
-        name="tie",
-    )(*values, *after)
-
-
-class Hops:
-    def __init__(self, steps):
-        self.steps = steps
-        self.pending, self.sent = next(steps)
-        self.result = None
-
-    def arrived(self, values):
-        try:
-            self.pending, self.sent = self.steps.send(values)
-        except StopIteration as stop:
-            self.pending, self.sent, self.result = [], [], stop.value
-
-
-class Order:
-    def __init__(self, after):
-        self.after = [after]
-
-    def enter(self, *values):
-        out = tie(list(values), self.after)
-        self.after = [out[0]]
-        return out
-
-    def done(self, *values):
-        self.after.extend(values)
-
-    def wait(self, *hops):
-        values = [v for h in hops for v in h.pending]
-        out = self.enter(*values)
-        self.after = []
-        for h in hops:
-            count = len(h.pending)
-            h.arrived(out[:count])
-            self.after.extend(h.sent if h.sent else h.result)
-            out = out[count:]
-
-
 def on_line(value, pairs):
     return lax.ppermute(value, "dp", pairs)
-
-
-def at_end():
-    place = lax.axis_index("dp")
-    return (place == 0) | (place == 3)
-
-
-def line_hops(mine):
-    (arrived,) = yield [on_line(mine, INWARD)], [mine]
-    inner = low(wide(mine) + wide(arrived))
-    (arrived,) = yield [on_line(inner, MIDDLE)], [inner]
-    total = low(wide(inner) + wide(arrived))
-    (arrived,) = yield [on_line(total, OUTWARD)], [total]
-    total = low(jnp.where(at_end(), arrived, total))
-    (arrived,) = yield [over(total)], [total]
-    return [total, arrived]
-
-
-def pair_hops(own, other):
-    (arrived,) = yield [over(other)], [other, own]
-    return (yield from line_hops(low(wide(own) + wide(arrived))))
-
-
-def middle_hops(both):
-    (arrived,) = yield [on_line(both, INWARD)], [both]
-    inner = low(wide(both) + wide(arrived))
-    size = both.shape[1] // 2
-    upper = lax.axis_index("dp") // 2
-    keep = lax.dynamic_slice_in_dim(inner, upper * size, size, 1)
-    give = low(lax.dynamic_slice_in_dim(inner, (1 - upper) * size, size, 1))
-    (arrived,) = yield [on_line(give, MIDDLE)], [give]
-    kept = low(wide(keep) + wide(arrived))
-    (arrived,) = yield [over(kept)], [kept]
-    total = low(wide(kept) + wide(jnp.concatenate([arrived[1:], arrived[:1]])))
-    first, second = yield [on_line(total, MIDDLE), on_line(total, OUTWARD)], [total]
-    total = low(jnp.where(at_end(), second, total))
-    (arrived,) = yield [on_line(first, OUTWARD)], [first, total]
-    return [total, low(jnp.where(at_end(), arrived, first))]
 
 
 def vector_sum(group, pair):
@@ -530,7 +467,111 @@
     return lax.psum(group, ("dp", "seq", "tensor")), lax.psum(pair, ("dp", "seq"))
 
 
-def local(
+def tie(values, after, name):
+    count = len(values)
+    return pl.pallas_call(
+        lambda *refs: None,
+        out_shape=[jax.ShapeDtypeStruct(v.shape, v.dtype) for v in values],
+        in_specs=[pl.BlockSpec(memory_space=pl.ANY)] * (count + len(after)),
+        out_specs=[pl.BlockSpec(memory_space=pl.ANY)] * count,
+        input_output_aliases={i: i for i in range(count)},
+        compiler_params=pltpu.CompilerParams(vmem_limit_bytes=1 << 16),
+        cost_estimate=cost(0),
+        name="tie_" + name,
+    )(*values, *after)
+
+
+class Order:
+    def __init__(self):
+        self.after, self.label = [], "front"
+
+    def enter(self, *values):
+        out = tie(list(values), self.after, self.label)
+        self.after = [out[0]]
+        return out if len(out) > 1 else out[0]
+
+    def done(self, *values):
+        self.after.extend(values)
+
+
+def feed_forward(pieces, weight, bias, grads, act, up_grad, chunk, tile=512):
+    half, model, units = 2 * pieces[0].shape[0], weight.shape[0], weight.shape[1]
+
+    def kernel(first, second, weight_ref, bias_ref, grads_ref, *refs):
+        act_ref, up_ref, sums_ref = refs[-3:]
+        rows = jnp.concatenate([first[...], second[...]], axis=0)
+        pre = dot_nn(rows, weight_ref[...]) + wide(bias_ref[...])
+        cdf = 0.5 * (1.0 + lax.erf(pre * (0.5**0.5)))
+        act_ref[...] = (pre * cdf).astype(jnp.bfloat16)
+        slope = cdf + pre * (jnp.exp(-0.5 * pre * pre) * 0.3989422804014327)
+        low_grad = (wide(grads_ref[...]) * slope).astype(jnp.bfloat16)
+        up_ref[...] = low_grad
+        sums_ref[...] = jnp.broadcast_to(jnp.sum(wide(low_grad), axis=0, keepdims=True), sums_ref.shape)
+
+    there = pl.BlockSpec(memory_space=pl.ANY)
+    whole = pl.BlockSpec(pieces[0].shape, lambda n: (0, 0))
+    filled = pl.BlockSpec((half, tile), lambda n: (chunk, n))
+    held = [] if act is None else [act, up_grad]
+    return pl.pallas_call(
+        kernel,
+        grid=(units // tile,),
+        out_shape=[jax.ShapeDtypeStruct((2 * half, units), jnp.bfloat16)] * 2 + [jax.ShapeDtypeStruct((8, units), jnp.float32)],
+        in_specs=[
+            whole,
+            whole,
+            pl.BlockSpec((model, tile), lambda n: (0, n)),
+            pl.BlockSpec((1, tile), lambda n: (0, n)),
+            pl.BlockSpec((half, tile), lambda n: (0, n)),
+            *[there] * len(held),
+        ],
+        out_specs=[filled, filled, pl.BlockSpec((8, tile), lambda n: (0, n))],
+        input_output_aliases={5: 0, 6: 1} if held else {},
+        compiler_params=pltpu.CompilerParams(vmem_limit_bytes=MATMUL_LIMIT),
+        cost_estimate=cost(0),
+        name="feed_forward",
+    )(*pieces, weight, bias.reshape(1, -1), grads, *held)
+
+
+def blank(shape):
+    return pl.pallas_call(
+        lambda out: None,
+        out_shape=jax.ShapeDtypeStruct(shape, jnp.float32),
+        out_specs=pl.BlockSpec(memory_space=pl.ANY),
+        compiler_params=pltpu.CompilerParams(vmem_limit_bytes=1 << 16),
+        cost_estimate=cost(0),
+        name="blank",
+    )()
+
+
+DOTS = {"nn": dot_nn, "nt": dot_nt, "tn": dot_tn}
+
+
+def matmul(name, kind, where, grid, left, right, outs, axis=0):
+    def kernel(where_ref, left_ref, right_ref, *out_refs):
+        total = DOTS[kind](left_ref[...], right_ref[...])
+        start = 0
+        for out in out_refs:
+            size = out.shape[axis]
+            piece = total[start : start + size] if axis == 0 else total[:, start : start + size]
+            out[...] = piece.astype(jnp.bfloat16)
+            start += size
+
+    return pl.pallas_call(
+        kernel,
+        grid_spec=pltpu.PrefetchScalarGridSpec(
+            num_scalar_prefetch=1,
+            grid=grid,
+            in_specs=[pl.BlockSpec(block, index) for _, block, index in (left, right)],
+            out_specs=[pl.BlockSpec(block, index) for _, block, index in outs],
+        ),
+        out_shape=[jax.ShapeDtypeStruct(shape, jnp.bfloat16) for shape, _, _ in outs],
+        compiler_params=pltpu.CompilerParams(vmem_limit_bytes=MATMUL_LIMIT),
+        cost_estimate=cost(0),
+        name=name,
+    )(where, left[0], right[0])
+
+
+def plain_local(
     hidden_in, norm1_gain, norm1_bias, query_weight, query_bias, key_weight, value_weight, value_bias, out_weight,
     out_bias, norm2_gain, norm2_bias, up_weight, up_bias, down_weight, down_bias, seg_lengths, parents, out_grad,
 ):
@@ -548,8 +589,6 @@
     f32 = jnp.float32
     gain_one, gain_two = wide(norm1_gain), wide(norm2_gain)
 
-    quick = tensor_count == 4 and lax.axis_size("dp") == 4
-
     inputs = wide(hidden_in)
     first, normed_one, inverse_one = norm_forward(inputs, gain_one, wide(norm1_bias))
     chunks_one = gather_slot(low(first))
@@ -576,11 +615,11 @@
     qkv = jnp.concatenate(
         [(jnp.dot(rows, qkv_weight, preferred_element_type=f32) + wide(qkv_bias)).astype(jnp.bfloat16) for rows in chunks_one]
     )
-    order = Order(qkv)
-    (out_grad_late,) = order.enter(out_grad)
-    grad_near, grad_far = gather_group(out_grad_late)
-    mixed, log_totals = attention_forward(place, key_lists, qkv, fq, fk, slope_rows, block)
-    heads_out = jnp.concatenate([mixed[:group], over(mixed[group:])], axis=1)
+    grad_near, grad_far = gather_group(out_grad)
+    side = whole // block // 2
+    mixed_other, logs_other = attention_forward(jnp.int32(side), side, place, key_lists, qkv, fq, fk, slope_rows, block)
+    mixed_own, logs_own = attention_forward(jnp.int32(0), side, place, key_lists, qkv, fq, fk, slope_rows, block)
+    heads_out = jnp.concatenate([mixed_own, over(mixed_other)], axis=1)
     half = group // 2
 
     def product(left, right):
@@ -594,14 +633,10 @@
 
     branch = scatter_group(product(heads_out[half:], out_rel), product(heads_out[:half], out_rel)) + wide(out_bias)
     act_grad_near = low(dot_nt(grad_near, down_rel))
-    order = Order(act_grad_near)
-    (branch,) = order.enter(branch)
     middle = inputs + branch
     second, normed_two, inverse_two = norm_forward(middle, gain_two, wide(norm2_bias))
     two_near, two_far = gather_group(low(second))
     act_grad_far = low(dot_nt(grad_far, down_rel))
-    order = Order(act_grad_far)
-    (two_far,) = order.enter(two_far)
     activated, up_grad = [], []
     for rows, grads in ((two_near, act_grad_near), (two_far, act_grad_far)):
         pre = jnp.dot(rows, up_rel, preferred_element_type=f32) + up_bias_rel
@@ -639,7 +674,8 @@
 
     def attention_grads(arrived, near_grads):
         return attention_backward(
-            place, query_lists, qkv, jnp.concatenate([near_grads, arrived]), mixed, fq, fk, slope_rows, log_totals, block
+            place, query_lists, qkv, jnp.concatenate([near_grads, arrived]), (mixed_own, mixed_other),
+            fq, fk, slope_rows, (logs_own, logs_other), block,
         )
 
     def first_grads(grads):
@@ -648,121 +684,22 @@
     def qkv_part(grads, index):
         return low_dot(rows_one, grads[:, index * width : (index + 1) * width])
 
-    if quick:
-        order = Order(up_grad_all)
-        (act_all,) = order.enter(act_all)
-        down0 = Hops(pair_hops(*down_parts(0)))
-        order.done(*down0.sent)
-        (up_grad_all,) = order.enter(up_grad_all)
-        up0 = Hops(middle_hops(up_parts(0)))
-        order.done(*up0.sent)
-        (up_grad_all,) = order.enter(up_grad_all)
-        second_far = product_nt(up_grad_all[half:], up_rel)()
-        second_size = half // 2
-        second_sent = low(wide(second_far[:second_size]) + wide(core(second_far[second_size:])))
-        second_back = across(second_sent)
-        order.done(second_sent)
-        (act_all,) = order.enter(act_all)
-        down1 = Hops(pair_hops(*down_parts(1)))
-        order.done(*down1.sent)
-        (up_grad_all,) = order.enter(up_grad_all)
-        second_near = product_nt(up_grad_all[:half], up_rel)()
-        second_own = wide(second_near[:second_size]) + wide(core(second_near[second_size:]))
-        order.done(second_own)
-        (second_back,) = order.enter(second_back)
-        middle_grad, grad_norm2_gain, grad_norm2_bias = norm_two(second_own + wide(second_back))
-        branch_grad = low(middle_grad)
-        branch_near, branch_far = gather_group(branch_grad)
-        order.done(branch_grad)
-        (act_all,) = order.enter(act_all)
-        ffn_out = ffn_sum()
-        grad_up_bias = jnp.sum(wide(up_grad_all), axis=0)
-        order.wait(down0)
-        order.wait(up0)
-        (branch_far,) = order.enter(branch_far)
-        heads_grad = jnp.concatenate([heads_grads(branch_near), heads_grads(branch_far)])
-        heads_grad_sent = low(heads_grad[:, width:])
-        heads_grad_back = over(heads_grad_sent)
-        order.done(heads_grad, heads_grad_sent)
-        (up_grad_all,) = order.enter(up_grad_all)
-        up1 = Hops(middle_hops(up_parts(1)))
-        order.done(*up1.sent)
-        order.wait(up0)
-        branch_rows = jnp.concatenate([branch_near, branch_far])
-        order.wait(down1)
-        order.wait(down0)
-        (heads_grad_back,) = order.enter(heads_grad_back)
-        grads = attention_grads(heads_grad_back, heads_grad[:, :width])
-        order.done(grads)
-        (up_grad_all,) = order.enter(up_grad_all)
-        up2 = Hops(middle_hops(up_parts(2)))
-        order.done(*up2.sent)
-        order.wait(up0)
-        order.wait(up1)
-        order.wait(down0)
-        (grads,) = order.enter(grads)
-        first_grad = first_grads(grads)
-        out0 = Hops(pair_hops(low_dot(heads_out[:, :width], branch_rows), low_dot(heads_out[:, width:], branch_rows)))
-        order.done(*out0.sent)
-        order.wait(up1)
-        (up_grad_all,) = order.enter(up_grad_all)
-        up3 = Hops(middle_hops(up_parts(3)))
-        order.done(*up3.sent)
-        qkv0 = Hops(line_hops(qkv_part(grads, 0)))
-        order.wait(down0)
-        order.wait(down1)
-        order.wait(up0)
-        order.wait(up2)
-        order.wait(out0)
-        order.wait(up1)
-        qkv1 = Hops(line_hops(qkv_part(grads, 1)))
-        qkv2 = Hops(line_hops(qkv_part(grads, 2)))
-        order.wait(down0)
-        order.wait(up2)
-        order.wait(down1)
-        order.wait(up1)
-        order.wait(up3)
-        order.wait(up2)
-        order.wait(qkv0)
-        order.wait(out0)
-        order.wait(up0)
-        order.wait(up3)
-        order.wait(down1)
-        order.wait(qkv0, qkv1)
-        order.wait(out0)
-        order.wait(up2)
-        order.wait(up3)
-        order.wait(qkv0, qkv1, qkv2)
-        order.wait(out0)
-        order.wait(up1)
-        order.wait(qkv1, qkv2)
-        order.wait(up3)
-        order.wait(down1)
-        order.wait(out0)
-        order.wait(up2)
-        order.wait(qkv0, qkv2)
-        order.wait(up3)
-        order.wait(qkv1)
-        order.wait(qkv2)
-        for h in (down0, down1, up0, up1, up2, up3, out0, qkv0, qkv1, qkv2):
-            assert h.result is not None
-    else:
-        second_grad = scatter_group(product_nt(up_grad[1], up_rel), product_nt(up_grad[0], up_rel))
-        middle_grad, grad_norm2_gain, grad_norm2_bias = norm_two(second_grad)
-        branch_grad = low(middle_grad)
-        branch_near, branch_far = gather_group(branch_grad)
-        ffn_out = ffn_sum()
-        grad_up_bias = jnp.sum(wide(up_grad_all), axis=0)
-        heads_grad = jnp.concatenate([heads_grads(branch_near), heads_grads(branch_far)])
-        grads = attention_grads(over(heads_grad[:, width:]), heads_grad[:, :width])
-        branch_rows = jnp.concatenate([branch_near, branch_far])
-        first_grad = first_grads(grads)
-        sums = [[*down_parts(0)], [*down_parts(1)], *[[up[0], up[1]] for up in map(up_parts, range(4))]]
-        sums.append([low_dot(heads_out[:, :width], branch_rows), low_dot(heads_out[:, width:], branch_rows)])
-        axes = [0, 0, 1, 1, 1, 1, 0, 1, 1, 1]
-        for i in range(3):
-            sums.append([qkv_part(grads, i), jnp.zeros((model, width), jnp.bfloat16)])
-        sums = [lax.psum(in_order(own, other, axis, seq), ("dp", "seq")) for (own, other), axis in zip(sums, axes)]
+    second_grad = scatter_group(product_nt(up_grad[1], up_rel), product_nt(up_grad[0], up_rel))
+    middle_grad, grad_norm2_gain, grad_norm2_bias = norm_two(second_grad)
+    branch_grad = low(middle_grad)
+    branch_near, branch_far = gather_group(branch_grad)
+    ffn_out = ffn_sum()
+    grad_up_bias = jnp.sum(wide(up_grad_all), axis=0)
+    heads_grad = jnp.concatenate([heads_grads(branch_near), heads_grads(branch_far)])
+    grads = attention_grads(over(heads_grad[:, width:]), heads_grad[:, :width])
+    branch_rows = jnp.concatenate([branch_near, branch_far])
+    first_grad = first_grads(grads)
+    sums = [[*down_parts(0)], [*down_parts(1)], *[[up[0], up[1]] for up in map(up_parts, range(4))]]
+    sums.append([low_dot(heads_out[:, :width], branch_rows), low_dot(heads_out[:, width:], branch_rows)])
+    axes = [0, 0, 1, 1, 1, 1, 0, 1, 1, 1]
+    for i in range(3):
+        sums.append([qkv_part(grads, i), jnp.zeros((model, width), jnp.bfloat16)])
+    sums = [lax.psum(in_order(own, other, axis, seq), ("dp", "seq")) for (own, other), axis in zip(sums, axes)]
 
     layer_out = (middle + ffn_out).astype(jnp.bfloat16)
     grad_down_bias = jnp.sum(cotangent, axis=0)
@@ -782,32 +719,10 @@
     )
     pair_rows = pair_rows.reshape(-1)
 
-    def put(out, value, row, column):
-        return lax.dynamic_update_slice(out, wide(value), (row, column))
-
-    if quick:
-        down = jnp.zeros((units, model), f32)
-        for i, (own, other) in enumerate((down0.result, down1.result)):
-            down = put(down, own, seq * part, i * (model // 2))
-            down = put(down, other, (1 - seq) * part, i * (model // 2))
-        up = jnp.zeros((model, units), f32)
-        upper = lax.axis_index("dp") // 2
-        for i, h in enumerate((up0, up1, up2, up3)):
-            for value, side in zip(h.result, (upper, 1 - upper)):
-                row = i * quarter + side * (quarter // 2)
-                up = put(up, value[0], row, seq * part)
-                up = put(up, value[1], row, (1 - seq) * part)
-        out = jnp.zeros((columns, model), f32)
-        out = put(put(out, out0.result[0], seq * width, 0), out0.result[1], (1 - seq) * width, 0)
-        qkv_out = []
-        for h in (qkv0, qkv1, qkv2):
-            empty = jnp.zeros((model, columns), f32)
-            qkv_out.append(put(put(empty, h.result[0], 0, seq * width), h.result[1], 0, (1 - seq) * width))
-    else:
-        down = wide(jnp.concatenate(sums[:2], axis=1))
-        up = wide(jnp.concatenate(sums[2:6], axis=0))
-        out = wide(sums[6])
-        qkv_out = [wide(v) for v in sums[7:]]
+    down = wide(jnp.concatenate(sums[:2], axis=1))
+    up = wide(jnp.concatenate(sums[2:6], axis=0))
+    out = wide(sums[6])
+    qkv_out = [wide(v) for v in sums[7:]]
 
     return (
         layer_out,
@@ -828,6 +743,445 @@
         down,
         group_rows[5],
     )
+
+
+ORDER = " ".join((
+    "U0 SF SFa D0", "SN U2 S u0", "BN d0 BF u0", "D1 u2 ATT u0", "d0 u2 d1 u0", "F3 u2 Q0 u0",
+    "FB F1 d0 F2", "d1 U3 O u2", "FE FL q0 F0", "d0 o d1 u3", "u2 FN Q1 q0", "o u3 d0 d1",
+    "U1 q1 o u3", "q0 o q1 u1", "GF V d1 u3", "q0 u1 GFa q1", "v o u3 u1", "GN u1 v v",
+    "v v q1 u1",
+)).split()
+
+
+def line_steps(mine):
+    arrived = yield [on_line(mine, INWARD)], [mine]
+    inner = low(wide(mine) + wide(arrived))
+    arrived = yield [on_line(inner, MIDDLE)], [inner]
+    total = low(wide(inner) + wide(arrived))
+    arrived = yield [on_line(total, OUTWARD)], [total]
+    line = lax.axis_index("dp")
+    total = low(jnp.where((line == 0) | (line == 3), arrived, total))
+    arrived = yield [over(total)], [total]
+    return total, arrived
+
+
+def pair_steps(own, other):
+    arrived = yield [over(other)], [other, own]
+    return (yield from line_steps(low(wide(own) + wide(arrived))))
+
+
+def middle_steps(value):
+    arrived = yield [on_line(value, INWARD)], [value]
+    inner = wide(value) + wide(arrived)
+    size = value.shape[0] // 2
+    line = lax.axis_index("dp")
+    upper, end = line // 2, (line == 0) | (line == 3)
+    keep = lax.dynamic_slice_in_dim(inner, upper * size, size, 0)
+    give = low(lax.dynamic_slice_in_dim(inner, (1 - upper) * size, size, 0))
+    arrived = yield [on_line(give, MIDDLE)], [give]
+    kept = low(keep + wide(arrived))
+    arrived = yield [over(kept)], [kept]
+    total = low(wide(kept) + wide(arrived))
+    arrived, outer = yield [on_line(total, MIDDLE), on_line(total, OUTWARD)], [total]
+    total = low(jnp.where(end, outer, total))
+    last = yield [on_line(arrived, OUTWARD)], [arrived, total]
+    return total, low(jnp.where(end, last, arrived))
+
+
+def vector_steps(group, pair):
+    arrived = yield [core(group)], [group]
+    group = group + arrived
+    arrived = yield [across(group)], [group]
+    rows = jnp.concatenate([group + arrived, pair])
+    arrived = yield [over(rows)], [rows]
+    rows = rows + arrived
+    arrived = yield [on_line(rows, CORE)], [rows]
+    rows = rows + arrived
+    arrived = yield [on_line(rows, ACROSS)], [rows]
+    rows = rows + arrived
+    return rows[: group.shape[0]], rows[group.shape[0] :]
+
+
+class Sums:
+    def __init__(self, order):
+        self.order, self.steps, self.pending, self.results = order, {}, {}, {}
+
+    def start(self, name, steps):
+        self.steps[name] = steps
+        self.pending[name], sent = next(steps)
+        self.order.done(*sent)
+
+    def wait(self, name):
+        arrived = self.order.enter(*self.pending[name])
+        try:
+            self.pending[name], sent = self.steps[name].send(arrived)
+            self.order.done(*sent)
+        except StopIteration as stop:
+            self.results[name] = stop.value
+
+
+def quick_local(
+    hidden_in, norm1_gain, norm1_bias, query_weight, query_bias, key_weight, value_weight, value_bias, out_weight,
+    out_bias, norm2_gain, norm2_bias, up_weight, up_bias, down_weight, down_bias, seg_lengths, parents, out_grad,
+):
+    size, model = hidden_in.shape
+    half, group, whole = 2 * size, 4 * size, 8 * size
+    columns = query_weight.shape[1]
+    width = columns // 2
+    heads = width // HD
+    units = up_weight.shape[1]
+    part = units // 2
+    seq, tensor = lax.axis_index("seq"), lax.axis_index("tensor")
+    block = size
+    f32, bf16 = jnp.float32, jnp.bfloat16
+    gain_one, gain_two = wide(norm1_gain), wide(norm2_gain)
+
+    def product(left, right):
+        return jnp.dot(left, right, preferred_element_type=f32).astype(bf16)
+
+    def product_nt(left, right):
+        return dot_nt(left, right).astype(bf16)
+
+    def product_tn(left, right):
+        return dot_tn(left, right).astype(bf16)
+
+    order = Order()
+    inputs = wide(hidden_in)
+    first, normed_one, inverse_one = norm_forward(inputs, gain_one, wide(norm1_bias))
+    first = low(first)
+    far, past = across(first), over(first)
+    order.done(first)
+    lengths, parent_ids = order.enter(seg_lengths, parents)
+    qkv_weight = jnp.concatenate([halves_of(w, 1, seq)[0] for w in (query_weight, key_weight, value_weight)], axis=1)
+    qkv_bias = jnp.concatenate(
+        [halves_of(query_bias, 0, seq)[0], jnp.zeros((width,), bf16), halves_of(value_bias, 0, seq)[0]]
+    )
+
+    def projected(rows):
+        return (jnp.dot(rows, qkv_weight, preferred_element_type=f32) + wide(qkv_bias)).astype(bf16)
+
+    blocks = jnp.arange(whole // block, dtype=jnp.int32)
+    place = blocks ^ (seq * 4 + tensor)
+    fq, fk, slope_rows, key_lists, query_lists = tree_features(
+        lengths[0], parent_ids[0], tensor * (columns // HD) + seq * heads, heads, block, whole
+    )
+    chunks_one = [jnp.concatenate([first, core(first)])]
+    qkv_parts = [projected(chunks_one[0])]
+    out_rel = jnp.concatenate(halves_of(out_weight, 0, seq))
+    order.done(qkv_parts[0], fk, fq, out_rel)
+    far, past = order.enter(far, past)
+    both = [over(low(far[: size // 2])), across(low(past[size // 2 :]))]
+    for piece in (far, past):
+        chunks_one.append(jnp.concatenate([piece, core(piece)]))
+        qkv_parts.append(projected(chunks_one[-1]))
+        order.done(qkv_parts[-1])
+    both = jnp.concatenate(order.enter(*both))
+    chunks_one.append(jnp.concatenate([both, core(both)]))
+    qkv_parts.append(projected(chunks_one[-1]))
+    qkv = jnp.concatenate(qkv_parts)
+
+    order.done(qkv)
+    grad_piece = order.enter(out_grad)
+    grad_back = across(grad_piece)
+    side = whole // block // 2
+
+    def attend(first_block, count):
+        place_now = order.enter(place)
+        mixed, logs = attention_forward(jnp.int32(first_block), count, place_now, key_lists, qkv, fq, fk, slope_rows, block)
+        order.done(mixed)
+        return mixed, logs
+
+    mixed_other, logs_other = attend(side, side)
+    far_part = attend(side // 2, side - side // 2)
+    mixed_past = over(mixed_other)
+    near_part = attend(0, side // 2)
+    mixed_own, logs_own = (jnp.concatenate(pair) for pair in zip(near_part, far_part))
+    mixed_past, grad_back = order.enter(mixed_past, grad_back)
+    heads_out = jnp.concatenate([mixed_own, mixed_past], axis=1)
+    branch_far = product(heads_out[half:], out_rel)
+    branch_sent = low(wide(branch_far[:size]) + wide(core(branch_far[size:])))
+    branch_back = across(branch_sent)
+    branch_near = product(heads_out[:half], out_rel)
+    grad_near = jnp.concatenate([grad_piece, core(grad_piece)])
+    grad_far = jnp.concatenate([grad_back, core(grad_back)])
+    order.done(branch_near, branch_sent)
+    grad_near = order.enter(grad_near)
+    act_grad_near = product_nt(grad_near, down_weight)
+    order.done(act_grad_near)
+    branch_back = order.enter(branch_back)
+    branch = wide(branch_near[:size]) + wide(core(branch_near[size:])) + wide(branch_back)
+    middle = inputs + branch + wide(out_bias)
+    second, normed_two, inverse_two = norm_forward(middle, gain_two, wide(norm2_bias))
+    second = low(second)
+    second_core, second_back = core(second), across(second)
+    order.done(second)
+    grad_far = order.enter(grad_far)
+    act_grad_far = product_nt(grad_far, down_weight)
+    order.done(act_grad_far)
+    second_core = order.enter(second_core)
+    act, up_grad, up_sums_near = feed_forward((second, second_core), up_weight, up_bias, act_grad_near, None, None, 0)
+    order.done(act, up_grad)
+    second_back = order.enter(second_back)
+    second_last = core(second_back)
+    act, up_grad, up_sums_far = feed_forward(
+        (second_back, second_last), up_weight, up_bias, act_grad_far, act, up_grad, 1
+    )
+    order.done(act, up_grad)
+    grad_near, grad_far = order.enter(grad_near, grad_far)
+    grad_rows = jnp.concatenate([grad_near, grad_far])
+    rows_two = jnp.concatenate([second, second_core, second_back, second_last])
+    rows_one = jnp.concatenate(chunks_one)
+    cotangent = wide(out_grad)
+
+    sums = Sums(order)
+    state = {}
+    order.done(act, up_grad)
+
+    down_parts, up_parts = 2, sum(name.startswith("U") for name in ORDER)
+    where = seq.reshape(1)
+    tile = 512
+
+    def start_down(index):
+        cols = model // down_parts
+        steps = part // tile
+        rows = order.enter(grad_rows)
+        halves = [
+            matmul(
+                "down_part", "tn", where, (steps,),
+                (act, (group, tile), lambda m, w, s=s: (0, (w[0] ^ s) * steps + m)),
+                (rows, (group, cols), lambda m, w: (0, index)),
+                [((part, cols), (tile, cols), lambda m, w: (m, 0))],
+            )[0]
+            for s in range(2)
+        ]
+        sums.start("d%d" % index, pair_steps(*halves))
+
+    def start_up(index):
+        rows = model // up_parts
+        (value,) = matmul(
+            "up_part", "tn", where, (units // 1024,),
+            (order.enter(rows_two), (group, rows), lambda n, w: (0, index)),
+            (up_grad, (group, 1024), lambda n, w: (0, n)),
+            [((rows, units), (rows, 1024), lambda n, w: (0, n))],
+        )
+        sums.start("u%d" % index, middle_steps(value))
+
+    def chunk_rows(name, kind, left, chunk, right, tile):
+        depth = left.shape[1]
+        cols = right.shape[0] if kind == "nt" else right.shape[1]
+        block, index = ((tile, depth), lambda n, w: (n, 0)) if kind == "nt" else ((depth, tile), lambda n, w: (0, n))
+        return matmul(
+            name, kind, where, (cols // tile,),
+            (left, (half, depth), lambda n, w: (chunk, 0)), (right, block, index),
+            [((size, cols), (size, tile), lambda n, w: (0, n))] * 2,
+        )
+
+    def second_far():
+        own, other = chunk_rows("second_gradient", "nt", order.enter(up_grad), 1, up_weight, 512)
+        state["second_far"] = own, core(other)
+        order.done(own)
+
+    def second_send():
+        own, other = state["second_far"]
+        sent = low(wide(own) + wide(order.enter(other)))
+        state["second_back"] = across(sent)
+        order.done(sent)
+
+    def second_near():
+        own, other = chunk_rows("second_gradient", "nt", order.enter(up_grad), 0, up_weight, 512)
+        state["second_own"] = wide(own) + wide(core(other))
+        order.done(own)
+
+    def second_norm():
+        incoming = state["second_own"] + wide(order.enter(state["second_back"]))
+        inner, gain_grad, bias_grad = norm_backward(incoming, normed_two, inverse_two, gain_two)
+        middle_grad = cotangent + inner
+        branch_grad = low(middle_grad)
+        state["middle_grad"], state["norm2"] = middle_grad, (gain_grad, bias_grad)
+        state["dy"] = [branch_grad, core(branch_grad)]
+        state["dy_back"] = across(branch_grad)
+        order.done(branch_grad)
+
+    def heads_rows(pieces):
+        rows = jnp.concatenate(pieces)
+        return matmul(
+            "heads_gradient", "nt", where, (1,),
+            (rows, rows.shape, lambda n, w: (0, 0)), (out_rel, out_rel.shape, lambda n, w: (0, 0)),
+            [((half, width), (half, width), lambda n, w: (0, 0))] * 2, 1,
+        )
+
+    def heads_near():
+        state["dy"] = [order.enter(state["dy"][0]), state["dy"][1]]
+        state["do_near"] = heads_rows(state["dy"])
+        order.done(state["do_near"][0])
+
+    def heads_far():
+        back = order.enter(state["dy_back"])
+        state["dy"] += [back, core(back)]
+        far = heads_rows(state["dy"][2:])
+        state["do_own"], sent = (low(jnp.concatenate(pair)) for pair in zip(state["do_near"], far))
+        state["do_past"] = over(sent)
+        order.done(state["do_own"], sent)
+
+    def attention():
+        rows = jnp.concatenate([state["do_own"], order.enter(state["do_past"])])
+        state["grads"] = attention_backward(
+            place, query_lists, qkv, rows, (mixed_own, mixed_other), fq, fk, slope_rows, (logs_own, logs_other), block
+        )
+        order.done(state["grads"])
+
+    def ffn_far():
+        own, other = chunk_rows("feed_back", "nn", order.enter(act), 1, down_weight, 512)
+        state["ffn_far"] = own, core(other)
+        order.done(own)
+
+    def ffn_send():
+        own, other = state["ffn_far"]
+        sent = low(wide(own) + wide(order.enter(other)))
+        state["ffn_back"] = across(sent)
+        order.done(sent)
+
+    def ffn_near():
+        own, other = chunk_rows("feed_back", "nn", order.enter(act), 0, down_weight, 512)
+        state["ffn_own"] = wide(own) + wide(core(other))
+        order.done(own)
+
+    def start_out():
+        rows = order.enter(jnp.concatenate(state["dy"]))
+        halves = [
+            matmul(
+                "out_part", "tn", where, (2,),
+                (v, (group, width), lambda n, w: (0, 0)), (rows, (group, model // 2), lambda n, w: (0, n)),
+                [((width, model), (width, model // 2), lambda n, w: (0, n))],
+            )[0]
+            for v in (mixed_own, mixed_past)
+        ]
+        sums.start("o", pair_steps(*halves))
+
+    def first_rows(chunk):
+        grads = state["grads"] = order.enter(state["grads"])
+        own, other = chunk_rows("first_gradient", "nt", grads, chunk, qkv_weight, 1024)
+        state["F%d" % chunk] = wide(own) + wide(core(other))
+        order.done(own)
+
+    def first_both():
+        both = low(state["F3"])
+        state["both"] = across(both)
+        order.done(both)
+
+    def first_far():
+        far = low(state["F1"])
+        state["far"] = across(far)
+        order.done(far)
+
+    def first_past():
+        past = low(state["F2"] + wide(order.enter(state["both"])))
+        state["past"] = over(past)
+        order.done(past)
+
+    def first_norm():
+        far, past = order.enter(state["far"], state["past"])
+        incoming = state["F0"] + wide(far) + wide(past)
+        inner, gain_grad, bias_grad = norm_backward(incoming, normed_one, inverse_one, gain_one)
+        state["grad_in"] = (state["middle_grad"] + inner).astype(bf16)
+        state["norm1"] = gain_grad, bias_grad
+        order.done(state["grad_in"])
+
+    def start_qkv(index):
+        grads = state["grads"] = order.enter(state["grads"])
+        size_of = 3 * width // projection_parts
+        (value,) = matmul(
+            "projection_part", "tn", where, (4,),
+            (rows_one, (whole, model // 4), lambda m, w: (0, m)), (grads, (whole, size_of), lambda m, w: (0, index)),
+            [((model, size_of), (model // 4, size_of), lambda m, w: (m, 0))],
+        )
+        sums.start("q%d" % index, line_steps(value))
+
+    projection_parts = sum(name.startswith("Q") for name in ORDER)
+    steps = {
+        "SF": second_far, "SFa": second_send,
+        "SN": second_near, "S": second_norm, "BN": heads_near, "BF": heads_far, "ATT": attention, "GF": ffn_far, "GFa": ffn_send,
+        "GN": ffn_near, "O": start_out, "F0": partial(first_rows, 0), "F1": partial(first_rows, 1),
+        "F2": partial(first_rows, 2), "F3": partial(first_rows, 3), "FB": first_both, "FE": first_far, "FL": first_past,
+        "FN": first_norm, }
+    for i in range(4):
+        steps["D%d" % i], steps["U%d" % i], steps["Q%d" % i] = partial(start_down, i), partial(start_up, i), partial(start_qkv, i)
+    def start_vectors():
+        bias_sum = jnp.sum(wide(state["grads"]), axis=0)
+        nothing = jnp.zeros((width,), f32)
+        pairs = jnp.concatenate(
+            [
+                in_order(bias_sum[:width], nothing, 0, seq),
+                in_order(bias_sum[2 * width :], nothing, 0, seq),
+                up_sums_near[0] + up_sums_far[0],
+            ]
+        )
+        grad_out_bias = jnp.sum(wide(state["dy"][0]), axis=0)
+        grad_down_bias = jnp.sum(cotangent, axis=0)
+        group_rows = jnp.stack([*state["norm1"], grad_out_bias, *state["norm2"], grad_down_bias])
+        sums.start("v", vector_steps(group_rows, jnp.pad(pairs, (0, -pairs.shape[0] % model)).reshape(-1, model)))
+
+    steps["V"] = start_vectors
+    for name in ORDER:
+        order.label = name
+        if name in steps:
+            steps[name]()
+        else:
+            sums.wait(name)
+
+    layer_out = (middle + state["ffn_own"] + wide(state["ffn_back"]) + wide(down_bias)).astype(bf16)
+    group_rows, pair_rows = sums.results["v"]
+    pair_rows = pair_rows.reshape(-1)
+
+    def put(out, value, row, column):
+        return lax.dynamic_update_slice(out, wide(value), (row, column))
+
+    up = blank((model, units))
+    upper = lax.axis_index("dp") // 2
+    cols = model // up_parts
+    for i in range(up_parts):
+        kept, other = sums.results["u%d" % i]
+        up = put(put(up, kept, i * cols + upper * (cols // 2), 0), other, i * cols + (1 - upper) * (cols // 2), 0)
+    down = blank((units, model))
+    cols = model // down_parts
+    for i in range(down_parts):
+        own, other = sums.results["d%d" % i]
+        down = put(put(down, own, seq * part, i * cols), other, (1 - seq) * part, i * cols)
+    out = blank((columns, model))
+    own, other = sums.results["o"]
+    out = put(put(out, own, seq * width, 0), other, (1 - seq) * width, 0)
+    own, other = (
+        jnp.concatenate([sums.results["q%d" % i][j] for i in range(projection_parts)], axis=1) for j in range(2)
+    )
+    projections = []
+    for i in range(3):
+        cols = slice(i * width, (i + 1) * width)
+        projection = put(blank((model, columns)), own[:, cols], 0, seq * width)
+        projections.append(put(projection, other[:, cols], 0, (1 - seq) * width))
+    return (
+        layer_out,
+        state["grad_in"],
+        group_rows[0],
+        group_rows[1],
+        projections[0],
+        pair_rows[:columns],
+        projections[1],
+        projections[2],
+        pair_rows[columns : 2 * columns],
+        out,
+        group_rows[2],
+        group_rows[3],
+        group_rows[4],
+        up,
+        pair_rows[2 * columns : 2 * columns + units],
+        down,
+        group_rows[5],
+    )
+
+
+def local(*args):
+    quick = lax.axis_size("tensor") == 4 and lax.axis_size("dp") == 4 and args[0].shape[0] == 256
+    return quick_local(*args) if quick else plain_local(*args)
 
 
 def solution(mesh):

time: 1080 us -> 846 us (0.78)
  matrix products: 167 us -> 31.6 us
  other arithmetic: 244 us -> 124 us
  Pallas kernels: 65.6 us -> 160 us
  waiting for transfers between devices: 343 us -> 260 us
  starting transfers between devices: 128 us -> 152 us
    dot_general x27 -> x6, matrix products: 113 us -> 17.9 us  [the longest x4 15.3 us: projected(): jnp.dot(rows, qkv_weight, preferred_element_type=f32) + wide(qkv_bias)]
    pallas_call x2 -> x34, Pallas kernels: 65.5 us -> 160 us  [the longest x22 80.6 us: matmul(): pl.pallas_call(kernel, grid_spec=pltpu.PrefetchScalarGridSpec(num_scalar_...]
    convert_element_type x36 -> x30, other arithmetic: 98.5 us -> 47.8 us  [low(): return lax.optimization_barrier(value.astype(jnp.bfloat16))]
    unnamed x325 -> x366, local copies, waits for them, and re-layouts: 48.5 us -> 93.5 us
    dot_general x10 -> x2, matrix products: 54 us -> 13.7 us  [dot_nt(): lax.dot_general(left, right, (((1,), (1,)), ((), ())), preferred_element_...]
    ppermute x38 -> x37, waiting for transfers between devices: 186 us -> 148 us  [on_line(): return lax.ppermute(value, 'dp', pairs)]
    ppermute x12 -> x11, waiting for transfers between devices: 73.6 us -> 45.8 us  [across(): return lax.ppermute(value, 'tensor', ACROSS)]
    select_n x14 -> x13, other arithmetic: 29.3 us -> 7.2 us  [the longest x5 3.98 us: line_steps(): total = low(jnp.where((line == 0) | (line == 3), arrived, total))]
  transfers between devices with their start and end apart: 94 -> 87, of which waited for: 30 -> 34; matrix products, arithmetic and copies ran while one was open for 39% -> 20% of each run, Pallas kernels for 4% -> 16%
where the time goes in v2:
time: 846 us; the launch traced here: 840 us
  waiting for transfers between devices  260 us (31%)
  Pallas kernels  160 us (19%)
  starting transfers between devices  152 us (18%)
  other arithmetic  124 us (15%)
  local copies, waits for them, and re-layouts  108 us (13%)
  matrix products  31.6 us (4%)
    ppermute x37, waiting for transfers between devices, on_line(): return lax.ppermute(value, 'dp', pairs)  148 us
    ppermute x37, starting transfers between devices, on_line(): return lax.ppermute(value, 'dp', pairs)  106 us
    unnamed x366, local copies, waits for them, and re-layouts  93.5 us
    pallas_call x22, Pallas kernels, matmul(): pl.pallas_call(kernel, grid_spec=pltpu.PrefetchScalarGridSpec(num_scalar_...  80.6 us
    ppermute x18, waiting for transfers between devices, over(): return lax.ppermute(value, 'seq', SWAP)  64.2 us
    pallas_call x4, Pallas kernels, _attention_call(): pl.pallas_call(kernel, out_shape=outs, in_specs=[pl.BlockSpec(memory_spac...  61.6 us
    convert_element_type x30, other arithmetic, low(): return lax.optimization_barrier(value.astype(jnp.bfloat16))  47.8 us
    ppermute x11, waiting for transfers between devices, across(): return lax.ppermute(value, 'tensor', ACROSS)  45.8 us
  transfers between devices with their start and end apart: 87, of which 34 were waited for; matrix products, arithmetic and copies ran while one was open for 20% of the time, Pallas kernels for 16%

profile of v2, /device:TPU:0, one launch (start us, length us, event | category | flops | bytes accessed | tf_op | source)
XLA Modules:
  0.0 840.1 jit_solution(14896720966498668442)
XLA Ops:
  26.4 7.5 collective-permute-done.refs_0_
  65.7 17.4 %attention_forward.3 = (bf16[1024,256]{1,0:T(8,128)(2,1)S(1)}, f32[1024,128]{1,0:T(8,128)S(1)}) custom-call(s32[1]{0:T(128)} %constant.144.clone.1.first_block, s32[8]{0:T(128)S(1)} %tie_front.18.place.refs_1_, s32[8,9]{1,0:T(8,128)S(1)} %pad_add_fusion.lists, bf16[2048,768]{1,0:T(8,128)(2,1)S(1)} %pad_maximum_fusion.3.refs_2_.qkv, ...), custom_call_target="tpu_custom_call" | custom-call | tf_op jit(solution)/shard_map/attention_forward/pallas_call | solution.py:286
  113.3 16.5 %collective-permute-done.12.refs_0_ = bf16[256,2048]{1,0:T(8,128)(2,1)S(1)} collective-permute-done((bf16[256,2048]{1,0:T(8,128)(2,1)S(1)}, bf16[256,2048]{1,0:T(8,128)(2,1)S(1)}, u32[]{:S(2)}, u32[]{:S(2)}) %collective-permute-start.12) | collective-permute-done | bytes 1048608 | tf_op jit(solution)/shard_map/ppermute | solution.py:358
  134.8 8.9 %convolution_convert_fusion.refs_2_.grads_ref = bf16[512,2048]{1,0:T(8,128)(2,1)S(1)} fusion(bf16[512,2048]{1,0:T(8,128)(2,1)S(1)} %tie_front.24.refs_1_, bf16[2048,2048]{1,0:T(8,128)(2,1)} %right_ref.7), kind=kOutput, calls=%fused_computation.26 | convolution fusion | flops 4296015872 | bytes 12582912 | tf_op jit(solution)/shard_map/dot_general | solution.py:22
  146.2 8.2 feed_forward.2
  175.1 9.7 %feed_forward.3 = (bf16[1024,2048]{1,0:T(8,128)(2,1)S(1)}, bf16[1024,2048]{1,0:T(8,128)(2,1)S(1)}, f32[8,2048]{1,0:T(8,128)S(1)}) custom-call(bf16[256,2048]{1,0:T(8,128)(2,1)S(1)} %tie_front.26.first.refs_2_, bf16[256,2048]{1,0:T(8,128)(2,1)} %collective-permute-done.17.second, ...), custom_call_target="tpu_custom_call", output_to_operand_aliasing={{0}: (5, {}), {1}: (6, {})} | custom-call | tf_op jit(solution)/shard_map/feed_forward/pallas_call | solution.py:515
  242.4 8.3 collective-permute-start.24
  270.4 10.7 %collective-permute-done.18.refs_0_ = bf16[512,2048]{1,0:T(8,128)(2,1)S(1)} collective-permute-done((bf16[512,2048]{1,0:T(8,128)(2,1)S(1)}, bf16[512,2048]{1,0:T(8,128)(2,1)S(1)}, u32[]{:S(2)}, u32[]{:S(2)}) %collective-permute-start.18) | collective-permute-done | bytes 2097184 | tf_op jit(solution)/shard_map/ppermute | solution.py:455
  282.1 9.2 %collective-permute-done.23.refs_0_ = bf16[256,2048]{1,0:T(8,128)(2,1)S(1)} collective-permute-done((bf16[256,2048]{1,0:T(8,128)(2,1)S(1)}, bf16[256,2048]{1,0:T(8,128)(2,1)S(1)}, u32[]{:S(2)}, u32[]{:S(2)}) %collective-permute-start.23) | collective-permute-done | bytes 1048608 | tf_op jit(solution)/shard_map/ppermute | solution.py:358
  307.5 7.4 collective-permute-start.30
  345.6 34.3 %attention_backward.1.refs_2_.refs_0_ = bf16[2048,768]{1,0:T(8,128)(2,1)S(1)} custom-call(s32[8]{0:T(128)S(1)} %copy-done.94, s32[8,9]{1,0:T(8,128)S(1)} %pad_add_fusion.1.lists, bf16[2048,768]{1,0:T(8,128)(2,1)S(1)} %copy-done.11, bf16[2048,256]{1,0:T(8,128)(2,1)S(1)} %pad_maximum_fusion.12.do, bf16[1024,256]{1,0:T(8,128)(2,1)S(1)} %copy-done.75, ...), custom_call_target="tpu_custom_call" | custom-call | tf_op jit(solution)/shard_map/attention_backward/pallas_call | solution.py:286
  393.5 17.0 %collective-permute-done.27.refs_0_ = bf16[1024,1024]{1,0:T(8,128)(2,1)} collective-permute-done((bf16[1024,1024]{1,0:T(8,128)(2,1)}, bf16[1024,1024]{1,0:T(8,128)(2,1)}, u32[]{:S(2)}, u32[]{:S(2)}) %collective-permute-start.27) | collective-permute-done | bytes 2097184 | tf_op jit(solution)/shard_map/ppermute | solution.py:362
  413.1 18.2 %collective-permute-start.33 = (bf16[1024,1024]{1,0:T(8,128)(2,1)S(1)}, bf16[1024,1024]{1,0:T(8,128)(2,1)}, u32[]{:S(2)}, u32[]{:S(2)}) collective-permute-start(bf16[1024,1024]{1,0:T(8,128)(2,1)S(1)} %add_convert_fusion.3.refs_3_), channel_id=1, source_target_pairs={{0,8},{24,16},{1,9},{25,17},{2,10},{26,18},{3,11},{27,19},{4,12},{... | collective-permute-start | bytes 6291464 | tf_op jit(solution)/shard_map/ppermute | solution.py:455
  455.1 12.8 %collective-permute-start.43 = (bf16[2048,384]{1,0:T(8,128)(2,1)}, bf16[2048,384]{1,0:T(8,128)(2,1)S(1)}, u32[]{:S(2)}, u32[]{:S(2)}) collective-permute-start(bf16[2048,384]{1,0:T(8,128)(2,1)} %projection_part.2.refs_2_), channel_id=1, source_target_pairs={{0,8},{24,16},{1,9},{25,17},{2,10},{26,18},{3,11},{27,19},{4,12},{... | collective-permute-start | bytes 4718600 | tf_op jit(solution)/shard_map/ppermute | solution.py:455
  516.2 23.6 %collective-permute-done.42.refs_0_ = bf16[1024,1024]{1,0:T(8,128)(2,1)S(1)} collective-permute-done((bf16[1024,1024]{1,0:T(8,128)(2,1)S(1)}, bf16[1024,1024]{1,0:T(8,128)(2,1)S(1)}, u32[]{:S(2)}, u32[]{:S(2)}) %collective-permute-start.42) | collective-permute-done | bytes 2097184 | tf_op jit(solution)/shard_map/ppermute | solution.py:455
  578.8 15.4 %collective-permute-start.60 = (bf16[2048,384]{1,0:T(8,128)(2,1)}, bf16[2048,384]{1,0:T(8,128)(2,1)S(1)}, u32[]{:S(2)}, u32[]{:S(2)}) collective-permute-start(bf16[2048,384]{1,0:T(8,128)(2,1)} %projection_part.3.refs_2_), channel_id=1, source_target_pairs={{0,8},{24,16},{1,9},{25,17},{2,10},{26,18},{3,11},{27,19},{4,12},{... | collective-permute-start | bytes 4718600 | tf_op jit(solution)/shard_map/ppermute | solution.py:455
  625.9 7.8 collective-permute-start.59
  640.9 8.9 %collective-permute-done.64.refs_0_ = bf16[2048,384]{1,0:T(8,128)(2,1)S(1)} collective-permute-done((bf16[2048,384]{1,0:T(8,128)(2,1)S(1)}, bf16[2048,384]{1,0:T(8,128)(2,1)S(1)}, u32[]{:S(2)}, u32[]{:S(2)}) %collective-permute-start.64) | collective-permute-done | bytes 1572896 | tf_op jit(solution)/shard_map/ppermute | solution.py:455
  650.7 19.3 %collective-permute-done.63.refs_0_ = bf16[256,2048]{1,0:T(8,128)(2,1)S(1)} collective-permute-done((bf16[256,2048]{1,0:T(8,128)(2,1)S(1)}, bf16[256,2048]{1,0:T(8,128)(2,1)S(1)}, u32[]{:S(2)}, u32[]{:S(2)}) %collective-permute-start.63) | collective-permute-done | bytes 1048608 | tf_op jit(solution)/shard_map/ppermute | solution.py:455
  695.1 17.0 %collective-permute-done.67.refs_0_ = bf16[2048,384]{1,0:T(8,128)(2,1)S(1)} collective-permute-done((bf16[2048,384]{1,0:T(8,128)(2,1)S(1)}, bf16[2048,384]{1,0:T(8,128)(2,1)S(1)}, u32[]{:S(2)}, u32[]{:S(2)}) %collective-permute-start.67) | collective-permute-done | bytes 1572896 | tf_op jit(solution)/shard_map/ppermute | solution.py:362
  718.9 18.6 %collective-permute-done.75.refs_0_ = bf16[2048,384]{1,0:T(8,128)(2,1)S(1)} collective-permute-done((bf16[2048,384]{1,0:T(8,128)(2,1)S(1)}, bf16[2048,384]{1,0:T(8,128)(2,1)S(1)}, u32[]{:S(2)}, u32[]{:S(2)}) %collective-permute-start.75) | collective-permute-done | bytes 1572896 | tf_op jit(solution)/shard_map/ppermute | solution.py:455
  741.9 12.6 %collective-permute-done.72.refs_0_ = bf16[256,2048]{1,0:T(8,128)(2,1)S(1)} collective-permute-done((bf16[256,2048]{1,0:T(8,128)(2,1)S(1)}, bf16[256,2048]{1,0:T(8,128)(2,1)S(1)}, u32[]{:S(2)}, u32[]{:S(2)}) %collective-permute-start.72) | collective-permute-done | bytes 1048608 | tf_op jit(solution)/shard_map/ppermute | solution.py:455
  772.9 19.2 %collective-permute-done.81.refs_1_ = bf16[256,2048]{1,0:T(8,128)(2,1)S(1)} collective-permute-done((bf16[256,2048]{1,0:T(8,128)(2,1)S(1)}, bf16[256,2048]{1,0:T(8,128)(2,1)S(1)}, u32[]{:S(2)}, u32[]{:S(2)}) %collective-permute-start.81) | collective-permute-done | bytes 1048608 | tf_op jit(solution)/shard_map/ppermute | solution.py:455
  805.0 15.9 %collective-permute-done.83.refs_0_ = f32[8,2048]{1,0:T(8,128)S(1)} collective-permute-done((f32[8,2048]{1,0:T(8,128)S(1)}, f32[8,2048]{1,0:T(8,128)S(1)}, u32[]{:S(2)}, u32[]{:S(2)}) %collective-permute-start.83) | collective-permute-done | bytes 65568 | tf_op jit(solution)/shard_map/ppermute | solution.py:455
  (841 shorter events, 491.2 us)
Async XLA Ops:
  232.8 48.2 %collective-permute-start.18 = (bf16[512,2048]{1,0:T(8,128)(2,1)S(1)}, bf16[512,2048]{1,0:T(8,128)(2,1)S(1)}, u32[]{:S(2)}, u32[]{:S(2)}) collective-permute-start(bf16[512,2048]{1,0:T(8,128)(2,1)S(1)} %copy-done.37), channel_id=1, source_target_pairs={{0,8},{24,16},{1,9},{25,17},{2,10},{26,18},{3,11},{27,19},{4,12},{... | collective-permute-start | bytes 6291464 | tf_op jit(solution)/shard_map/ppermute | solution.py:455
  242.4 54.6 %collective-permute-start.24 = (bf16[1024,1024]{1,0:T(8,128)(2,1)}, bf16[1024,1024]{1,0:T(8,128)(2,1)S(1)}, u32[]{:S(2)}, u32[]{:S(2)}) collective-permute-start(bf16[1024,1024]{1,0:T(8,128)(2,1)} %copy-done.64), channel_id=1, source_target_pairs={{0,4},{4,0},{1,5},{5,1},{2,6},{6,2},{3,7},{7,3},{8,12},{12,8},{9,1... | collective-permute-start | bytes 6291464 | tf_op jit(solution)/shard_map/ppermute | solution.py:362
  267.8 64.4 %collective-permute-start.28 = (bf16[512,2048]{1,0:T(8,128)(2,1)}, bf16[512,2048]{1,0:T(8,128)(2,1)}, u32[]{:S(2)}, u32[]{:S(2)}) collective-permute-start(bf16[512,2048]{1,0:T(8,128)(2,1)} %up_part.5.refs_2_), channel_id=1, source_target_pairs={{0,8},{24,16},{1,9},{25,17},{2,10},{26,18},{3,11},{27,19},{4,12},{... | collective-permute-start | bytes 6291464 | tf_op jit(solution)/shard_map/ppermute | solution.py:455
  307.5 76.2 %collective-permute-start.30 = (bf16[1024,1024]{1,0:T(8,128)(2,1)}, bf16[1024,1024]{1,0:T(8,128)(2,1)}, u32[]{:S(2)}, u32[]{:S(2)}) collective-permute-start(bf16[1024,1024]{1,0:T(8,128)(2,1)} %add_convert_fusion.5.refs_2_), channel_id=1, source_target_pairs={{0,8},{24,16},{1,9},{25,17},{2,10},{26,18},{3,11},{27,19},{4,12},{... | collective-permute-start | bytes 6291464 | tf_op jit(solution)/shard_map/ppermute | solution.py:455
  330.2 49.8 %collective-permute-start.31 = (bf16[256,2048]{1,0:T(8,128)(2,1)}, bf16[256,2048]{1,0:T(8,128)(2,1)S(1)}, u32[]{:S(2)}, u32[]{:S(2)}) collective-permute-start(bf16[256,2048]{1,0:T(8,128)(2,1)} %add_convert_fusion.25.refs_2_), channel_id=1, source_target_pairs={{0,4},{4,0},{1,5},{5,1},{2,6},{6,2},{3,7},{7,3},{8,12},{12,8},{9,1... | collective-permute-start | bytes 3145736 | tf_op jit(solution)/shard_map/ppermute | solution.py:362
  330.2 80.3 %collective-permute-start.27 = (bf16[1024,1024]{1,0:T(8,128)(2,1)}, bf16[1024,1024]{1,0:T(8,128)(2,1)}, u32[]{:S(2)}, u32[]{:S(2)}) collective-permute-start(bf16[1024,1024]{1,0:T(8,128)(2,1)} %down_part.7.refs_2_), channel_id=1, source_target_pairs={{0,4},{4,0},{1,5},{5,1},{2,6},{6,2},{3,7},{7,3},{8,12},{12,8},{9,1... | collective-permute-start | bytes 6291464 | tf_op jit(solution)/shard_map/ppermute | solution.py:362
  335.4 51.5 %collective-permute-start.29 = (bf16[256,2048]{1,0:T(8,128)(2,1)S(1)}, bf16[256,2048]{1,0:T(8,128)(2,1)S(1)}, u32[]{:S(2)}, u32[]{:S(2)}) collective-permute-start(bf16[256,2048]{1,0:T(8,128)(2,1)S(1)} %dynamic-slice_convert_fusion.2.refs_2_), channel_id=1, source_target_pairs={{8,16},{16,8},{9,17},{17,9},{10,18},{18,10},{11,19},{19,11},{12,20... | collective-permute-start | bytes 3145736 | tf_op jit(solution)/shard_map/ppermute | solution.py:455
  381.6 49.7 %collective-permute-start.34 = (bf16[256,2048]{1,0:T(8,128)(2,1)S(1)}, bf16[256,2048]{1,0:T(8,128)(2,1)S(1)}, u32[]{:S(2)}, u32[]{:S(2)}) collective-permute-start(bf16[256,2048]{1,0:T(8,128)(2,1)S(1)} %add_convert_fusion.24.refs_2_), channel_id=1, source_target_pairs={{8,16},{16,8},{9,17},{17,9},{10,18},{18,10},{11,19},{19,11},{12,20... | collective-permute-start | bytes 3145736 | tf_op jit(solution)/shard_map/ppermute | solution.py:455
  382.3 49.0 %collective-permute-start.35 = (bf16[256,2048]{1,0:T(8,128)(2,1)S(1)}, bf16[256,2048]{1,0:T(8,128)(2,1)S(1)}, u32[]{:S(2)}, u32[]{:S(2)}) collective-permute-start(bf16[256,2048]{1,0:T(8,128)(2,1)S(1)} %add_convert_fusion.24.refs_2_), channel_id=1, source_target_pairs={{8,0},{16,24},{9,1},{17,25},{10,2},{18,26},{11,3},{19,27},{12,4},{... | collective-permute-start | bytes 3145736 | tf_op jit(solution)/shard_map/ppermute | solution.py:455
  392.5 78.4 %collective-permute-start.39 = (bf16[1024,1024]{1,0:T(8,128)(2,1)S(1)}, bf16[1024,1024]{1,0:T(8,128)(2,1)S(1)}, u32[]{:S(2)}, u32[]{:S(2)}) collective-permute-start(bf16[1024,1024]{1,0:T(8,128)(2,1)S(1)} %add_convert_fusion.4.refs_2_), channel_id=1, source_target_pairs={{8,16},{16,8},{9,17},{17,9},{10,18},{18,10},{11,19},{19,11},{12,20... | collective-permute-start | bytes 6291464 | tf_op jit(solution)/shard_map/ppermute | solution.py:455
  413.1 63.5 %collective-permute-start.33 = (bf16[1024,1024]{1,0:T(8,128)(2,1)S(1)}, bf16[1024,1024]{1,0:T(8,128)(2,1)}, u32[]{:S(2)}, u32[]{:S(2)}) collective-permute-start(bf16[1024,1024]{1,0:T(8,128)(2,1)S(1)} %add_convert_fusion.3.refs_3_), channel_id=1, source_target_pairs={{0,8},{24,16},{1,9},{25,17},{2,10},{26,18},{3,11},{27,19},{4,12},{... | collective-permute-start | bytes 6291464 | tf_op jit(solution)/shard_map/ppermute | solution.py:455
  439.5 49.8 %collective-permute-start.45 = (bf16[256,2048]{1,0:T(8,128)(2,1)}, bf16[256,2048]{1,0:T(8,128)(2,1)S(1)}, u32[]{:S(2)}, u32[]{:S(2)}) collective-permute-start(bf16[256,2048]{1,0:T(8,128)(2,1)} %add_convert_fusion.22.refs_2_), channel_id=1, source_target_pairs={{8,16},{16,8},{9,17},{17,9},{10,18},{18,10},{11,19},{19,11},{12,20... | collective-permute-start | bytes 3145736 | tf_op jit(solution)/shard_map/ppermute | solution.py:455
  455.1 52.6 %collective-permute-start.43 = (bf16[2048,384]{1,0:T(8,128)(2,1)}, bf16[2048,384]{1,0:T(8,128)(2,1)S(1)}, u32[]{:S(2)}, u32[]{:S(2)}) collective-permute-start(bf16[2048,384]{1,0:T(8,128)(2,1)} %projection_part.2.refs_2_), channel_id=1, source_target_pairs={{0,8},{24,16},{1,9},{25,17},{2,10},{26,18},{3,11},{27,19},{4,12},{... | collective-permute-start | bytes 4718600 | tf_op jit(solution)/shard_map/ppermute | solution.py:455
  489.3 50.4 %collective-permute-start.42 = (bf16[1024,1024]{1,0:T(8,128)(2,1)S(1)}, bf16[1024,1024]{1,0:T(8,128)(2,1)S(1)}, u32[]{:S(2)}, u32[]{:S(2)}) collective-permute-start(bf16[1024,1024]{1,0:T(8,128)(2,1)S(1)} %add_convert_fusion.2.refs_2_), channel_id=1, source_target_pairs={{8,0},{16,24},{9,1},{17,25},{10,2},{18,26},{11,3},{19,27},{12,4},{... | collective-permute-start | bytes 6291464 | tf_op jit(solution)/shard_map/ppermute | solution.py:455
  492.2 50.5 %collective-permute-start.41 = (bf16[256,2048]{1,0:T(8,128)(2,1)S(1)}, bf16[256,2048]{1,0:T(8,128)(2,1)S(1)}, u32[]{:S(2)}, u32[]{:S(2)}) collective-permute-start(bf16[256,2048]{1,0:T(8,128)(2,1)S(1)} %out_part.2.refs_3_), channel_id=1, source_target_pairs={{0,4},{4,0},{1,5},{5,1},{2,6},{6,2},{3,7},{7,3},{8,12},{12,8},{9,1... | collective-permute-start | bytes 3145736 | tf_op jit(solution)/shard_map/ppermute | solution.py:362
  502.5 50.2 %collective-permute-start.51 = (bf16[512,2048]{1,0:T(8,128)(2,1)}, bf16[512,2048]{1,0:T(8,128)(2,1)S(1)}, u32[]{:S(2)}, u32[]{:S(2)}) collective-permute-start(bf16[512,2048]{1,0:T(8,128)(2,1)} %up_part.6.refs_2_), channel_id=1, source_target_pairs={{0,8},{24,16},{1,9},{25,17},{2,10},{26,18},{3,11},{27,19},{4,12},{... | collective-permute-start | bytes 6291464 | tf_op jit(solution)/shard_map/ppermute | solution.py:455
  507.7 53.2 %collective-permute-start.57 = (bf16[256,2048]{1,0:T(8,128)(2,1)S(1)}, bf16[256,2048]{1,0:T(8,128)(2,1)S(1)}, u32[]{:S(2)}, u32[]{:S(2)}) collective-permute-start(bf16[256,2048]{1,0:T(8,128)(2,1)S(1)} %get-tuple-element.103.refs_1_.refs_2_), channel_id=1, source_target_pairs={{8,0},{16,24},{9,1},{17,25},{10,2},{18,26},{11,3},{19,27},{12,4},{... | collective-permute-start | bytes 3145736 | tf_op jit(solution)/shard_map/ppermute | solution.py:455
  566.1 50.8 %collective-permute-start.49 = (bf16[1024,1024]{1,0:T(8,128)(2,1)}, bf16[1024,1024]{1,0:T(8,128)(2,1)}, u32[]{:S(2)}, u32[]{:S(2)}) collective-permute-start(bf16[1024,1024]{1,0:T(8,128)(2,1)} %add_convert_fusion.refs_2_), channel_id=1, source_target_pairs={{8,0},{16,24},{9,1},{17,25},{10,2},{18,26},{11,3},{19,27},{12,4},{... | collective-permute-start | bytes 6291464 | tf_op jit(solution)/shard_map/ppermute | solution.py:455
  596.4 53.4 %collective-permute-start.64 = (bf16[2048,384]{1,0:T(8,128)(2,1)S(1)}, bf16[2048,384]{1,0:T(8,128)(2,1)S(1)}, u32[]{:S(2)}, u32[]{:S(2)}) collective-permute-start(bf16[2048,384]{1,0:T(8,128)(2,1)S(1)} %add_convert_fusion.8.refs_2_), channel_id=1, source_target_pairs={{8,0},{16,24},{9,1},{17,25},{10,2},{18,26},{11,3},{19,27},{12,4},{... | collective-permute-start | bytes 4718600 | tf_op jit(solution)/shard_map/ppermute | solution.py:455
  619.7 72.9 %collective-permute-start.70 = (bf16[1024,1024]{1,0:T(8,128)(2,1)S(1)}, bf16[1024,1024]{1,0:T(8,128)(2,1)S(1)}, u32[]{:S(2)}, u32[]{:S(2)}) collective-permute-start(bf16[1024,1024]{1,0:T(8,128)(2,1)S(1)} %broadcast_select_fusion.refs_2_), channel_id=1, source_target_pairs={{0,4},{4,0},{1,5},{5,1},{2,6},{6,2},{3,7},{7,3},{8,12},{12,8},{9,1... | collective-permute-start | bytes 6291464 | tf_op jit(solution)/shard_map/ppermute | solution.py:362
  625.9 51.9 %collective-permute-start.59 = (bf16[512,2048]{1,0:T(8,128)(2,1)S(1)}, bf16[512,2048]{1,0:T(8,128)(2,1)S(1)}, u32[]{:S(2)}, u32[]{:S(2)}) collective-permute-start(bf16[512,2048]{1,0:T(8,128)(2,1)S(1)} %up_part.7.refs_2_), channel_id=1, source_target_pairs={{0,8},{24,16},{1,9},{25,17},{2,10},{26,18},{3,11},{27,19},{4,12},{... | collective-permute-start | bytes 6291464 | tf_op jit(solution)/shard_map/ppermute | solution.py:455
  737.5 64.4 %collective-permute-start.78 = (bf16[256,2048]{1,0:T(8,128)(2,1)S(1)}, bf16[256,2048]{1,0:T(8,128)(2,1)}, u32[]{:S(2)}, u32[]{:S(2)}) collective-permute-start(bf16[256,2048]{1,0:T(8,128)(2,1)S(1)} %add_convert_fusion.12.refs_2_), channel_id=1, source_target_pairs={{0,2},{2,0},{1,3},{3,1},{4,6},{6,4},{5,7},{7,5},{8,10},{10,8},{9,1... | collective-permute-start | bytes 3145736 | tf_op jit(solution)/shard_map/ppermute | solution.py:358
  739.9 87.4 %collective-permute-start.85 = (bf16[2048,384]{1,0:T(8,128)(2,1)S(1)}, bf16[2048,384]{1,0:T(8,128)(2,1)S(1)}, u32[]{:S(2)}, u32[]{:S(2)}) collective-permute-start(bf16[2048,384]{1,0:T(8,128)(2,1)S(1)} %broadcast_select_fusion.2.refs_2_), channel_id=1, source_target_pairs={{0,4},{4,0},{1,5},{5,1},{2,6},{6,2},{3,7},{7,3},{8,12},{12,8},{9,1... | collective-permute-start | bytes 4718600 | tf_op jit(solution)/shard_map/ppermute | solution.py:362
  740.6 51.7 %collective-permute-start.79 = (f32[6,2048]{1,0:T(8,128)S(1)}, f32[6,2048]{1,0:T(8,128)S(1)}, u32[]{:S(2)}, u32[]{:S(2)}) collective-permute-start(f32[6,2048]{1,0:T(8,128)S(1)} %add.491.refs_2_), channel_id=1, source_target_pairs={{0,2},{2,0},{1,3},{3,1},{4,6},{6,4},{5,7},{7,5},{8,10},{10,8},{9,1... | collective-permute-start | bytes 147464 | tf_op jit(solution)/shard_map/ppermute | solution.py:358
  (233 other events, 2981.9 us)

commit v3 on v2

--- a/solution.py
+++ b/solution.py
@@ -477,28 +477,59 @@
         input_output_aliases={i: i for i in range(count)},
         compiler_params=pltpu.CompilerParams(vmem_limit_bytes=1 << 16),
         cost_estimate=cost(0),
-        name="tie_" + name,
+        name="tie_%d" % name,
     )(*values, *after)
 
 
 class Order:
     def __init__(self):
-        self.after, self.label = [], "front"
+        self.after, self.label = [], 999
 
     def enter(self, *values):
         out = tie(list(values), self.after, self.label)
         self.after = [out[0]]
         return out if len(out) > 1 else out[0]
 
+    def here(self):
+        self.token = self.enter(self.token)
+        return self.token
+
     def done(self, *values):
         self.after.extend(values)
 
 
-def feed_forward(pieces, weight, bias, grads, act, up_grad, chunk, tile=512):
-    half, model, units = 2 * pieces[0].shape[0], weight.shape[0], weight.shape[1]
-
-    def kernel(first, second, weight_ref, bias_ref, grads_ref, *refs):
-        act_ref, up_ref, sums_ref = refs[-3:]
+def act_gradient(where, pieces, weight, tile=256):
+    size, model = pieces[0].shape
+    part = weight.shape[0] // 2
+    count = len(pieces)
+    steps = part // tile
+
+    def kernel(where_ref, *refs):
+        weight_ref, out, rows_out = refs[count:]
+        block = jnp.concatenate([ref[...] for ref in refs[:count]], axis=0)
+        out[...] = dot_nt(block, weight_ref[...]).astype(jnp.bfloat16)
+
+        @pl.when(pl.program_id(0) == 0)
+        def _():
+            rows_out[...] = block
+
+    return fused(
+        "act_gradient", kernel, where, (steps,),
+        [(p, p.shape, lambda n, w: (0, 0)) for p in pieces] + [(weight, (tile, model), lambda n, w: (w[0] * steps + n, 0))],
+        [
+            ((count * size, part), jnp.bfloat16, (count * size, tile), lambda n, w: (0, n)),
+            ((count * size, model), jnp.bfloat16, (count * size, model), lambda n, w: (0, 0)),
+        ],
+    )
+
+
+def feed_forward(where, pieces, weight, bias, grads, chunk, tile=512):
+    size, model = pieces[0].shape
+    part = weight.shape[1] // 2
+    steps = part // tile
+    half = 2 * size
+
+    def kernel(where_ref, first, second, weight_ref, bias_ref, grads_ref, act_ref, up_ref, rows_ref, sums_ref):
         rows = jnp.concatenate([first[...], second[...]], axis=0)
         pre = dot_nn(rows, weight_ref[...]) + wide(bias_ref[...])
         cdf = 0.5 * (1.0 + lax.erf(pre * (0.5**0.5)))
@@ -508,28 +539,25 @@
         up_ref[...] = low_grad
         sums_ref[...] = jnp.broadcast_to(jnp.sum(wide(low_grad), axis=0, keepdims=True), sums_ref.shape)
 
-    there = pl.BlockSpec(memory_space=pl.ANY)
-    whole = pl.BlockSpec(pieces[0].shape, lambda n: (0, 0))
-    filled = pl.BlockSpec((half, tile), lambda n: (chunk, n))
-    held = [] if act is None else [act, up_grad]
-    return pl.pallas_call(
-        kernel,
-        grid=(units // tile,),
-        out_shape=[jax.ShapeDtypeStruct((2 * half, units), jnp.bfloat16)] * 2 + [jax.ShapeDtypeStruct((8, units), jnp.float32)],
-        in_specs=[
-            whole,
-            whole,
-            pl.BlockSpec((model, tile), lambda n: (0, n)),
-            pl.BlockSpec((1, tile), lambda n: (0, n)),
-            pl.BlockSpec((half, tile), lambda n: (0, n)),
-            *[there] * len(held),
+        @pl.when(pl.program_id(0) == 0)
+        def _():
+            rows_ref[...] = rows
+
+    return fused(
+        "feed_forward", kernel, where, (steps,),
+        [(p, p.shape, lambda n, w: (0, 0)) for p in pieces]
+        + [
+            (weight, (model, tile), lambda n, w: (0, w[0] * steps + n)),
+            (bias.reshape(1, -1), (1, tile), lambda n, w: (0, w[0] * steps + n)),
+            (grads, (half, tile), lambda n, w: (chunk, n)),
         ],
-        out_specs=[filled, filled, pl.BlockSpec((8, tile), lambda n: (0, n))],
-        input_output_aliases={5: 0, 6: 1} if held else {},
-        compiler_params=pltpu.CompilerParams(vmem_limit_bytes=MATMUL_LIMIT),
-        cost_estimate=cost(0),
-        name="feed_forward",
-    )(*pieces, weight, bias.reshape(1, -1), grads, *held)
+        [
+            ((half, part), jnp.bfloat16, (half, tile), lambda n, w: (0, n)),
+            ((half, part), jnp.bfloat16, (half, tile), lambda n, w: (0, n)),
+            ((half, model), jnp.bfloat16, (half, model), lambda n, w: (0, 0)),
+            ((8, part), jnp.float32, (8, tile), lambda n, w: (0, n)),
+        ],
+    )
 
 
 def blank(shape):
@@ -546,29 +574,39 @@
 DOTS = {"nn": dot_nn, "nt": dot_nt, "tn": dot_tn}
 
 
-def matmul(name, kind, where, grid, left, right, outs, axis=0):
-    def kernel(where_ref, left_ref, right_ref, *out_refs):
-        total = DOTS[kind](left_ref[...], right_ref[...])
-        start = 0
-        for out in out_refs:
-            size = out.shape[axis]
-            piece = total[start : start + size] if axis == 0 else total[:, start : start + size]
-            out[...] = piece.astype(jnp.bfloat16)
-            start += size
-
+def fused(name, kernel, where, grid, operands, outs):
     return pl.pallas_call(
         kernel,
         grid_spec=pltpu.PrefetchScalarGridSpec(
             num_scalar_prefetch=1,
             grid=grid,
-            in_specs=[pl.BlockSpec(block, index) for _, block, index in (left, right)],
-            out_specs=[pl.BlockSpec(block, index) for _, block, index in outs],
+            in_specs=[pl.BlockSpec(block, index) for _, block, index in operands],
+            out_specs=[pl.BlockSpec(block, index) for _, _, block, index in outs],
         ),
-        out_shape=[jax.ShapeDtypeStruct(shape, jnp.bfloat16) for shape, _, _ in outs],
+        out_shape=[jax.ShapeDtypeStruct(shape, kind) for shape, kind, _, _ in outs],
         compiler_params=pltpu.CompilerParams(vmem_limit_bytes=MATMUL_LIMIT),
         cost_estimate=cost(0),
         name=name,
-    )(where, left[0], right[0])
+    )(where, *[array for array, _, _ in operands])
+
+
+def matmul(name, kind, where, grid, pairs, outs, axis=0):
+    count = len(pairs)
+
+    def kernel(where_ref, *refs):
+        total = None
+        for left, right in zip(refs[:count], refs[count : 2 * count]):
+            part = DOTS[kind](left[...], right[...])
+            total = part if total is None else total + part
+        start = 0
+        for out in refs[2 * count :]:
+            size = out.shape[axis]
+            piece = total[start : start + size] if axis == 0 else total[:, start : start + size]
+            out[...] = piece.astype(jnp.bfloat16)
+            start += size
+
+    operands = [left for left, _ in pairs] + [right for _, right in pairs]
+    return fused(name, kernel, where, grid, operands, [(shape, jnp.bfloat16, block, index) for shape, block, index in outs])
 
 
 def plain_local(
@@ -745,12 +783,18 @@
     )
 
 
-ORDER = " ".join((
-    "U0 SF SFa D0", "SN U2 S u0", "BN d0 BF u0", "D1 u2 ATT u0", "d0 u2 d1 u0", "F3 u2 Q0 u0",
-    "FB F1 d0 F2", "d1 U3 O u2", "FE FL q0 F0", "d0 o d1 u3", "u2 FN Q1 q0", "o u3 d0 d1",
-    "U1 q1 o u3", "q0 o q1 u1", "GF V d1 u3", "q0 u1 GFa q1", "v o u3 u1", "GN u1 v v",
-    "v v q1 u1",
-)).split()
+(
+    D0, D1, U0, U1, Q0, Q1, Q2, S0, S1, S2, S3, SB, SE, SL, G0, G1, G2, G3, GB, GE, GL, F0, F1, F2, F3, FB, FE, FL, S, G, BN, BF,
+    ATT, O, FN, V, d0, d1, u0, u1, q0, q1, q2, o, v,
+) = range(45)
+D_STEPS, U_STEPS, Q_STEPS = (D0, D1), (U0, U1), (Q0, Q1, Q2)
+S_STEPS, G_STEPS, F_STEPS = [S0, S1, S2, S3, SB, SE, SL], [G0, G1, G2, G3, GB, GE, GL], [F0, F1, F2, F3, FB, FE, FL]
+D_HOPS, U_HOPS, Q_HOPS, O_HOPS, V_HOPS = (d0, d1), (u0, u1), (q0, q1, q2), o, v
+ORDER = (
+    S3, U1, SB, S1, S2, SE, SL, D0, S0, u1, S, D1, BN, BF, d0, u1, O, ATT, d0, d1, o, F3, u1, FB, U0, F1, F2, o,
+    d0, d1, FE, FL, u1, u0, G3, F0, o, d0, d1, GB, FN, G1, G2, u0, Q0, GE, GL, G0, o, d1, Q1, q0, G, u0, Q2, V,
+    q0, q1, v, o, q2, q0, q1, v, u0, q2, q1, v, v, q0, q2, q1, v, q2,
+)
 
 
 def line_steps(mine):
@@ -768,24 +812,6 @@
 def pair_steps(own, other):
     arrived = yield [over(other)], [other, own]
     return (yield from line_steps(low(wide(own) + wide(arrived))))
-
-
-def middle_steps(value):
-    arrived = yield [on_line(value, INWARD)], [value]
-    inner = wide(value) + wide(arrived)
-    size = value.shape[0] // 2
-    line = lax.axis_index("dp")
-    upper, end = line // 2, (line == 0) | (line == 3)
-    keep = lax.dynamic_slice_in_dim(inner, upper * size, size, 0)
-    give = low(lax.dynamic_slice_in_dim(inner, (1 - upper) * size, size, 0))
-    arrived = yield [on_line(give, MIDDLE)], [give]
-    kept = low(keep + wide(arrived))
-    arrived = yield [over(kept)], [kept]
-    total = low(wide(kept) + wide(arrived))
-    arrived, outer = yield [on_line(total, MIDDLE), on_line(total, OUTWARD)], [total]
-    total = low(jnp.where(end, outer, total))
-    last = yield [on_line(arrived, OUTWARD)], [arrived, total]
-    return total, low(jnp.where(end, last, arrived))
 
 
 def vector_steps(group, pair):
@@ -842,8 +868,8 @@
     def product_nt(left, right):
         return dot_nt(left, right).astype(bf16)
 
-    def product_tn(left, right):
-        return dot_tn(left, right).astype(bf16)
+    def whole_block(value):
+        return (value, value.shape, lambda n, w: (0, 0))
 
     order = Order()
     inputs = wide(hidden_in)
@@ -882,118 +908,131 @@
 
     order.done(qkv)
     grad_piece = order.enter(out_grad)
-    grad_back = across(grad_piece)
+    grad_far, grad_past = across(grad_piece), over(grad_piece)
     side = whole // block // 2
 
-    def attend(first_block, count):
-        place_now = order.enter(place)
+    def attend(first_block, count, place_now):
         mixed, logs = attention_forward(jnp.int32(first_block), count, place_now, key_lists, qkv, fq, fk, slope_rows, block)
         order.done(mixed)
         return mixed, logs
 
-    mixed_other, logs_other = attend(side, side)
-    far_part = attend(side // 2, side - side // 2)
+    mixed_other, logs_other = attend(side, side, place)
+    far_part = attend(side // 2, side - side // 2, order.enter(place))
     mixed_past = over(mixed_other)
-    near_part = attend(0, side // 2)
+    place_now, grad_far, grad_past = order.enter(place, grad_far, grad_past)
+    grad_both = [over(low(grad_far[: size // 2])), across(low(grad_past[size // 2 :]))]
+    near_part = attend(0, side // 2, place_now)
     mixed_own, logs_own = (jnp.concatenate(pair) for pair in zip(near_part, far_part))
-    mixed_past, grad_back = order.enter(mixed_past, grad_back)
+    mixed_past, *grad_both = order.enter(mixed_past, *grad_both)
     heads_out = jnp.concatenate([mixed_own, mixed_past], axis=1)
     branch_far = product(heads_out[half:], out_rel)
     branch_sent = low(wide(branch_far[:size]) + wide(core(branch_far[size:])))
     branch_back = across(branch_sent)
     branch_near = product(heads_out[:half], out_rel)
-    grad_near = jnp.concatenate([grad_piece, core(grad_piece)])
-    grad_far = jnp.concatenate([grad_back, core(grad_back)])
     order.done(branch_near, branch_sent)
-    grad_near = order.enter(grad_near)
-    act_grad_near = product_nt(grad_near, down_weight)
-    order.done(act_grad_near)
+
+    where = seq.reshape(1)
+    grad_far = order.enter(grad_far)
+    pieces = [grad_piece, core(grad_piece), grad_far, core(grad_far)]
+    act_grad, grad_rows = ([v] for v in act_gradient(where, pieces, down_weight))
+    order.done(act_grad[0])
     branch_back = order.enter(branch_back)
     branch = wide(branch_near[:size]) + wide(core(branch_near[size:])) + wide(branch_back)
     middle = inputs + branch + wide(out_bias)
     second, normed_two, inverse_two = norm_forward(middle, gain_two, wide(norm2_bias))
     second = low(second)
-    second_core, second_back = core(second), across(second)
+    second_core, second_far, second_past = core(second), across(second), over(second)
     order.done(second)
-    grad_far = order.enter(grad_far)
-    act_grad_far = product_nt(grad_far, down_weight)
-    order.done(act_grad_far)
+    act, up_grad, rows_two, up_sums = [], [], [], []
+
+    def feed(pieces, chunk):
+        out = feed_forward(where, pieces, up_weight, up_bias, act_grad[chunk // 2], chunk % 2)
+        for held, value in zip((act, up_grad, rows_two, up_sums), out):
+            held.append(value)
+        order.done(out[0])
+
     second_core = order.enter(second_core)
-    act, up_grad, up_sums_near = feed_forward((second, second_core), up_weight, up_bias, act_grad_near, None, None, 0)
-    order.done(act, up_grad)
-    second_back = order.enter(second_back)
-    second_last = core(second_back)
-    act, up_grad, up_sums_far = feed_forward(
-        (second_back, second_last), up_weight, up_bias, act_grad_far, act, up_grad, 1
-    )
-    order.done(act, up_grad)
-    grad_near, grad_far = order.enter(grad_near, grad_far)
-    grad_rows = jnp.concatenate([grad_near, grad_far])
-    rows_two = jnp.concatenate([second, second_core, second_back, second_last])
-    rows_one = jnp.concatenate(chunks_one)
+    feed((second, second_core), 0)
+    grad_both = jnp.concatenate(grad_both)
+    pieces = [grad_past, core(grad_past), grad_both, core(grad_both)]
+    for held, value in zip((act_grad, grad_rows), act_gradient(where, pieces, down_weight)):
+        held.append(value)
+    order.done(act_grad[1])
+    second_far, second_past = order.enter(second_far, second_past)
+    second_both = [over(low(second_far[: size // 2])), across(low(second_past[size // 2 :]))]
+    feed((second_far, core(second_far)), 1)
+    feed((second_past, core(second_past)), 2)
+    second_both = jnp.concatenate(order.enter(*second_both))
+    feed((second_both, core(second_both)), 3)
     cotangent = wide(out_grad)
 
     sums = Sums(order)
+    order.token = where
     state = {}
-    order.done(act, up_grad)
-
-    down_parts, up_parts = 2, sum(name.startswith("U") for name in ORDER)
-    where = seq.reshape(1)
+    order.done(*act, *up_grad)
+
+    parts = 2
+    cols = model // parts
+
+    def start_down(index):
+        pairs = [
+            (
+                (act[c], (half, part // 2), lambda m, w: (0, m)),
+                (grad_rows[c // 2], (half, cols), lambda m, w, c=c: (c % 2, index)),
+            )
+            for c in range(4)
+        ]
+        out = ((part, cols), (part // 2, cols), lambda m, w: (m, 0))
+        sums.start(D_HOPS[index], line_steps(*matmul("down_part", "tn", order.here(), (2,), pairs, [out])))
+
+    def start_up(index):
+        pairs = [
+            (
+                (rows_two[c], (half, cols // 2), lambda m, w: (0, 2 * index + m)),
+                (up_grad[c], (half, part), lambda m, w: (0, 0)),
+            )
+            for c in range(4)
+        ]
+        out = ((cols, part), (cols // 2, part), lambda m, w: (m, 0))
+        sums.start(U_HOPS[index], line_steps(*matmul("up_part", "tn", order.here(), (2,), pairs, [out])))
+
+    def scatter_steps(name, kind, source, right, tile):
+        def rows(chunk):
+            own, other = matmul(
+                name, kind, order.here(), (model // tile,), [(source(chunk), right)],
+                [((size, model), (size, tile), lambda n, w: (0, n))] * 2,
+            )
+            state[name, chunk] = own, core(other)
+            order.done(own)
+
+        def total(chunk):
+            own, other = state[name, chunk]
+            return wide(own) + wide(other)
+
+        def send(key, transfer, value):
+            sent = low(value)
+            state[name, key] = transfer(sent)
+            order.done(sent)
+
+        def both():
+            send("both", across, total(3))
+
+        def far():
+            send("far", across, total(1))
+
+        def past():
+            send("past", over, total(2) + wide(order.enter(state[name, "both"])))
+
+        def own_rows():
+            far, past = order.enter(state[name, "far"], state[name, "past"])
+            return total(0) + wide(far) + wide(past)
+
+        return [partial(rows, i) for i in range(4)] + [both, far, past], own_rows
+
     tile = 512
 
-    def start_down(index):
-        cols = model // down_parts
-        steps = part // tile
-        rows = order.enter(grad_rows)
-        halves = [
-            matmul(
-                "down_part", "tn", where, (steps,),
-                (act, (group, tile), lambda m, w, s=s: (0, (w[0] ^ s) * steps + m)),
-                (rows, (group, cols), lambda m, w: (0, index)),
-                [((part, cols), (tile, cols), lambda m, w: (m, 0))],
-            )[0]
-            for s in range(2)
-        ]
-        sums.start("d%d" % index, pair_steps(*halves))
-
-    def start_up(index):
-        rows = model // up_parts
-        (value,) = matmul(
-            "up_part", "tn", where, (units // 1024,),
-            (order.enter(rows_two), (group, rows), lambda n, w: (0, index)),
-            (up_grad, (group, 1024), lambda n, w: (0, n)),
-            [((rows, units), (rows, 1024), lambda n, w: (0, n))],
-        )
-        sums.start("u%d" % index, middle_steps(value))
-
-    def chunk_rows(name, kind, left, chunk, right, tile):
-        depth = left.shape[1]
-        cols = right.shape[0] if kind == "nt" else right.shape[1]
-        block, index = ((tile, depth), lambda n, w: (n, 0)) if kind == "nt" else ((depth, tile), lambda n, w: (0, n))
-        return matmul(
-            name, kind, where, (cols // tile,),
-            (left, (half, depth), lambda n, w: (chunk, 0)), (right, block, index),
-            [((size, cols), (size, tile), lambda n, w: (0, n))] * 2,
-        )
-
-    def second_far():
-        own, other = chunk_rows("second_gradient", "nt", order.enter(up_grad), 1, up_weight, 512)
-        state["second_far"] = own, core(other)
-        order.done(own)
-
-    def second_send():
-        own, other = state["second_far"]
-        sent = low(wide(own) + wide(order.enter(other)))
-        state["second_back"] = across(sent)
-        order.done(sent)
-
-    def second_near():
-        own, other = chunk_rows("second_gradient", "nt", order.enter(up_grad), 0, up_weight, 512)
-        state["second_own"] = wide(own) + wide(core(other))
-        order.done(own)
-
     def second_norm():
-        incoming = state["second_own"] + wide(order.enter(state["second_back"]))
+        incoming = second_rows()
         inner, gain_grad, bias_grad = norm_backward(incoming, normed_two, inverse_two, gain_two)
         middle_grad = cotangent + inner
         branch_grad = low(middle_grad)
@@ -1005,13 +1044,12 @@
     def heads_rows(pieces):
         rows = jnp.concatenate(pieces)
         return matmul(
-            "heads_gradient", "nt", where, (1,),
-            (rows, rows.shape, lambda n, w: (0, 0)), (out_rel, out_rel.shape, lambda n, w: (0, 0)),
+            "heads_gradient", "nt", order.here(), (1,),
+            [(whole_block(rows), whole_block(out_rel))],
             [((half, width), (half, width), lambda n, w: (0, 0))] * 2, 1,
         )
 
     def heads_near():
-        state["dy"] = [order.enter(state["dy"][0]), state["dy"][1]]
         state["do_near"] = heads_rows(state["dy"])
         order.done(state["do_near"][0])
 
@@ -1024,88 +1062,59 @@
         order.done(state["do_own"], sent)
 
     def attention():
+        rows_one = jnp.concatenate(order.enter(*chunks_one))
+        state["rows_one"] = rows_one
+        order.done(rows_one)
         rows = jnp.concatenate([state["do_own"], order.enter(state["do_past"])])
         state["grads"] = attention_backward(
             place, query_lists, qkv, rows, (mixed_own, mixed_other), fq, fk, slope_rows, (logs_own, logs_other), block
         )
         order.done(state["grads"])
 
-    def ffn_far():
-        own, other = chunk_rows("feed_back", "nn", order.enter(act), 1, down_weight, 512)
-        state["ffn_far"] = own, core(other)
-        order.done(own)
-
-    def ffn_send():
-        own, other = state["ffn_far"]
-        sent = low(wide(own) + wide(order.enter(other)))
-        state["ffn_back"] = across(sent)
-        order.done(sent)
-
-    def ffn_near():
-        own, other = chunk_rows("feed_back", "nn", order.enter(act), 0, down_weight, 512)
-        state["ffn_own"] = wide(own) + wide(core(other))
-        order.done(own)
+    def layer_end():
+        state["layer_out"] = (middle + ffn_rows() + wide(down_bias)).astype(bf16)
+        order.done(state["layer_out"])
 
     def start_out():
-        rows = order.enter(jnp.concatenate(state["dy"]))
+        rows = jnp.concatenate(state["dy"])
+        here = order.here()
         halves = [
             matmul(
-                "out_part", "tn", where, (2,),
-                (v, (group, width), lambda n, w: (0, 0)), (rows, (group, model // 2), lambda n, w: (0, n)),
+                "out_part", "tn", here, (2,),
+                [(whole_block(v), (rows, (group, model // 2), lambda n, w: (0, n)))],
                 [((width, model), (width, model // 2), lambda n, w: (0, n))],
             )[0]
             for v in (mixed_own, mixed_past)
         ]
-        sums.start("o", pair_steps(*halves))
-
-    def first_rows(chunk):
-        grads = state["grads"] = order.enter(state["grads"])
-        own, other = chunk_rows("first_gradient", "nt", grads, chunk, qkv_weight, 1024)
-        state["F%d" % chunk] = wide(own) + wide(core(other))
-        order.done(own)
-
-    def first_both():
-        both = low(state["F3"])
-        state["both"] = across(both)
-        order.done(both)
-
-    def first_far():
-        far = low(state["F1"])
-        state["far"] = across(far)
-        order.done(far)
-
-    def first_past():
-        past = low(state["F2"] + wide(order.enter(state["both"])))
-        state["past"] = over(past)
-        order.done(past)
+        sums.start(O_HOPS, pair_steps(*halves))
 
     def first_norm():
-        far, past = order.enter(state["far"], state["past"])
-        incoming = state["F0"] + wide(far) + wide(past)
+        incoming = first_rows()
         inner, gain_grad, bias_grad = norm_backward(incoming, normed_one, inverse_one, gain_one)
         state["grad_in"] = (state["middle_grad"] + inner).astype(bf16)
         state["norm1"] = gain_grad, bias_grad
         order.done(state["grad_in"])
 
     def start_qkv(index):
-        grads = state["grads"] = order.enter(state["grads"])
+        grads = state["grads"]
         size_of = 3 * width // projection_parts
         (value,) = matmul(
-            "projection_part", "tn", where, (4,),
-            (rows_one, (whole, model // 4), lambda m, w: (0, m)), (grads, (whole, size_of), lambda m, w: (0, index)),
+            "projection_part", "tn", order.here(), (4,),
+            [((state["rows_one"], (whole, model // 4), lambda m, w: (0, m)), (grads, (whole, size_of), lambda m, w: (0, index)))],
             [((model, size_of), (model // 4, size_of), lambda m, w: (m, 0))],
         )
-        sums.start("q%d" % index, line_steps(value))
-
-    projection_parts = sum(name.startswith("Q") for name in ORDER)
-    steps = {
-        "SF": second_far, "SFa": second_send,
-        "SN": second_near, "S": second_norm, "BN": heads_near, "BF": heads_far, "ATT": attention, "GF": ffn_far, "GFa": ffn_send,
-        "GN": ffn_near, "O": start_out, "F0": partial(first_rows, 0), "F1": partial(first_rows, 1),
-        "F2": partial(first_rows, 2), "F3": partial(first_rows, 3), "FB": first_both, "FE": first_far, "FL": first_past,
-        "FN": first_norm, }
-    for i in range(4):
-        steps["D%d" % i], steps["U%d" % i], steps["Q%d" % i] = partial(start_down, i), partial(start_up, i), partial(start_qkv, i)
+        sums.start(Q_HOPS[index], line_steps(value))
+
+    projection_parts = sum(step in ORDER for step in Q_STEPS)
+    second_steps, second_rows = scatter_steps(
+        "second_gradient", "nt", lambda c: whole_block(up_grad[c]), (up_weight, (tile, part), lambda n, w: (n, w[0])), tile
+    )
+    ffn_steps, ffn_rows = scatter_steps(
+        "feed_back", "nn", lambda c: whole_block(act[c]), (down_weight, (part, tile), lambda n, w: (w[0], n)), tile
+    )
+    first_steps, first_rows = scatter_steps(
+        "first_gradient", "nt", lambda c: (state["grads"], (half, 3 * width), lambda n, w: (c, 0)), (qkv_weight, (2 * tile, 3 * width), lambda n, w: (n, 0)), 2 * tile
+    )
     def start_vectors():
         bias_sum = jnp.sum(wide(state["grads"]), axis=0)
         nothing = jnp.zeros((width,), f32)
@@ -1113,45 +1122,44 @@
             [
                 in_order(bias_sum[:width], nothing, 0, seq),
                 in_order(bias_sum[2 * width :], nothing, 0, seq),
-                up_sums_near[0] + up_sums_far[0],
+                in_order(sum(s[0] for s in up_sums), jnp.zeros((part,), f32), 0, seq),
             ]
         )
         grad_out_bias = jnp.sum(wide(state["dy"][0]), axis=0)
         grad_down_bias = jnp.sum(cotangent, axis=0)
         group_rows = jnp.stack([*state["norm1"], grad_out_bias, *state["norm2"], grad_down_bias])
-        sums.start("v", vector_steps(group_rows, jnp.pad(pairs, (0, -pairs.shape[0] % model)).reshape(-1, model)))
-
-    steps["V"] = start_vectors
-    for name in ORDER:
-        order.label = name
-        if name in steps:
-            steps[name]()
+        sums.start(V_HOPS, vector_steps(group_rows, jnp.pad(pairs, (0, -pairs.shape[0] % model)).reshape(-1, model)))
+
+    steps = dict(zip(S_STEPS + G_STEPS + F_STEPS, second_steps + ffn_steps + first_steps))
+    steps |= {S: second_norm, G: layer_end, BN: heads_near, BF: heads_far, ATT: attention, O: start_out, FN: first_norm, V: start_vectors}
+    for i in range(3):
+        steps[Q_STEPS[i]] = partial(start_qkv, i)
+    for i in range(parts):
+        steps[D_STEPS[i]], steps[U_STEPS[i]] = partial(start_down, i), partial(start_up, i)
+    for step in ORDER:
+        order.label = step
+        if step in steps:
+            steps[step]()
         else:
-            sums.wait(name)
-
-    layer_out = (middle + state["ffn_own"] + wide(state["ffn_back"]) + wide(down_bias)).astype(bf16)
-    group_rows, pair_rows = sums.results["v"]
+            sums.wait(step)
+
+    group_rows, pair_rows = sums.results[V_HOPS]
     pair_rows = pair_rows.reshape(-1)
 
     def put(out, value, row, column):
         return lax.dynamic_update_slice(out, wide(value), (row, column))
 
-    up = blank((model, units))
-    upper = lax.axis_index("dp") // 2
-    cols = model // up_parts
-    for i in range(up_parts):
-        kept, other = sums.results["u%d" % i]
-        up = put(put(up, kept, i * cols + upper * (cols // 2), 0), other, i * cols + (1 - upper) * (cols // 2), 0)
-    down = blank((units, model))
-    cols = model // down_parts
-    for i in range(down_parts):
-        own, other = sums.results["d%d" % i]
+    up, down = blank((model, units)), blank((units, model))
+    for i in range(parts):
+        own, other = sums.results[U_HOPS[i]]
+        up = put(put(up, own, i * cols, seq * part), other, i * cols, (1 - seq) * part)
+        own, other = sums.results[D_HOPS[i]]
         down = put(put(down, own, seq * part, i * cols), other, (1 - seq) * part, i * cols)
     out = blank((columns, model))
-    own, other = sums.results["o"]
+    own, other = sums.results[O_HOPS]
     out = put(put(out, own, seq * width, 0), other, (1 - seq) * width, 0)
     own, other = (
-        jnp.concatenate([sums.results["q%d" % i][j] for i in range(projection_parts)], axis=1) for j in range(2)
+        jnp.concatenate([sums.results[Q_HOPS[i]][j] for i in range(projection_parts)], axis=1) for j in range(2)
     )
     projections = []
     for i in range(3):
@@ -1159,7 +1167,7 @@
         projection = put(blank((model, columns)), own[:, cols], 0, seq * width)
         projections.append(put(projection, other[:, cols], 0, (1 - seq) * width))
     return (
-        layer_out,
+        state["layer_out"],
         state["grad_in"],
         group_rows[0],
         group_rows[1],

time: 846 us -> 798 us (0.943)
  Pallas kernels: 160 us -> 224 us
  starting transfers between devices: 152 us -> 101 us
  local copies, waits for them, and re-layouts: 108 us -> 78 us
  other arithmetic: 124 us -> 102 us
  matrix products: 31.6 us -> 12.3 us
    ppermute x37 -> x26, waiting for transfers between devices: 148 us -> 82.6 us  [on_line(): return lax.ppermute(value, 'dp', pairs)]
    ppermute x37 -> x26, starting transfers between devices: 106 us -> 55 us  [on_line(): return lax.ppermute(value, 'dp', pairs)]
    ppermute x18 -> x21, waiting for transfers between devices: 64.2 us -> 110 us  [over(): return lax.ppermute(value, 'seq', SWAP)]
    pallas_call x87 -> x81, Pallas kernels: 0.1 us -> 36.6 us  [tie(): pl.pallas_call(lambda *refs: None, out_shape=[jax.ShapeDtypeStruct(v.shap...]
    unnamed x366 -> x385, local copies, waits for them, and re-layouts: 93.5 us -> 60.5 us
    pallas_call x24 -> x29, Pallas kernels: 98.5 us -> 127 us  [fused(): pl.pallas_call(kernel, grid_spec=pltpu.PrefetchScalarGridSpec(num_scalar_...]
    ppermute x11 -> x15, waiting for transfers between devices: 45.8 us -> 65.4 us  [across(): return lax.ppermute(value, 'tensor', ACROSS)]
    dot_general x2 -> x0, matrix products: 13.7 us -> none  [dot_nt(): lax.dot_general(left, right, (((1,), (1,)), ((), ())), preferred_element_...]
  transfers between devices with their start and end apart: 87 -> 91, of which waited for: 34 -> 36; matrix products, arithmetic and copies ran while one was open for 20% -> 15% of each run, Pallas kernels for 16% -> 26%
where the time goes in v3:
time: 798 us; the launch traced here: 791 us
  waiting for transfers between devices  263 us (33%)
  Pallas kernels  224 us (28%)
  other arithmetic  102 us (13%)
  starting transfers between devices  101 us (13%)
  local copies, waits for them, and re-layouts  78 us (10%)
  matrix products  12.3 us (2%)
  between operations  10.8 us (1%)
    pallas_call x29, Pallas kernels, fused(): pl.pallas_call(kernel, grid_spec=pltpu.PrefetchScalarGridSpec(num_scalar_...  127 us
    ppermute x21, waiting for transfers between devices, over(): return lax.ppermute(value, 'seq', SWAP)  110 us
    ppermute x26, waiting for transfers between devices, on_line(): return lax.ppermute(value, 'dp', pairs)  82.6 us
    ppermute x15, waiting for transfers between devices, across(): return lax.ppermute(value, 'tensor', ACROSS)  65.4 us
    pallas_call x4, Pallas kernels, _attention_call(): pl.pallas_call(kernel, out_shape=outs, in_specs=[pl.BlockSpec(memory_spac...  60.5 us
    unnamed x385, local copies, waits for them, and re-layouts  60.5 us
    ppermute x26, starting transfers between devices, on_line(): return lax.ppermute(value, 'dp', pairs)  55 us
    convert_element_type x30, other arithmetic, low(): return lax.optimization_barrier(value.astype(jnp.bfloat16))  40.7 us
  transfers between devices with their start and end apart: 91, of which 36 were waited for; matrix products, arithmetic and copies ran while one was open for 15% of the time, Pallas kernels for 26%

profile of v3, /device:TPU:0, one launch (start us, length us, event | category | flops | bytes accessed | tf_op | source)
XLA Modules:
  0.0 790.9 jit_solution(16699954411723462801)
XLA Ops:
  26.5 7.5 collective-permute-done.refs_0_
  67.6 16.8 %attention_forward.3 = (bf16[1024,256]{1,0:T(8,128)(2,1)S(1)}, f32[1024,128]{1,0:T(8,128)S(1)}) custom-call(s32[1]{0:T(128)} %constant.120.clone.1.first_block, s32[8]{0:T(128)S(1)} %iota_xor_fusion.place, s32[8,9]{1,0:T(8,128)S(1)} %pad_add_fusion.lists, bf16[2048,768]{1,0:T(8,128)(2,1)S(1)} %pad_maximum_fusion.2.refs_2_.qkv, ...), custom_call_target="tpu_custom_call" | custom-call | tf_op jit(solution)/shard_map/attention_forward/pallas_call | solution.py:286
  104.0 8.1 %collective-permute-done.11.refs_1_ = bf16[128,2048]{1,0:T(8,128)(2,1)S(1)} collective-permute-done((bf16[128,2048]{1,0:T(8,128)(2,1)S(1)}, bf16[128,2048]{1,0:T(8,128)(2,1)S(1)}, u32[]{:S(2)}, u32[]{:S(2)}) %collective-permute-start.11) | collective-permute-done | bytes 524320 | tf_op jit(solution)/shard_map/ppermute | solution.py:362
  120.4 7.3 act_gradient.2
  127.8 15.4 %collective-permute-done.15.refs_0_ = bf16[256,2048]{1,0:T(8,128)(2,1)S(1)} collective-permute-done((bf16[256,2048]{1,0:T(8,128)(2,1)S(1)}, bf16[256,2048]{1,0:T(8,128)(2,1)S(1)}, u32[]{:S(2)}, u32[]{:S(2)}) %collective-permute-start.15) | collective-permute-done | bytes 1048608 | tf_op jit(solution)/shard_map/ppermute | solution.py:358
  165.1 7.8 collective-permute-done.18.refs_0_
  238.4 13.8 %collective-permute-done.29.refs_0_ = bf16[256,2048]{1,0:T(8,128)(2,1)S(1)} collective-permute-done((bf16[256,2048]{1,0:T(8,128)(2,1)S(1)}, bf16[256,2048]{1,0:T(8,128)(2,1)S(1)}, u32[]{:S(2)}, u32[]{:S(2)}) %collective-permute-start.29) | collective-permute-done | bytes 1048608 | tf_op jit(solution)/shard_map/ppermute | solution.py:358
  258.4 7.2 down_part.2.refs_2_
  270.9 12.4 %collective-permute-done.34.refs_0_ = bf16[1024,1024]{1,0:T(8,128)(2,1)S(1)} collective-permute-done((bf16[1024,1024]{1,0:T(8,128)(2,1)S(1)}, bf16[1024,1024]{1,0:T(8,128)(2,1)S(1)}, u32[]{:S(2)}, u32[]{:S(2)}) %collective-permute-start.34) | collective-permute-done | bytes 2097184 | tf_op jit(solution)/shard_map/ppermute | solution.py:455
  340.6 8.4 %collective-permute-done.39.refs_0_ = bf16[1024,1024]{1,0:T(8,128)(2,1)} collective-permute-done((bf16[1024,1024]{1,0:T(8,128)(2,1)}, bf16[1024,1024]{1,0:T(8,128)(2,1)}, u32[]{:S(2)}, u32[]{:S(2)}) %collective-permute-start.39) | collective-permute-done | bytes 2097184 | tf_op jit(solution)/shard_map/ppermute | solution.py:455
  371.1 9.8 %collective-permute-done.44.refs_0_ = bf16[1024,256]{1,0:T(8,128)(2,1)S(1)} collective-permute-done((bf16[1024,256]{1,0:T(8,128)(2,1)S(1)}, bf16[1024,256]{1,0:T(8,128)(2,1)S(1)}, u32[]{:S(2)}, u32[]{:S(2)}) %collective-permute-start.44) | collective-permute-done | bytes 524320 | tf_op jit(solution)/shard_map/ppermute | solution.py:362
  383.5 33.6 %attention_backward.1.refs_2_.refs_0_.refs_1_ = bf16[2048,768]{1,0:T(8,128)(2,1)S(1)} custom-call(s32[8]{0:T(128)S(1)} %iota_xor_fusion.place, s32[8,9]{1,0:T(8,128)S(1)} %pad_add_fusion.1.lists, bf16[2048,768]{1,0:T(8,128)(2,1)S(1)} %copy-done.5, bf16[2048,256]{1,0:T(8,128)(2,1)S(1)} %pad_maximum_fusion.8.do, bf16[1024,256]{1,0:T(8,128)(2,1)S(1)} %copy-done.99, ...), custom_call_target="tpu_custom_call" | custom-call | tf_op jit(solution)/shard_map/attention_backward/pallas_call | solution.py:286
  431.6 8.3 %collective-permute-start.52 = (bf16[256,2048]{1,0:T(8,128)(2,1)}, bf16[256,2048]{1,0:T(8,128)(2,1)}, u32[]{:S(2)}, u32[]{:S(2)}) collective-permute-start(bf16[256,2048]{1,0:T(8,128)(2,1)} %add_convert_fusion.23.refs_2_), channel_id=1, source_target_pairs={{0,8},{24,16},{1,9},{25,17},{2,10},{26,18},{3,11},{27,19},{4,12},{... | collective-permute-start | bytes 3145736 | tf_op jit(solution)/shard_map/ppermute | solution.py:455
  479.0 14.0 %collective-permute-done.49.refs_0_ = bf16[256,2048]{1,0:T(8,128)(2,1)S(1)} collective-permute-done((bf16[256,2048]{1,0:T(8,128)(2,1)S(1)}, bf16[256,2048]{1,0:T(8,128)(2,1)S(1)}, u32[]{:S(2)}, u32[]{:S(2)}) %collective-permute-start.49) | collective-permute-done | bytes 1048608 | tf_op jit(solution)/shard_map/ppermute | solution.py:358
  497.4 9.9 %collective-permute-done.48.refs_0_ = bf16[1024,1024]{1,0:T(8,128)(2,1)S(1)} collective-permute-done((bf16[1024,1024]{1,0:T(8,128)(2,1)}, bf16[1024,1024]{1,0:T(8,128)(2,1)S(1)}, u32[]{:S(2)}, u32[]{:S(2)}) %collective-permute-start.48) | collective-permute-done | bytes 2097184 | tf_op jit(solution)/shard_map/ppermute | solution.py:362
  507.3 8.7 %collective-permute-done.47.refs_0_ = bf16[1024,1024]{1,0:T(8,128)(2,1)S(1)} collective-permute-done((bf16[1024,1024]{1,0:T(8,128)(2,1)S(1)}, bf16[1024,1024]{1,0:T(8,128)(2,1)S(1)}, u32[]{:S(2)}, u32[]{:S(2)}) %collective-permute-start.47) | collective-permute-done | bytes 2097184 | tf_op jit(solution)/shard_map/ppermute | solution.py:455
  534.5 17.8 %collective-permute-done.58.refs_0_ = bf16[1024,1024]{1,0:T(8,128)(2,1)S(1)} collective-permute-done((bf16[1024,1024]{1,0:T(8,128)(2,1)S(1)}, bf16[1024,1024]{1,0:T(8,128)(2,1)S(1)}, u32[]{:S(2)}, u32[]{:S(2)}) %collective-permute-start.58) | collective-permute-done | bytes 2097184 | tf_op jit(solution)/shard_map/ppermute | solution.py:362
  558.9 15.8 %collective-permute-done.56.refs_1_ = bf16[256,2048]{1,0:T(8,128)(2,1)S(1)} collective-permute-done((bf16[256,2048]{1,0:T(8,128)(2,1)S(1)}, bf16[256,2048]{1,0:T(8,128)(2,1)S(1)}, u32[]{:S(2)}, u32[]{:S(2)}) %collective-permute-start.56) | collective-permute-done | bytes 1048608 | tf_op jit(solution)/shard_map/ppermute | solution.py:362
  657.2 13.8 %collective-permute-done.75.refs_0_ = bf16[1024,1024]{1,0:T(8,128)(2,1)S(1)} collective-permute-done((bf16[1024,1024]{1,0:T(8,128)(2,1)S(1)}, bf16[1024,1024]{1,0:T(8,128)(2,1)S(1)}, u32[]{:S(2)}, u32[]{:S(2)}) %collective-permute-start.75) | collective-permute-done | bytes 2097184 | tf_op jit(solution)/shard_map/ppermute | solution.py:455
  687.5 16.4 %collective-permute-done.79.refs_0_ = bf16[2048,256]{1,0:T(8,128)(2,1)S(1)} collective-permute-done((bf16[2048,256]{1,0:T(8,128)(2,1)S(1)}, bf16[2048,256]{1,0:T(8,128)(2,1)S(1)}, u32[]{:S(2)}, u32[]{:S(2)}) %collective-permute-start.79) | collective-permute-done | bytes 1048608 | tf_op jit(solution)/shard_map/ppermute | solution.py:455
  713.5 7.5 collective-permute-done.84.refs_0_
  736.8 8.1 %collective-permute-done.81.refs_0_ = f32[8,2048]{1,0:T(8,128)S(1)} collective-permute-done((f32[8,2048]{1,0:T(8,128)S(1)}, f32[8,2048]{1,0:T(8,128)S(1)}, u32[]{:S(2)}, u32[]{:S(2)}) %collective-permute-start.81) | collective-permute-done | bytes 65568 | tf_op jit(solution)/shard_map/ppermute | solution.py:362
  746.6 13.3 %collective-permute-done.85.refs_0_ = f32[8,2048]{1,0:T(8,128)S(1)} collective-permute-done((f32[8,2048]{1,0:T(8,128)S(1)}, f32[8,2048]{1,0:T(8,128)S(1)}, u32[]{:S(2)}, u32[]{:S(2)}) %collective-permute-start.85) | collective-permute-done | bytes 65568 | tf_op jit(solution)/shard_map/ppermute | solution.py:455
  769.6 18.4 %collective-permute-done.90.refs_0_ = bf16[2048,256]{1,0:T(8,128)(2,1)S(1)} collective-permute-done((bf16[2048,256]{1,0:T(8,128)(2,1)S(1)}, bf16[2048,256]{1,0:T(8,128)(2,1)S(1)}, u32[]{:S(2)}, u32[]{:S(2)}) %collective-permute-start.90) | collective-permute-done | bytes 1048608 | tf_op jit(solution)/shard_map/ppermute | solution.py:362
  (860 shorter events, 480.0 us)
Async XLA Ops:
  232.9 50.4 %collective-permute-start.34 = (bf16[1024,1024]{1,0:T(8,128)(2,1)S(1)}, bf16[1024,1024]{1,0:T(8,128)(2,1)S(1)}, u32[]{:S(2)}, u32[]{:S(2)}) collective-permute-start(bf16[1024,1024]{1,0:T(8,128)(2,1)S(1)} %up_part.2.refs_2_), channel_id=1, source_target_pairs={{0,8},{24,16},{1,9},{25,17},{2,10},{26,18},{3,11},{27,19},{4,12},{... | collective-permute-start | bytes 6291464 | tf_op jit(solution)/shard_map/ppermute | solution.py:455
  298.4 50.7 %collective-permute-start.39 = (bf16[1024,1024]{1,0:T(8,128)(2,1)}, bf16[1024,1024]{1,0:T(8,128)(2,1)}, u32[]{:S(2)}, u32[]{:S(2)}) collective-permute-start(bf16[1024,1024]{1,0:T(8,128)(2,1)} %down_part.2.refs_2_), channel_id=1, source_target_pairs={{0,8},{24,16},{1,9},{25,17},{2,10},{26,18},{3,11},{27,19},{4,12},{... | collective-permute-start | bytes 6291464 | tf_op jit(solution)/shard_map/ppermute | solution.py:455
  307.1 46.7 %collective-permute-start.38 = (bf16[1024,1024]{1,0:T(8,128)(2,1)}, bf16[1024,1024]{1,0:T(8,128)(2,1)}, u32[]{:S(2)}, u32[]{:S(2)}) collective-permute-start(bf16[1024,1024]{1,0:T(8,128)(2,1)} %copy-done.26), channel_id=1, source_target_pairs={{8,16},{16,8},{9,17},{17,9},{10,18},{18,10},{11,19},{19,11},{12,20... | collective-permute-start | bytes 6291464 | tf_op jit(solution)/shard_map/ppermute | solution.py:455
  332.4 89.3 %collective-permute-start.42 = (bf16[1024,1024]{1,0:T(8,128)(2,1)S(1)}, bf16[1024,1024]{1,0:T(8,128)(2,1)S(1)}, u32[]{:S(2)}, u32[]{:S(2)}) collective-permute-start(bf16[1024,1024]{1,0:T(8,128)(2,1)S(1)} %copy-done.39), channel_id=1, source_target_pairs={{0,8},{24,16},{1,9},{25,17},{2,10},{26,18},{3,11},{27,19},{4,12},{... | collective-permute-start | bytes 6291464 | tf_op jit(solution)/shard_map/ppermute | solution.py:455
  352.9 65.0 %collective-permute-start.43 = (bf16[1024,1024]{1,0:T(8,128)(2,1)S(1)}, bf16[1024,1024]{1,0:T(8,128)(2,1)S(1)}, u32[]{:S(2)}, u32[]{:S(2)}) collective-permute-start(bf16[1024,1024]{1,0:T(8,128)(2,1)S(1)} %add_convert_fusion.6.refs_2_), channel_id=1, source_target_pairs={{8,16},{16,8},{9,17},{17,9},{10,18},{18,10},{11,19},{19,11},{12,20... | collective-permute-start | bytes 6291464 | tf_op jit(solution)/shard_map/ppermute | solution.py:455
  366.5 73.4 %collective-permute-start.45 = (bf16[1024,1024]{1,0:T(8,128)(2,1)S(1)}, bf16[1024,1024]{1,0:T(8,128)(2,1)S(1)}, u32[]{:S(2)}, u32[]{:S(2)}) collective-permute-start(bf16[1024,1024]{1,0:T(8,128)(2,1)S(1)} %add_convert_fusion.5.refs_2_), channel_id=1, source_target_pairs={{8,0},{16,24},{9,1},{17,25},{10,2},{18,26},{11,3},{19,27},{12,4},{... | collective-permute-start | bytes 6291464 | tf_op jit(solution)/shard_map/ppermute | solution.py:455
  367.8 56.3 %collective-permute-start.41 = (bf16[256,2048]{1,0:T(8,128)(2,1)S(1)}, bf16[256,2048]{1,0:T(8,128)(2,1)S(1)}, u32[]{:S(2)}, u32[]{:S(2)}) collective-permute-start(bf16[256,2048]{1,0:T(8,128)(2,1)S(1)} %out_part.2.refs_5_), channel_id=1, source_target_pairs={{0,4},{4,0},{1,5},{5,1},{2,6},{6,2},{3,7},{7,3},{8,12},{12,8},{9,1... | collective-permute-start | bytes 3145736 | tf_op jit(solution)/shard_map/ppermute | solution.py:362
  420.2 49.1 %collective-permute-start.51 = (bf16[1024,1024]{1,0:T(8,128)(2,1)}, bf16[1024,1024]{1,0:T(8,128)(2,1)}, u32[]{:S(2)}, u32[]{:S(2)}) collective-permute-start(bf16[1024,1024]{1,0:T(8,128)(2,1)} %add_convert_fusion.4.refs_2_), channel_id=1, source_target_pairs={{8,0},{16,24},{9,1},{17,25},{10,2},{18,26},{11,3},{19,27},{12,4},{... | collective-permute-start | bytes 6291464 | tf_op jit(solution)/shard_map/ppermute | solution.py:455
  429.5 43.3 %collective-permute-start.50 = (bf16[1024,1024]{1,0:T(8,128)(2,1)}, bf16[1024,1024]{1,0:T(8,128)(2,1)}, u32[]{:S(2)}, u32[]{:S(2)}) collective-permute-start(bf16[1024,1024]{1,0:T(8,128)(2,1)} %add_convert_fusion.3.refs_2_), channel_id=1, source_target_pairs={{8,16},{16,8},{9,17},{17,9},{10,18},{18,10},{11,19},{19,11},{12,20... | collective-permute-start | bytes 6291464 | tf_op jit(solution)/shard_map/ppermute | solution.py:455
  458.6 48.7 %collective-permute-start.48 = (bf16[1024,1024]{1,0:T(8,128)(2,1)}, bf16[1024,1024]{1,0:T(8,128)(2,1)S(1)}, u32[]{:S(2)}, u32[]{:S(2)}) collective-permute-start(bf16[1024,1024]{1,0:T(8,128)(2,1)} %copy-done.36), channel_id=1, source_target_pairs={{0,4},{4,0},{1,5},{5,1},{2,6},{6,2},{3,7},{7,3},{8,12},{12,8},{9,1... | collective-permute-start | bytes 6291464 | tf_op jit(solution)/shard_map/ppermute | solution.py:362
  469.4 46.6 %collective-permute-start.47 = (bf16[1024,1024]{1,0:T(8,128)(2,1)S(1)}, bf16[1024,1024]{1,0:T(8,128)(2,1)S(1)}, u32[]{:S(2)}, u32[]{:S(2)}) collective-permute-start(bf16[1024,1024]{1,0:T(8,128)(2,1)S(1)} %copy-done.41), channel_id=1, source_target_pairs={{0,8},{24,16},{1,9},{25,17},{2,10},{26,18},{3,11},{27,19},{4,12},{... | collective-permute-start | bytes 6291464 | tf_op jit(solution)/shard_map/ppermute | solution.py:455
  474.8 77.5 %collective-permute-start.58 = (bf16[1024,1024]{1,0:T(8,128)(2,1)S(1)}, bf16[1024,1024]{1,0:T(8,128)(2,1)S(1)}, u32[]{:S(2)}, u32[]{:S(2)}) collective-permute-start(bf16[1024,1024]{1,0:T(8,128)(2,1)S(1)} %broadcast_select_fusion.2.refs_2_), channel_id=1, source_target_pairs={{0,4},{4,0},{1,5},{5,1},{2,6},{6,2},{3,7},{7,3},{8,12},{12,8},{9,1... | collective-permute-start | bytes 6291464 | tf_op jit(solution)/shard_map/ppermute | solution.py:362
  493.0 59.7 %collective-permute-start.57 = (bf16[1024,1024]{1,0:T(8,128)(2,1)S(1)}, bf16[1024,1024]{1,0:T(8,128)(2,1)S(1)}, u32[]{:S(2)}, u32[]{:S(2)}) collective-permute-start(bf16[1024,1024]{1,0:T(8,128)(2,1)S(1)} %add_convert_fusion.2.refs_2_), channel_id=1, source_target_pairs={{8,0},{16,24},{9,1},{17,25},{10,2},{18,26},{11,3},{19,27},{12,4},{... | collective-permute-start | bytes 6291464 | tf_op jit(solution)/shard_map/ppermute | solution.py:455
  495.9 36.9 %collective-permute-start.59 = (bf16[256,2048]{1,0:T(8,128)(2,1)S(1)}, bf16[256,2048]{1,0:T(8,128)(2,1)S(1)}, u32[]{:S(2)}, u32[]{:S(2)}) collective-permute-start(bf16[256,2048]{1,0:T(8,128)(2,1)S(1)} %add_convert_fusion.21.refs_2_), channel_id=1, source_target_pairs={{8,16},{16,8},{9,17},{17,9},{10,18},{18,10},{11,19},{19,11},{12,20... | collective-permute-start | bytes 3145736 | tf_op jit(solution)/shard_map/ppermute | solution.py:455
  527.2 47.5 %collective-permute-start.56 = (bf16[256,2048]{1,0:T(8,128)(2,1)S(1)}, bf16[256,2048]{1,0:T(8,128)(2,1)S(1)}, u32[]{:S(2)}, u32[]{:S(2)}) collective-permute-start(bf16[256,2048]{1,0:T(8,128)(2,1)S(1)} %add_convert_fusion.19.refs_2_), channel_id=1, source_target_pairs={{0,4},{4,0},{1,5},{5,1},{2,6},{6,2},{3,7},{7,3},{8,12},{12,8},{9,1... | collective-permute-start | bytes 3145736 | tf_op jit(solution)/shard_map/ppermute | solution.py:362
  532.8 41.9 %collective-permute-start.55 = (bf16[256,2048]{1,0:T(8,128)(2,1)S(1)}, bf16[256,2048]{1,0:T(8,128)(2,1)S(1)}, u32[]{:S(2)}, u32[]{:S(2)}) collective-permute-start(bf16[256,2048]{1,0:T(8,128)(2,1)S(1)} %add_convert_fusion.20.refs_3_), channel_id=1, source_target_pairs={{0,2},{2,0},{1,3},{3,1},{4,6},{6,4},{5,7},{7,5},{8,10},{10,8},{9,1... | collective-permute-start | bytes 3145736 | tf_op jit(solution)/shard_map/ppermute | solution.py:358
  552.7 45.4 %collective-permute-start.62 = (bf16[1024,1024]{1,0:T(8,128)(2,1)}, bf16[1024,1024]{1,0:T(8,128)(2,1)}, u32[]{:S(2)}, u32[]{:S(2)}) collective-permute-start(bf16[1024,1024]{1,0:T(8,128)(2,1)} %add_convert_fusion.1.refs_2_), channel_id=1, source_target_pairs={{8,16},{16,8},{9,17},{17,9},{10,18},{18,10},{11,19},{19,11},{12,20... | collective-permute-start | bytes 6291464 | tf_op jit(solution)/shard_map/ppermute | solution.py:455
  556.3 75.3 %collective-permute-start.70 = (bf16[1024,1024]{1,0:T(8,128)(2,1)}, bf16[1024,1024]{1,0:T(8,128)(2,1)}, u32[]{:S(2)}, u32[]{:S(2)}) collective-permute-start(bf16[1024,1024]{1,0:T(8,128)(2,1)} %broadcast_select_fusion.1.refs_3_), channel_id=1, source_target_pairs={{0,4},{4,0},{1,5},{5,1},{2,6},{6,2},{3,7},{7,3},{8,12},{12,8},{9,1... | collective-permute-start | bytes 6291464 | tf_op jit(solution)/shard_map/ppermute | solution.py:362
  611.0 60.0 %collective-permute-start.75 = (bf16[1024,1024]{1,0:T(8,128)(2,1)S(1)}, bf16[1024,1024]{1,0:T(8,128)(2,1)S(1)}, u32[]{:S(2)}, u32[]{:S(2)}) collective-permute-start(bf16[1024,1024]{1,0:T(8,128)(2,1)S(1)} %add_convert_fusion.refs_2_), channel_id=1, source_target_pairs={{8,0},{16,24},{9,1},{17,25},{10,2},{18,26},{11,3},{19,27},{12,4},{... | collective-permute-start | bytes 6291464 | tf_op jit(solution)/shard_map/ppermute | solution.py:455
  644.9 40.1 %collective-permute-start.72 = (f32[6,2048]{1,0:T(8,128)S(1)}, f32[6,2048]{1,0:T(8,128)S(1)}, u32[]{:S(2)}, u32[]{:S(2)}) collective-permute-start(f32[6,2048]{1,0:T(8,128)S(1)} %stack.34.refs_3_), channel_id=1, source_target_pairs={{0,1},{1,0},{2,3},{3,2},{4,5},{5,4},{6,7},{7,6},{8,9},{9,8},{10,11... | collective-permute-start | bytes 147464 | tf_op jit(solution)/shard_map/ppermute | solution.py:354
  648.8 37.1 %collective-permute-start.80 = (bf16[256,2048]{1,0:T(8,128)(2,1)S(1)}, bf16[256,2048]{1,0:T(8,128)(2,1)S(1)}, u32[]{:S(2)}, u32[]{:S(2)}) collective-permute-start(bf16[256,2048]{1,0:T(8,128)(2,1)S(1)} %broadcast_select_fusion.7.refs_2_), channel_id=1, source_target_pairs={{0,4},{4,0},{1,5},{5,1},{2,6},{6,2},{3,7},{7,3},{8,12},{12,8},{9,1... | collective-permute-start | bytes 3145736 | tf_op jit(solution)/shard_map/ppermute | solution.py:362
  672.4 48.6 %collective-permute-start.84 = (bf16[1024,1024]{1,0:T(8,128)(2,1)S(1)}, bf16[1024,1024]{1,0:T(8,128)(2,1)S(1)}, u32[]{:S(2)}, u32[]{:S(2)}) collective-permute-start(bf16[1024,1024]{1,0:T(8,128)(2,1)S(1)} %broadcast_select_fusion.refs_2_), channel_id=1, source_target_pairs={{0,4},{4,0},{1,5},{5,1},{2,6},{6,2},{3,7},{7,3},{8,12},{12,8},{9,1... | collective-permute-start | bytes 6291464 | tf_op jit(solution)/shard_map/ppermute | solution.py:362
  709.1 51.5 %collective-permute-start.89 = (bf16[2048,256]{1,0:T(8,128)(2,1)S(1)}, bf16[2048,256]{1,0:T(8,128)(2,1)S(1)}, u32[]{:S(2)}, u32[]{:S(2)}) collective-permute-start(bf16[2048,256]{1,0:T(8,128)(2,1)S(1)} %broadcast_select_fusion.6.refs_2_), channel_id=1, source_target_pairs={{0,4},{4,0},{1,5},{5,1},{2,6},{6,2},{3,7},{7,3},{8,12},{12,8},{9,1... | collective-permute-start | bytes 3145736 | tf_op jit(solution)/shard_map/ppermute | solution.py:362
  721.4 39.5 %collective-permute-start.88 = (bf16[2048,256]{1,0:T(8,128)(2,1)S(1)}, bf16[2048,256]{1,0:T(8,128)(2,1)S(1)}, u32[]{:S(2)}, u32[]{:S(2)}) collective-permute-start(bf16[2048,256]{1,0:T(8,128)(2,1)S(1)} %add_convert_fusion.8.refs_2_), channel_id=1, source_target_pairs={{8,0},{16,24},{9,1},{17,25},{10,2},{18,26},{11,3},{19,27},{12,4},{... | collective-permute-start | bytes 3145736 | tf_op jit(solution)/shard_map/ppermute | solution.py:455
  (250 other events, 2740.2 us)

commit v4 on v3

--- a/solution.py
+++ b/solution.py
@@ -791,9 +791,9 @@
 S_STEPS, G_STEPS, F_STEPS = [S0, S1, S2, S3, SB, SE, SL], [G0, G1, G2, G3, GB, GE, GL], [F0, F1, F2, F3, FB, FE, FL]
 D_HOPS, U_HOPS, Q_HOPS, O_HOPS, V_HOPS = (d0, d1), (u0, u1), (q0, q1, q2), o, v
 ORDER = (
-    S3, U1, SB, S1, S2, SE, SL, D0, S0, u1, S, D1, BN, BF, d0, u1, O, ATT, d0, d1, o, F3, u1, FB, U0, F1, F2, o,
-    d0, d1, FE, FL, u1, u0, G3, F0, o, d0, d1, GB, FN, G1, G2, u0, Q0, GE, GL, G0, o, d1, Q1, q0, G, u0, Q2, V,
-    q0, q1, v, o, q2, q0, q1, v, u0, q2, q1, v, v, q0, q2, q1, v, q2,
+    S3, U1, SB, S1, S2, SE, SL, D0, S0, u1, S, D1, BN, BF, d0, u1, O, ATT, d1, o, d0, u1, U0, o, d1, d0, u1, u0,
+    o, d1, Q0, d0, F3, u0, FB, F1, o, F2, q0, FE, d1, FL, Q2, F0, u0, o, Q1, q0, FN, q2, q0, q1, q2, V, u0, v,
+    q1, q2, G3, v, q0, GB, G1, G2, q1, q2, GE, GL, v, G0, v, q1, v, G,
 )
 
 

time: 798 us -> 763 us (0.956)
  waiting for transfers between devices: 263 us -> 228 us
    ppermute x21, waiting for transfers between devices: 110 us -> 46.1 us  [over(): return lax.ppermute(value, 'seq', SWAP)]
    ppermute x26, waiting for transfers between devices: 82.6 us -> 101 us  [on_line(): return lax.ppermute(value, 'dp', pairs)]
    ppermute x15, waiting for transfers between devices: 65.4 us -> 75.5 us  [across(): return lax.ppermute(value, 'tensor', ACROSS)]
    unnamed x385 -> x359, local copies, waits for them, and re-layouts: 60.5 us -> 55.9 us
  transfers between devices with their start and end apart: 91 -> 91, of which waited for: 36 -> 32; matrix products, arithmetic and copies ran while one was open for 15% -> 16% of each run, Pallas kernels for 26% -> 28%
where the time goes in v4:
time: 763 us; the launch traced here: 756 us
  waiting for transfers between devices  228 us (30%)
  Pallas kernels  224 us (29%)
  other arithmetic  106 us (14%)
  starting transfers between devices  102 us (13%)
  local copies, waits for them, and re-layouts  73.6 us (10%)
  matrix products  12.3 us (2%)
  between operations  9.42 us (1%)
    pallas_call x29, Pallas kernels, fused(): pl.pallas_call(kernel, grid_spec=pltpu.PrefetchScalarGridSpec(num_scalar_...  124 us
    ppermute x26, waiting for transfers between devices, on_line(): return lax.ppermute(value, 'dp', pairs)  101 us
    ppermute x15, waiting for transfers between devices, across(): return lax.ppermute(value, 'tensor', ACROSS)  75.5 us
    pallas_call x4, Pallas kernels, _attention_call(): pl.pallas_call(kernel, out_shape=outs, in_specs=[pl.BlockSpec(memory_spac...  61.9 us
    ppermute x26, starting transfers between devices, on_line(): return lax.ppermute(value, 'dp', pairs)  56.8 us
    unnamed x359, local copies, waits for them, and re-layouts  55.9 us
    ppermute x21, waiting for transfers between devices, over(): return lax.ppermute(value, 'seq', SWAP)  46.1 us
    pallas_call x81, Pallas kernels, tie(): pl.pallas_call(lambda *refs: None, out_shape=[jax.ShapeDtypeStruct(v.shap...  38.1 us
  transfers between devices with their start and end apart: 91, of which 32 were waited for; matrix products, arithmetic and copies ran while one was open for 16% of the time, Pallas kernels for 28%

profile of v4, /device:TPU:0, one launch (start us, length us, event | category | flops | bytes accessed | tf_op | source)
XLA Modules:
  0.0 755.6 jit_solution(16951544961460710169)
XLA Ops:
  27.1 7.6 collective-permute-done.refs_0_
  68.8 17.4 %attention_forward.3 = (bf16[1024,256]{1,0:T(8,128)(2,1)S(1)}, f32[1024,128]{1,0:T(8,128)S(1)}) custom-call(s32[1]{0:T(128)} %constant.120.clone.1.first_block, s32[8]{0:T(128)S(1)} %iota_xor_fusion.place, s32[8,9]{1,0:T(8,128)S(1)} %pad_add_fusion.lists, bf16[2048,768]{1,0:T(8,128)(2,1)S(1)} %pad_maximum_fusion.2.refs_2_.qkv, ...), custom_call_target="tpu_custom_call" | custom-call | tf_op jit(solution)/shard_map/attention_forward/pallas_call | solution.py:286
  87.1 6.1 attention_forward.4
  94.3 6.4 collective-permute-start.11
  106.1 7.6 %collective-permute-done.11.refs_1_ = bf16[128,2048]{1,0:T(8,128)(2,1)S(1)} collective-permute-done((bf16[128,2048]{1,0:T(8,128)(2,1)S(1)}, bf16[128,2048]{1,0:T(8,128)(2,1)S(1)}, u32[]{:S(2)}, u32[]{:S(2)}) %collective-permute-start.11) | collective-permute-done | bytes 524320 | tf_op jit(solution)/shard_map/ppermute | solution.py:362
  123.3 7.3 act_gradient.2
  130.6 15.4 %collective-permute-done.15.refs_0_ = bf16[256,2048]{1,0:T(8,128)(2,1)S(1)} collective-permute-done((bf16[256,2048]{1,0:T(8,128)(2,1)S(1)}, bf16[256,2048]{1,0:T(8,128)(2,1)S(1)}, u32[]{:S(2)}, u32[]{:S(2)}) %collective-permute-start.15) | collective-permute-done | bytes 1048608 | tf_op jit(solution)/shard_map/ppermute | solution.py:358
  154.4 7.0 act_gradient.3
  241.2 14.3 %collective-permute-done.29.refs_0_ = bf16[256,2048]{1,0:T(8,128)(2,1)S(1)} collective-permute-done((bf16[256,2048]{1,0:T(8,128)(2,1)S(1)}, bf16[256,2048]{1,0:T(8,128)(2,1)S(1)}, u32[]{:S(2)}, u32[]{:S(2)}) %collective-permute-start.29) | collective-permute-done | bytes 1048608 | tf_op jit(solution)/shard_map/ppermute | solution.py:358
  260.5 6.2 down_part.2.refs_2_
  272.1 13.0 %collective-permute-done.34.refs_0_ = bf16[1024,1024]{1,0:T(8,128)(2,1)S(1)} collective-permute-done((bf16[1024,1024]{1,0:T(8,128)(2,1)S(1)}, bf16[1024,1024]{1,0:T(8,128)(2,1)S(1)}, u32[]{:S(2)}, u32[]{:S(2)}) %collective-permute-start.34) | collective-permute-done | bytes 2097184 | tf_op jit(solution)/shard_map/ppermute | solution.py:455
  338.9 8.1 %collective-permute-done.39.refs_0_ = bf16[1024,1024]{1,0:T(8,128)(2,1)} collective-permute-done((bf16[1024,1024]{1,0:T(8,128)(2,1)}, bf16[1024,1024]{1,0:T(8,128)(2,1)}, u32[]{:S(2)}, u32[]{:S(2)}) %collective-permute-start.39) | collective-permute-done | bytes 2097184 | tf_op jit(solution)/shard_map/ppermute | solution.py:455
  375.3 34.4 %attention_backward.1.refs_2_.refs_1_.refs_0_ = bf16[2048,768]{1,0:T(8,128)(2,1)S(1)} custom-call(s32[8]{0:T(128)S(1)} %iota_xor_fusion.place, s32[8,9]{1,0:T(8,128)S(1)} %pad_add_fusion.1.lists, bf16[2048,768]{1,0:T(8,128)(2,1)S(1)} %copy-done.5, bf16[2048,256]{1,0:T(8,128)(2,1)S(1)} %pad_maximum_fusion.8.do, bf16[1024,256]{1,0:T(8,128)(2,1)S(1)} %copy-done.89, ...), custom_call_target="tpu_custom_call" | custom-call | tf_op jit(solution)/shard_map/attention_backward/pallas_call | solution.py:286
  412.0 8.4 %collective-permute-start.47 = (bf16[256,2048]{1,0:T(8,128)(2,1)S(1)}, bf16[256,2048]{1,0:T(8,128)(2,1)}, u32[]{:S(2)}, u32[]{:S(2)}) collective-permute-start(bf16[256,2048]{1,0:T(8,128)(2,1)S(1)} %add_convert_fusion.23.refs_2_), channel_id=1, source_target_pairs={{0,8},{24,16},{1,9},{25,17},{2,10},{26,18},{3,11},{27,19},{4,12},{... | collective-permute-start | bytes 3145736 | tf_op jit(solution)/shard_map/ppermute | solution.py:455
  451.5 20.4 %collective-permute-done.52.refs_0_ = bf16[1024,1024]{1,0:T(8,128)(2,1)S(1)} collective-permute-done((bf16[1024,1024]{1,0:T(8,128)(2,1)S(1)}, bf16[1024,1024]{1,0:T(8,128)(2,1)S(1)}, u32[]{:S(2)}, u32[]{:S(2)}) %collective-permute-start.52) | collective-permute-done | bytes 2097184 | tf_op jit(solution)/shard_map/ppermute | solution.py:455
  474.9 9.8 %collective-permute-done.50.refs_0_ = bf16[1024,1024]{1,0:T(8,128)(2,1)S(1)} collective-permute-done((bf16[1024,1024]{1,0:T(8,128)(2,1)S(1)}, bf16[1024,1024]{1,0:T(8,128)(2,1)S(1)}, u32[]{:S(2)}, u32[]{:S(2)}) %collective-permute-start.50) | collective-permute-done | bytes 2097184 | tf_op jit(solution)/shard_map/ppermute | solution.py:455
  498.2 18.7 %collective-permute-done.48.refs_0_ = bf16[1024,1024]{1,0:T(8,128)(2,1)} collective-permute-done((bf16[1024,1024]{1,0:T(8,128)(2,1)}, bf16[1024,1024]{1,0:T(8,128)(2,1)}, u32[]{:S(2)}, u32[]{:S(2)}) %collective-permute-start.48) | collective-permute-done | bytes 2097184 | tf_op jit(solution)/shard_map/ppermute | solution.py:455
  563.9 8.6 %collective-permute-done.57.refs_0_ = bf16[256,2048]{1,0:T(8,128)(2,1)S(1)} collective-permute-done((bf16[256,2048]{1,0:T(8,128)(2,1)S(1)}, bf16[256,2048]{1,0:T(8,128)(2,1)S(1)}, u32[]{:S(2)}, u32[]{:S(2)}) %collective-permute-start.57) | collective-permute-done | bytes 1048608 | tf_op jit(solution)/shard_map/ppermute | solution.py:358
  623.1 15.1 %collective-permute-done.71.refs_0_ = bf16[2048,256]{1,0:T(8,128)(2,1)S(1)} collective-permute-done((bf16[2048,256]{1,0:T(8,128)(2,1)S(1)}, bf16[2048,256]{1,0:T(8,128)(2,1)S(1)}, u32[]{:S(2)}, u32[]{:S(2)}) %collective-permute-start.71) | collective-permute-done | bytes 1048608 | tf_op jit(solution)/shard_map/ppermute | solution.py:455
  648.4 11.6 %collective-permute-done.75.refs_0_ = bf16[1024,1024]{1,0:T(8,128)(2,1)S(1)} collective-permute-done((bf16[1024,1024]{1,0:T(8,128)(2,1)}, bf16[1024,1024]{1,0:T(8,128)(2,1)S(1)}, u32[]{:S(2)}, u32[]{:S(2)}) %collective-permute-start.75) | collective-permute-done | bytes 2097184 | tf_op jit(solution)/shard_map/ppermute | solution.py:362
  670.7 8.9 %collective-permute-done.72.refs_0_ = bf16[2048,256]{1,0:T(8,128)(2,1)S(1)} collective-permute-done((bf16[2048,256]{1,0:T(8,128)(2,1)S(1)}, bf16[2048,256]{1,0:T(8,128)(2,1)S(1)}, u32[]{:S(2)}, u32[]{:S(2)}) %collective-permute-start.72) | collective-permute-done | bytes 1048608 | tf_op jit(solution)/shard_map/ppermute | solution.py:455
  708.0 11.4 %collective-permute-done.80.refs_0_ = bf16[256,2048]{1,0:T(8,128)(2,1)S(1)} collective-permute-done((bf16[256,2048]{1,0:T(8,128)(2,1)S(1)}, bf16[256,2048]{1,0:T(8,128)(2,1)S(1)}, u32[]{:S(2)}, u32[]{:S(2)}) %collective-permute-start.80) | collective-permute-done | bytes 1048608 | tf_op jit(solution)/shard_map/ppermute | solution.py:358
  738.1 7.7 %collective-permute-done.86.refs_0_ = bf16[256,2048]{1,0:T(8,128)(2,1)S(1)} collective-permute-done((bf16[256,2048]{1,0:T(8,128)(2,1)S(1)}, bf16[256,2048]{1,0:T(8,128)(2,1)S(1)}, u32[]{:S(2)}, u32[]{:S(2)}) %collective-permute-start.86) | collective-permute-done | bytes 1048608 | tf_op jit(solution)/shard_map/ppermute | solution.py:358
  745.7 7.5 collective-permute-done.87.refs_1_
  (833 shorter events, 467.3 us)
Async XLA Ops:
  235.8 49.2 %collective-permute-start.34 = (bf16[1024,1024]{1,0:T(8,128)(2,1)S(1)}, bf16[1024,1024]{1,0:T(8,128)(2,1)S(1)}, u32[]{:S(2)}, u32[]{:S(2)}) collective-permute-start(bf16[1024,1024]{1,0:T(8,128)(2,1)S(1)} %up_part.2.refs_2_), channel_id=1, source_target_pairs={{0,8},{24,16},{1,9},{25,17},{2,10},{26,18},{3,11},{27,19},{4,12},{... | collective-permute-start | bytes 6291464 | tf_op jit(solution)/shard_map/ppermute | solution.py:455
  240.1 46.7 %collective-permute-start.32 = (bf16[256,2048]{1,0:T(8,128)(2,1)S(1)}, bf16[256,2048]{1,0:T(8,128)(2,1)S(1)}, u32[]{:S(2)}, u32[]{:S(2)}) collective-permute-start(bf16[256,2048]{1,0:T(8,128)(2,1)S(1)} %add_convert_fusion.25.refs_3_), channel_id=1, source_target_pairs={{0,2},{2,0},{1,3},{3,1},{4,6},{6,4},{5,7},{7,5},{8,10},{10,8},{9,1... | collective-permute-start | bytes 3145736 | tf_op jit(solution)/shard_map/ppermute | solution.py:358
  296.4 50.7 %collective-permute-start.39 = (bf16[1024,1024]{1,0:T(8,128)(2,1)}, bf16[1024,1024]{1,0:T(8,128)(2,1)}, u32[]{:S(2)}, u32[]{:S(2)}) collective-permute-start(bf16[1024,1024]{1,0:T(8,128)(2,1)} %copy-done.37), channel_id=1, source_target_pairs={{0,8},{24,16},{1,9},{25,17},{2,10},{26,18},{3,11},{27,19},{4,12},{... | collective-permute-start | bytes 6291464 | tf_op jit(solution)/shard_map/ppermute | solution.py:455
  303.5 46.8 %collective-permute-start.38 = (bf16[1024,1024]{1,0:T(8,128)(2,1)}, bf16[1024,1024]{1,0:T(8,128)(2,1)}, u32[]{:S(2)}, u32[]{:S(2)}) collective-permute-start(bf16[1024,1024]{1,0:T(8,128)(2,1)} %copy-done.27), channel_id=1, source_target_pairs={{8,16},{16,8},{9,17},{17,9},{10,18},{18,10},{11,19},{19,11},{12,20... | collective-permute-start | bytes 6291464 | tf_op jit(solution)/shard_map/ppermute | solution.py:455
  332.1 77.6 %collective-permute-start.44 = (bf16[1024,1024]{1,0:T(8,128)(2,1)S(1)}, bf16[1024,1024]{1,0:T(8,128)(2,1)S(1)}, u32[]{:S(2)}, u32[]{:S(2)}) collective-permute-start(bf16[1024,1024]{1,0:T(8,128)(2,1)S(1)} %copy-done.40), channel_id=1, source_target_pairs={{0,8},{24,16},{1,9},{25,17},{2,10},{26,18},{3,11},{27,19},{4,12},{... | collective-permute-start | bytes 6291464 | tf_op jit(solution)/shard_map/ppermute | solution.py:455
  355.6 67.3 %collective-permute-start.41 = (bf16[1024,1024]{1,0:T(8,128)(2,1)S(1)}, bf16[1024,1024]{1,0:T(8,128)(2,1)S(1)}, u32[]{:S(2)}, u32[]{:S(2)}) collective-permute-start(bf16[1024,1024]{1,0:T(8,128)(2,1)S(1)} %add_convert_fusion.5.refs_2_), channel_id=1, source_target_pairs={{8,0},{16,24},{9,1},{17,25},{10,2},{18,26},{11,3},{19,27},{12,4},{... | collective-permute-start | bytes 6291464 | tf_op jit(solution)/shard_map/ppermute | solution.py:455
  357.0 63.4 %collective-permute-start.42 = (bf16[1024,1024]{1,0:T(8,128)(2,1)S(1)}, bf16[1024,1024]{1,0:T(8,128)(2,1)S(1)}, u32[]{:S(2)}, u32[]{:S(2)}) collective-permute-start(bf16[1024,1024]{1,0:T(8,128)(2,1)S(1)} %add_convert_fusion.6.refs_2_), channel_id=1, source_target_pairs={{8,16},{16,8},{9,17},{17,9},{10,18},{18,10},{11,19},{19,11},{12,20... | collective-permute-start | bytes 6291464 | tf_op jit(solution)/shard_map/ppermute | solution.py:455
  366.5 45.0 %collective-permute-start.43 = (bf16[256,2048]{1,0:T(8,128)(2,1)S(1)}, bf16[256,2048]{1,0:T(8,128)(2,1)S(1)}, u32[]{:S(2)}, u32[]{:S(2)}) collective-permute-start(bf16[256,2048]{1,0:T(8,128)(2,1)S(1)} %out_part.2.refs_5_), channel_id=1, source_target_pairs={{0,4},{4,0},{1,5},{5,1},{2,6},{6,2},{3,7},{7,3},{8,12},{12,8},{9,1... | collective-permute-start | bytes 3145736 | tf_op jit(solution)/shard_map/ppermute | solution.py:362
  410.8 37.1 %collective-permute-start.46 = (bf16[1024,1024]{1,0:T(8,128)(2,1)S(1)}, bf16[1024,1024]{1,0:T(8,128)(2,1)S(1)}, u32[]{:S(2)}, u32[]{:S(2)}) collective-permute-start(bf16[1024,1024]{1,0:T(8,128)(2,1)S(1)} %add_convert_fusion.4.refs_2_), channel_id=1, source_target_pairs={{8,16},{16,8},{9,17},{17,9},{10,18},{18,10},{11,19},{19,11},{12,20... | collective-permute-start | bytes 6291464 | tf_op jit(solution)/shard_map/ppermute | solution.py:455
  421.4 50.5 %collective-permute-start.52 = (bf16[1024,1024]{1,0:T(8,128)(2,1)S(1)}, bf16[1024,1024]{1,0:T(8,128)(2,1)S(1)}, u32[]{:S(2)}, u32[]{:S(2)}) collective-permute-start(bf16[1024,1024]{1,0:T(8,128)(2,1)S(1)} %add_convert_fusion.3.refs_2_), channel_id=1, source_target_pairs={{8,0},{16,24},{9,1},{17,25},{10,2},{18,26},{11,3},{19,27},{12,4},{... | collective-permute-start | bytes 6291464 | tf_op jit(solution)/shard_map/ppermute | solution.py:455
  425.0 49.9 %collective-permute-start.51 = (bf16[1024,1024]{1,0:T(8,128)(2,1)S(1)}, bf16[1024,1024]{1,0:T(8,128)(2,1)S(1)}, u32[]{:S(2)}, u32[]{:S(2)}) collective-permute-start(bf16[1024,1024]{1,0:T(8,128)(2,1)S(1)} %broadcast_select_fusion.3.refs_2_), channel_id=1, source_target_pairs={{0,4},{4,0},{1,5},{5,1},{2,6},{6,2},{3,7},{7,3},{8,12},{12,8},{9,1... | collective-permute-start | bytes 6291464 | tf_op jit(solution)/shard_map/ppermute | solution.py:362
  434.0 50.8 %collective-permute-start.50 = (bf16[1024,1024]{1,0:T(8,128)(2,1)S(1)}, bf16[1024,1024]{1,0:T(8,128)(2,1)S(1)}, u32[]{:S(2)}, u32[]{:S(2)}) collective-permute-start(bf16[1024,1024]{1,0:T(8,128)(2,1)S(1)} %up_part.3.refs_2_), channel_id=1, source_target_pairs={{0,8},{24,16},{1,9},{25,17},{2,10},{26,18},{3,11},{27,19},{4,12},{... | collective-permute-start | bytes 6291464 | tf_op jit(solution)/shard_map/ppermute | solution.py:455
  446.3 42.9 %collective-permute-start.49 = (bf16[256,2048]{1,0:T(8,128)(2,1)}, bf16[256,2048]{1,0:T(8,128)(2,1)}, u32[]{:S(2)}, u32[]{:S(2)}) collective-permute-start(bf16[256,2048]{1,0:T(8,128)(2,1)} %add_convert_fusion.22.refs_2_), channel_id=1, source_target_pairs={{8,16},{16,8},{9,17},{17,9},{10,18},{18,10},{11,19},{19,11},{12,20... | collective-permute-start | bytes 3145736 | tf_op jit(solution)/shard_map/ppermute | solution.py:455
  450.2 66.7 %collective-permute-start.48 = (bf16[1024,1024]{1,0:T(8,128)(2,1)}, bf16[1024,1024]{1,0:T(8,128)(2,1)}, u32[]{:S(2)}, u32[]{:S(2)}) collective-permute-start(bf16[1024,1024]{1,0:T(8,128)(2,1)} %add_convert_fusion.2.refs_2_), channel_id=1, source_target_pairs={{8,0},{16,24},{9,1},{17,25},{10,2},{18,26},{11,3},{19,27},{12,4},{... | collective-permute-start | bytes 6291464 | tf_op jit(solution)/shard_map/ppermute | solution.py:455
  473.4 54.9 %collective-permute-start.53 = (bf16[1024,1024]{1,0:T(8,128)(2,1)}, bf16[1024,1024]{1,0:T(8,128)(2,1)}, u32[]{:S(2)}, u32[]{:S(2)}) collective-permute-start(bf16[1024,1024]{1,0:T(8,128)(2,1)} %broadcast_select_fusion.2.refs_2_), channel_id=1, source_target_pairs={{0,4},{4,0},{1,5},{5,1},{2,6},{6,2},{3,7},{7,3},{8,12},{12,8},{9,1... | collective-permute-start | bytes 6291464 | tf_op jit(solution)/shard_map/ppermute | solution.py:362
  487.1 46.3 %collective-permute-start.54 = (bf16[1024,1024]{1,0:T(8,128)(2,1)}, bf16[1024,1024]{1,0:T(8,128)(2,1)}, u32[]{:S(2)}, u32[]{:S(2)}) collective-permute-start(bf16[1024,1024]{1,0:T(8,128)(2,1)} %add_convert_fusion.1.refs_2_), channel_id=1, source_target_pairs={{8,16},{16,8},{9,17},{17,9},{10,18},{18,10},{11,19},{19,11},{12,20... | collective-permute-start | bytes 6291464 | tf_op jit(solution)/shard_map/ppermute | solution.py:455
  492.8 58.4 %collective-permute-start.56 = (bf16[256,2048]{1,0:T(8,128)(2,1)S(1)}, bf16[256,2048]{1,0:T(8,128)(2,1)S(1)}, u32[]{:S(2)}, u32[]{:S(2)}) collective-permute-start(bf16[256,2048]{1,0:T(8,128)(2,1)S(1)} %add_convert_fusion.21.refs_2_), channel_id=1, source_target_pairs={{8,0},{16,24},{9,1},{17,25},{10,2},{18,26},{11,3},{19,27},{12,4},{... | collective-permute-start | bytes 3145736 | tf_op jit(solution)/shard_map/ppermute | solution.py:455
  520.8 40.7 %collective-permute-start.58 = (bf16[1024,1024]{1,0:T(8,128)(2,1)S(1)}, bf16[1024,1024]{1,0:T(8,128)(2,1)S(1)}, u32[]{:S(2)}, u32[]{:S(2)}) collective-permute-start(bf16[1024,1024]{1,0:T(8,128)(2,1)S(1)} %broadcast_select_fusion.1.refs_2_), channel_id=1, source_target_pairs={{0,4},{4,0},{1,5},{5,1},{2,6},{6,2},{3,7},{7,3},{8,12},{12,8},{9,1... | collective-permute-start | bytes 6291464 | tf_op jit(solution)/shard_map/ppermute | solution.py:362
  537.3 52.1 %collective-permute-start.63 = (bf16[1024,1024]{1,0:T(8,128)(2,1)S(1)}, bf16[1024,1024]{1,0:T(8,128)(2,1)S(1)}, u32[]{:S(2)}, u32[]{:S(2)}) collective-permute-start(bf16[1024,1024]{1,0:T(8,128)(2,1)S(1)} %add_convert_fusion.refs_2_), channel_id=1, source_target_pairs={{8,0},{16,24},{9,1},{17,25},{10,2},{18,26},{11,3},{19,27},{12,4},{... | collective-permute-start | bytes 6291464 | tf_op jit(solution)/shard_map/ppermute | solution.py:455
  580.9 38.3 %collective-permute-start.64 = (bf16[2048,256]{1,0:T(8,128)(2,1)S(1)}, bf16[2048,256]{1,0:T(8,128)(2,1)S(1)}, u32[]{:S(2)}, u32[]{:S(2)}) collective-permute-start(bf16[2048,256]{1,0:T(8,128)(2,1)S(1)} %projection_part.4.refs_2_), channel_id=1, source_target_pairs={{0,8},{24,16},{1,9},{25,17},{2,10},{26,18},{3,11},{27,19},{4,12},{... | collective-permute-start | bytes 3145736 | tf_op jit(solution)/shard_map/ppermute | solution.py:455
  597.5 42.2 %collective-permute-start.70 = (bf16[2048,256]{1,0:T(8,128)(2,1)S(1)}, bf16[2048,256]{1,0:T(8,128)(2,1)S(1)}, u32[]{:S(2)}, u32[]{:S(2)}) collective-permute-start(bf16[2048,256]{1,0:T(8,128)(2,1)S(1)} %projection_part.5.refs_2_), channel_id=1, source_target_pairs={{0,8},{24,16},{1,9},{25,17},{2,10},{26,18},{3,11},{27,19},{4,12},{... | collective-permute-start | bytes 3145736 | tf_op jit(solution)/shard_map/ppermute | solution.py:455
  608.0 52.1 %collective-permute-start.75 = (bf16[1024,1024]{1,0:T(8,128)(2,1)}, bf16[1024,1024]{1,0:T(8,128)(2,1)S(1)}, u32[]{:S(2)}, u32[]{:S(2)}) collective-permute-start(bf16[1024,1024]{1,0:T(8,128)(2,1)} %broadcast_select_fusion.refs_2_), channel_id=1, source_target_pairs={{0,4},{4,0},{1,5},{5,1},{2,6},{6,2},{3,7},{7,3},{8,12},{12,8},{9,1... | collective-permute-start | bytes 6291464 | tf_op jit(solution)/shard_map/ppermute | solution.py:362
  639.3 48.8 %collective-permute-start.76 = (bf16[2048,256]{1,0:T(8,128)(2,1)}, bf16[2048,256]{1,0:T(8,128)(2,1)}, u32[]{:S(2)}, u32[]{:S(2)}) collective-permute-start(bf16[2048,256]{1,0:T(8,128)(2,1)} %broadcast_select_fusion.6.refs_2_), channel_id=1, source_target_pairs={{0,4},{4,0},{1,5},{5,1},{2,6},{6,2},{3,7},{7,3},{8,12},{12,8},{9,1... | collective-permute-start | bytes 3145736 | tf_op jit(solution)/shard_map/ppermute | solution.py:362
  661.7 42.6 %collective-permute-start.82 = (bf16[2048,256]{1,0:T(8,128)(2,1)S(1)}, bf16[2048,256]{1,0:T(8,128)(2,1)S(1)}, u32[]{:S(2)}, u32[]{:S(2)}) collective-permute-start(bf16[2048,256]{1,0:T(8,128)(2,1)S(1)} %add_convert_fusion.12.refs_2_), channel_id=1, source_target_pairs={{8,0},{16,24},{9,1},{17,25},{10,2},{18,26},{11,3},{19,27},{12,4},{... | collective-permute-start | bytes 3145736 | tf_op jit(solution)/shard_map/ppermute | solution.py:455
  (237 other events, 2532.6 us)

commit v5 on v4

--- a/solution.py
+++ b/solution.py
@@ -791,9 +791,9 @@
 S_STEPS, G_STEPS, F_STEPS = [S0, S1, S2, S3, SB, SE, SL], [G0, G1, G2, G3, GB, GE, GL], [F0, F1, F2, F3, FB, FE, FL]
 D_HOPS, U_HOPS, Q_HOPS, O_HOPS, V_HOPS = (d0, d1), (u0, u1), (q0, q1, q2), o, v
 ORDER = (
-    S3, U1, SB, S1, S2, SE, SL, D0, S0, u1, S, D1, BN, BF, d0, u1, O, ATT, d1, o, d0, u1, U0, o, d1, d0, u1, u0,
-    o, d1, Q0, d0, F3, u0, FB, F1, o, F2, q0, FE, d1, FL, Q2, F0, u0, o, Q1, q0, FN, q2, q0, q1, q2, V, u0, v,
-    q1, q2, G3, v, q0, GB, G1, G2, q1, q2, GE, GL, v, G0, v, q1, v, G,
+    S3, U1, SB, S1, S2, SE, SL, D0, S0, u1, S, D1, BN, BF, d0, u1, O, ATT, o, d1, d0, u1, U0, o, d1, d0, u1, u0,
+    o, d1, Q2, F3, d0, u0, FB, o, F1, F2, q2, d1, FE, FL, Q0, u0, o, F0, q2, Q1, q0, FN, q1, q0, q2, G3, u0, V,
+    q1, q0, v, GB, q2, G1, v, G2, q1, GE, q0, GL, v, G0, q1, v, v, G,
 )
 
 

time: 763 us -> 772 us (1.012)
  waiting for transfers between devices: 228 us -> 243 us
    ppermute x21, waiting for transfers between devices: 46.1 us -> 78.2 us  [over(): return lax.ppermute(value, 'seq', SWAP)]
    ppermute x15, waiting for transfers between devices: 75.5 us -> 58.8 us  [across(): return lax.ppermute(value, 'tensor', ACROSS)]
    unnamed x359 -> x375, local copies, waits for them, and re-layouts: 55.9 us -> 55.2 us
  transfers between devices with their start and end apart: 91 -> 91, of which waited for: 32 -> 35; matrix products, arithmetic and copies ran while one was open for 16% -> 16% of each run, Pallas kernels for 28% -> 27%
where the time goes in v5:
time: 772 us; the launch traced here: 765 us
  waiting for transfers between devices  243 us (31%)
  Pallas kernels  222 us (29%)
  other arithmetic  105 us (14%)
  starting transfers between devices  102 us (13%)
  local copies, waits for them, and re-layouts  72 us (9%)
  matrix products  12.3 us (2%)
  between operations  9.58 us (1%)
    pallas_call x29, Pallas kernels, fused(): pl.pallas_call(kernel, grid_spec=pltpu.PrefetchScalarGridSpec(num_scalar_...  125 us
    ppermute x26, waiting for transfers between devices, on_line(): return lax.ppermute(value, 'dp', pairs)  100 us
    ppermute x21, waiting for transfers between devices, over(): return lax.ppermute(value, 'seq', SWAP)  78.2 us
    pallas_call x4, Pallas kernels, _attention_call(): pl.pallas_call(kernel, out_shape=outs, in_specs=[pl.BlockSpec(memory_spac...  59.1 us
    ppermute x15, waiting for transfers between devices, across(): return lax.ppermute(value, 'tensor', ACROSS)  58.8 us
    unnamed x375, local copies, waits for them, and re-layouts  55.2 us
    ppermute x26, starting transfers between devices, on_line(): return lax.ppermute(value, 'dp', pairs)  55.1 us
    convert_element_type x30, other arithmetic, low(): return lax.optimization_barrier(value.astype(jnp.bfloat16))  38.6 us
  transfers between devices with their start and end apart: 91, of which 35 were waited for; matrix products, arithmetic and copies ran while one was open for 16% of the time, Pallas kernels for 27%

profile of v5, /device:TPU:0, one launch (start us, length us, event | category | flops | bytes accessed | tf_op | source)
XLA Modules:
  0.0 765.4 jit_solution(6854767555500755356)
XLA Ops:
  26.5 7.5 collective-permute-done.refs_0_
  67.6 16.2 %attention_forward.3 = (bf16[1024,256]{1,0:T(8,128)(2,1)S(1)}, f32[1024,128]{1,0:T(8,128)S(1)}) custom-call(s32[1]{0:T(128)} %constant.120.clone.1.first_block, s32[8]{0:T(128)S(1)} %iota_xor_fusion.place, s32[8,9]{1,0:T(8,128)S(1)} %pad_add_fusion.lists, bf16[2048,768]{1,0:T(8,128)(2,1)S(1)} %pad_maximum_fusion.2.refs_2_.qkv, ...), custom_call_target="tpu_custom_call" | custom-call | tf_op jit(solution)/shard_map/attention_forward/pallas_call | solution.py:286
  84.6 6.1 attention_forward.4
  103.4 8.7 %collective-permute-done.11.refs_1_ = bf16[128,2048]{1,0:T(8,128)(2,1)S(1)} collective-permute-done((bf16[128,2048]{1,0:T(8,128)(2,1)S(1)}, bf16[128,2048]{1,0:T(8,128)(2,1)S(1)}, u32[]{:S(2)}, u32[]{:S(2)}) %collective-permute-start.11) | collective-permute-done | bytes 524320 | tf_op jit(solution)/shard_map/ppermute | solution.py:362
  120.3 7.3 act_gradient.2
  127.6 15.4 %collective-permute-done.15.refs_0_ = bf16[256,2048]{1,0:T(8,128)(2,1)S(1)} collective-permute-done((bf16[256,2048]{1,0:T(8,128)(2,1)S(1)}, bf16[256,2048]{1,0:T(8,128)(2,1)S(1)}, u32[]{:S(2)}, u32[]{:S(2)}) %collective-permute-start.15) | collective-permute-done | bytes 1048608 | tf_op jit(solution)/shard_map/ppermute | solution.py:358
  149.1 7.1 act_gradient.3
  165.0 7.6 collective-permute-done.18.refs_0_
  238.4 13.8 %collective-permute-done.29.refs_0_ = bf16[256,2048]{1,0:T(8,128)(2,1)S(1)} collective-permute-done((bf16[256,2048]{1,0:T(8,128)(2,1)S(1)}, bf16[256,2048]{1,0:T(8,128)(2,1)S(1)}, u32[]{:S(2)}, u32[]{:S(2)}) %collective-permute-start.29) | collective-permute-done | bytes 1048608 | tf_op jit(solution)/shard_map/ppermute | solution.py:358
  258.2 6.2 down_part.2.refs_2_
  269.8 13.5 %collective-permute-done.34.refs_0_ = bf16[1024,1024]{1,0:T(8,128)(2,1)S(1)} collective-permute-done((bf16[1024,1024]{1,0:T(8,128)(2,1)S(1)}, bf16[1024,1024]{1,0:T(8,128)(2,1)S(1)}, u32[]{:S(2)}, u32[]{:S(2)}) %collective-permute-start.34) | collective-permute-done | bytes 2097184 | tf_op jit(solution)/shard_map/ppermute | solution.py:455
  338.3 7.6 collective-permute-done.39.refs_0_
  368.9 9.0 %collective-permute-done.45.refs_0_ = bf16[1024,256]{1,0:T(8,128)(2,1)S(1)} collective-permute-done((bf16[1024,256]{1,0:T(8,128)(2,1)S(1)}, bf16[1024,256]{1,0:T(8,128)(2,1)S(1)}, u32[]{:S(2)}, u32[]{:S(2)}) %collective-permute-start.45) | collective-permute-done | bytes 524320 | tf_op jit(solution)/shard_map/ppermute | solution.py:362
  380.7 32.8 %attention_backward.1.refs_2_.refs_1_.refs_0_ = bf16[2048,768]{1,0:T(8,128)(2,1)S(1)} custom-call(s32[8]{0:T(128)S(1)} %iota_xor_fusion.place, s32[8,9]{1,0:T(8,128)S(1)} %pad_add_fusion.1.lists, bf16[2048,768]{1,0:T(8,128)(2,1)S(1)} %copy-done.5, bf16[2048,256]{1,0:T(8,128)(2,1)S(1)} %pad_maximum_fusion.8.do, bf16[1024,256]{1,0:T(8,128)(2,1)S(1)} %copy-done.93, ...), custom_call_target="tpu_custom_call" | custom-call | tf_op jit(solution)/shard_map/attention_backward/pallas_call | solution.py:286
  416.7 6.9 collective-permute-start.47
  455.6 20.7 %collective-permute-done.52.refs_0_ = bf16[1024,1024]{1,0:T(8,128)(2,1)S(1)} collective-permute-done((bf16[1024,1024]{1,0:T(8,128)(2,1)S(1)}, bf16[1024,1024]{1,0:T(8,128)(2,1)S(1)}, u32[]{:S(2)}, u32[]{:S(2)}) %collective-permute-start.52) | collective-permute-done | bytes 2097184 | tf_op jit(solution)/shard_map/ppermute | solution.py:455
  478.2 7.4 collective-permute-done.50.refs_0_
  499.1 26.1 %collective-permute-done.48.refs_0_ = bf16[1024,1024]{1,0:T(8,128)(2,1)} collective-permute-done((bf16[1024,1024]{1,0:T(8,128)(2,1)}, bf16[1024,1024]{1,0:T(8,128)(2,1)}, u32[]{:S(2)}, u32[]{:S(2)}) %collective-permute-start.48) | collective-permute-done | bytes 2097184 | tf_op jit(solution)/shard_map/ppermute | solution.py:455
  571.9 11.6 %collective-permute-done.57.refs_0_ = bf16[256,2048]{1,0:T(8,128)(2,1)S(1)} collective-permute-done((bf16[256,2048]{1,0:T(8,128)(2,1)S(1)}, bf16[256,2048]{1,0:T(8,128)(2,1)S(1)}, u32[]{:S(2)}, u32[]{:S(2)}) %collective-permute-start.57) | collective-permute-done | bytes 1048608 | tf_op jit(solution)/shard_map/ppermute | solution.py:358
  629.9 14.5 %collective-permute-done.68.refs_0_ = bf16[2048,256]{1,0:T(8,128)(2,1)S(1)} collective-permute-done((bf16[2048,256]{1,0:T(8,128)(2,1)S(1)}, bf16[2048,256]{1,0:T(8,128)(2,1)S(1)}, u32[]{:S(2)}, u32[]{:S(2)}) %collective-permute-start.68) | collective-permute-done | bytes 1048608 | tf_op jit(solution)/shard_map/ppermute | solution.py:455
  660.7 11.9 %collective-permute-done.76.refs_0_ = bf16[1024,1024]{1,0:T(8,128)(2,1)S(1)} collective-permute-done((bf16[1024,1024]{1,0:T(8,128)(2,1)}, bf16[1024,1024]{1,0:T(8,128)(2,1)S(1)}, u32[]{:S(2)}, u32[]{:S(2)}) %collective-permute-start.76) | collective-permute-done | bytes 2097184 | tf_op jit(solution)/shard_map/ppermute | solution.py:362
  688.5 6.6 collective-permute-done.72.refs_0_
  724.8 15.5 %collective-permute-done.89.refs_0_ = bf16[2048,256]{1,0:T(8,128)(2,1)S(1)} collective-permute-done((bf16[2048,256]{1,0:T(8,128)(2,1)S(1)}, bf16[2048,256]{1,0:T(8,128)(2,1)S(1)}, u32[]{:S(2)}, u32[]{:S(2)}) %collective-permute-start.89) | collective-permute-done | bytes 1048608 | tf_op jit(solution)/shard_map/ppermute | solution.py:362
  746.9 14.9 %collective-permute-done.87.refs_1_ = bf16[256,2048]{1,0:T(8,128)(2,1)S(1)} collective-permute-done((bf16[256,2048]{1,0:T(8,128)(2,1)S(1)}, bf16[256,2048]{1,0:T(8,128)(2,1)S(1)}, u32[]{:S(2)}, u32[]{:S(2)}) %collective-permute-start.87) | collective-permute-done | bytes 1048608 | tf_op jit(solution)/shard_map/ppermute | solution.py:362
  (849 shorter events, 460.8 us)
Async XLA Ops:
  232.7 50.6 %collective-permute-start.34 = (bf16[1024,1024]{1,0:T(8,128)(2,1)S(1)}, bf16[1024,1024]{1,0:T(8,128)(2,1)S(1)}, u32[]{:S(2)}, u32[]{:S(2)}) collective-permute-start(bf16[1024,1024]{1,0:T(8,128)(2,1)S(1)} %up_part.2.refs_2_), channel_id=1, source_target_pairs={{0,8},{24,16},{1,9},{25,17},{2,10},{26,18},{3,11},{27,19},{4,12},{... | collective-permute-start | bytes 6291464 | tf_op jit(solution)/shard_map/ppermute | solution.py:455
  295.2 50.7 %collective-permute-start.39 = (bf16[1024,1024]{1,0:T(8,128)(2,1)}, bf16[1024,1024]{1,0:T(8,128)(2,1)}, u32[]{:S(2)}, u32[]{:S(2)}) collective-permute-start(bf16[1024,1024]{1,0:T(8,128)(2,1)} %copy-done.39), channel_id=1, source_target_pairs={{0,8},{24,16},{1,9},{25,17},{2,10},{26,18},{3,11},{27,19},{4,12},{... | collective-permute-start | bytes 6291464 | tf_op jit(solution)/shard_map/ppermute | solution.py:455
  302.3 46.8 %collective-permute-start.38 = (bf16[1024,1024]{1,0:T(8,128)(2,1)}, bf16[1024,1024]{1,0:T(8,128)(2,1)}, u32[]{:S(2)}, u32[]{:S(2)}) collective-permute-start(bf16[1024,1024]{1,0:T(8,128)(2,1)} %copy-done.27), channel_id=1, source_target_pairs={{8,16},{16,8},{9,17},{17,9},{10,18},{18,10},{11,19},{19,11},{12,20... | collective-permute-start | bytes 6291464 | tf_op jit(solution)/shard_map/ppermute | solution.py:455
  331.5 92.2 %collective-permute-start.43 = (bf16[1024,1024]{1,0:T(8,128)(2,1)S(1)}, bf16[1024,1024]{1,0:T(8,128)(2,1)S(1)}, u32[]{:S(2)}, u32[]{:S(2)}) collective-permute-start(bf16[1024,1024]{1,0:T(8,128)(2,1)S(1)} %copy-done.38), channel_id=1, source_target_pairs={{0,8},{24,16},{1,9},{25,17},{2,10},{26,18},{3,11},{27,19},{4,12},{... | collective-permute-start | bytes 6291464 | tf_op jit(solution)/shard_map/ppermute | solution.py:455
  363.4 63.3 %collective-permute-start.42 = (bf16[1024,1024]{1,0:T(8,128)(2,1)S(1)}, bf16[1024,1024]{1,0:T(8,128)(2,1)S(1)}, u32[]{:S(2)}, u32[]{:S(2)}) collective-permute-start(bf16[1024,1024]{1,0:T(8,128)(2,1)S(1)} %add_convert_fusion.6.refs_2_), channel_id=1, source_target_pairs={{8,16},{16,8},{9,17},{17,9},{10,18},{18,10},{11,19},{19,11},{12,20... | collective-permute-start | bytes 6291464 | tf_op jit(solution)/shard_map/ppermute | solution.py:455
  364.2 65.0 %collective-permute-start.41 = (bf16[1024,1024]{1,0:T(8,128)(2,1)S(1)}, bf16[1024,1024]{1,0:T(8,128)(2,1)S(1)}, u32[]{:S(2)}, u32[]{:S(2)}) collective-permute-start(bf16[1024,1024]{1,0:T(8,128)(2,1)S(1)} %add_convert_fusion.5.refs_2_), channel_id=1, source_target_pairs={{8,0},{16,24},{9,1},{17,25},{10,2},{18,26},{11,3},{19,27},{12,4},{... | collective-permute-start | bytes 6291464 | tf_op jit(solution)/shard_map/ppermute | solution.py:455
  365.5 48.0 %collective-permute-start.44 = (bf16[256,2048]{1,0:T(8,128)(2,1)}, bf16[256,2048]{1,0:T(8,128)(2,1)S(1)}, u32[]{:S(2)}, u32[]{:S(2)}) collective-permute-start(bf16[256,2048]{1,0:T(8,128)(2,1)} %out_part.2.refs_5_), channel_id=1, source_target_pairs={{0,4},{4,0},{1,5},{5,1},{2,6},{6,2},{3,7},{7,3},{8,12},{12,8},{9,1... | collective-permute-start | bytes 3145736 | tf_op jit(solution)/shard_map/ppermute | solution.py:362
  427.7 48.5 %collective-permute-start.52 = (bf16[1024,1024]{1,0:T(8,128)(2,1)S(1)}, bf16[1024,1024]{1,0:T(8,128)(2,1)S(1)}, u32[]{:S(2)}, u32[]{:S(2)}) collective-permute-start(bf16[1024,1024]{1,0:T(8,128)(2,1)S(1)} %add_convert_fusion.3.refs_2_), channel_id=1, source_target_pairs={{8,0},{16,24},{9,1},{17,25},{10,2},{18,26},{11,3},{19,27},{12,4},{... | collective-permute-start | bytes 6291464 | tf_op jit(solution)/shard_map/ppermute | solution.py:455
  431.4 46.9 %collective-permute-start.51 = (bf16[1024,1024]{1,0:T(8,128)(2,1)S(1)}, bf16[1024,1024]{1,0:T(8,128)(2,1)S(1)}, u32[]{:S(2)}, u32[]{:S(2)}) collective-permute-start(bf16[1024,1024]{1,0:T(8,128)(2,1)S(1)} %broadcast_select_fusion.3.refs_2_), channel_id=1, source_target_pairs={{0,4},{4,0},{1,5},{5,1},{2,6},{6,2},{3,7},{7,3},{8,12},{12,8},{9,1... | collective-permute-start | bytes 6291464 | tf_op jit(solution)/shard_map/ppermute | solution.py:362
  440.3 45.4 %collective-permute-start.50 = (bf16[1024,1024]{1,0:T(8,128)(2,1)S(1)}, bf16[1024,1024]{1,0:T(8,128)(2,1)S(1)}, u32[]{:S(2)}, u32[]{:S(2)}) collective-permute-start(bf16[1024,1024]{1,0:T(8,128)(2,1)S(1)} %up_part.3.refs_2_), channel_id=1, source_target_pairs={{0,8},{24,16},{1,9},{25,17},{2,10},{26,18},{3,11},{27,19},{4,12},{... | collective-permute-start | bytes 6291464 | tf_op jit(solution)/shard_map/ppermute | solution.py:455
  450.3 39.8 %collective-permute-start.49 = (bf16[256,2048]{1,0:T(8,128)(2,1)}, bf16[256,2048]{1,0:T(8,128)(2,1)}, u32[]{:S(2)}, u32[]{:S(2)}) collective-permute-start(bf16[256,2048]{1,0:T(8,128)(2,1)} %add_convert_fusion.22.refs_2_), channel_id=1, source_target_pairs={{8,16},{16,8},{9,17},{17,9},{10,18},{18,10},{11,19},{19,11},{12,20... | collective-permute-start | bytes 3145736 | tf_op jit(solution)/shard_map/ppermute | solution.py:455
  454.3 71.0 %collective-permute-start.48 = (bf16[1024,1024]{1,0:T(8,128)(2,1)}, bf16[1024,1024]{1,0:T(8,128)(2,1)}, u32[]{:S(2)}, u32[]{:S(2)}) collective-permute-start(bf16[1024,1024]{1,0:T(8,128)(2,1)} %add_convert_fusion.2.refs_2_), channel_id=1, source_target_pairs={{8,0},{16,24},{9,1},{17,25},{10,2},{18,26},{11,3},{19,27},{12,4},{... | collective-permute-start | bytes 6291464 | tf_op jit(solution)/shard_map/ppermute | solution.py:455
  477.8 62.8 %collective-permute-start.55 = (bf16[1024,1024]{1,0:T(8,128)(2,1)}, bf16[1024,1024]{1,0:T(8,128)(2,1)}, u32[]{:S(2)}, u32[]{:S(2)}) collective-permute-start(bf16[1024,1024]{1,0:T(8,128)(2,1)} %broadcast_select_fusion.2.refs_2_), channel_id=1, source_target_pairs={{0,4},{4,0},{1,5},{5,1},{2,6},{6,2},{3,7},{7,3},{8,12},{12,8},{9,1... | collective-permute-start | bytes 6291464 | tf_op jit(solution)/shard_map/ppermute | solution.py:362
  488.0 53.3 %collective-permute-start.54 = (bf16[1024,1024]{1,0:T(8,128)(2,1)}, bf16[1024,1024]{1,0:T(8,128)(2,1)}, u32[]{:S(2)}, u32[]{:S(2)}) collective-permute-start(bf16[1024,1024]{1,0:T(8,128)(2,1)} %add_convert_fusion.1.refs_2_), channel_id=1, source_target_pairs={{8,16},{16,8},{9,17},{17,9},{10,18},{18,10},{11,19},{19,11},{12,20... | collective-permute-start | bytes 6291464 | tf_op jit(solution)/shard_map/ppermute | solution.py:455
  493.7 59.4 %collective-permute-start.53 = (bf16[256,2048]{1,0:T(8,128)(2,1)S(1)}, bf16[256,2048]{1,0:T(8,128)(2,1)S(1)}, u32[]{:S(2)}, u32[]{:S(2)}) collective-permute-start(bf16[256,2048]{1,0:T(8,128)(2,1)S(1)} %add_convert_fusion.21.refs_2_), channel_id=1, source_target_pairs={{8,0},{16,24},{9,1},{17,25},{10,2},{18,26},{11,3},{19,27},{12,4},{... | collective-permute-start | bytes 3145736 | tf_op jit(solution)/shard_map/ppermute | solution.py:455
  544.6 49.9 %collective-permute-start.63 = (bf16[1024,1024]{1,0:T(8,128)(2,1)S(1)}, bf16[1024,1024]{1,0:T(8,128)(2,1)S(1)}, u32[]{:S(2)}, u32[]{:S(2)}) collective-permute-start(bf16[1024,1024]{1,0:T(8,128)(2,1)S(1)} %add_convert_fusion.refs_2_), channel_id=1, source_target_pairs={{8,0},{16,24},{9,1},{17,25},{10,2},{18,26},{11,3},{19,27},{12,4},{... | collective-permute-start | bytes 6291464 | tf_op jit(solution)/shard_map/ppermute | solution.py:455
  585.2 38.6 %collective-permute-start.70 = (bf16[256,2048]{1,0:T(8,128)(2,1)S(1)}, bf16[256,2048]{1,0:T(8,128)(2,1)S(1)}, u32[]{:S(2)}, u32[]{:S(2)}) collective-permute-start(bf16[256,2048]{1,0:T(8,128)(2,1)S(1)} %add_convert_fusion.17.refs_2_), channel_id=1, source_target_pairs={{0,4},{4,0},{1,5},{5,1},{2,6},{6,2},{3,7},{7,3},{8,12},{12,8},{9,1... | collective-permute-start | bytes 3145736 | tf_op jit(solution)/shard_map/ppermute | solution.py:362
  586.9 38.6 %collective-permute-start.69 = (bf16[256,2048]{1,0:T(8,128)(2,1)S(1)}, bf16[256,2048]{1,0:T(8,128)(2,1)S(1)}, u32[]{:S(2)}, u32[]{:S(2)}) collective-permute-start(bf16[256,2048]{1,0:T(8,128)(2,1)S(1)} %add_convert_fusion.18.refs_2_), channel_id=1, source_target_pairs={{0,2},{2,0},{1,3},{3,1},{4,6},{6,4},{5,7},{7,5},{8,10},{10,8},{9,1... | collective-permute-start | bytes 3145736 | tf_op jit(solution)/shard_map/ppermute | solution.py:358
  605.6 46.4 %collective-permute-start.65 = (bf16[2048,256]{1,0:T(8,128)(2,1)}, bf16[2048,256]{1,0:T(8,128)(2,1)}, u32[]{:S(2)}, u32[]{:S(2)}) collective-permute-start(bf16[2048,256]{1,0:T(8,128)(2,1)} %add_convert_fusion.16.refs_2_), channel_id=1, source_target_pairs={{8,0},{16,24},{9,1},{17,25},{10,2},{18,26},{11,3},{19,27},{12,4},{... | collective-permute-start | bytes 3145736 | tf_op jit(solution)/shard_map/ppermute | solution.py:455
  623.8 48.8 %collective-permute-start.76 = (bf16[1024,1024]{1,0:T(8,128)(2,1)}, bf16[1024,1024]{1,0:T(8,128)(2,1)S(1)}, u32[]{:S(2)}, u32[]{:S(2)}) collective-permute-start(bf16[1024,1024]{1,0:T(8,128)(2,1)} %broadcast_select_fusion.refs_2_), channel_id=1, source_target_pairs={{0,4},{4,0},{1,5},{5,1},{2,6},{6,2},{3,7},{7,3},{8,12},{12,8},{9,1... | collective-permute-start | bytes 6291464 | tf_op jit(solution)/shard_map/ppermute | solution.py:362
  647.5 38.9 %collective-permute-start.73 = (f32[6,2048]{1,0:T(8,128)S(1)}, f32[6,2048]{1,0:T(8,128)S(1)}, u32[]{:S(2)}, u32[]{:S(2)}) collective-permute-start(f32[6,2048]{1,0:T(8,128)S(1)} %stack.34.refs_2_), channel_id=1, source_target_pairs={{0,1},{1,0},{2,3},{3,2},{4,5},{5,4},{6,7},{7,6},{8,9},{9,8},{10,11... | collective-permute-start | bytes 147464 | tf_op jit(solution)/shard_map/ppermute | solution.py:354
  654.7 40.5 %collective-permute-start.72 = (bf16[2048,256]{1,0:T(8,128)(2,1)S(1)}, bf16[2048,256]{1,0:T(8,128)(2,1)S(1)}, u32[]{:S(2)}, u32[]{:S(2)}) collective-permute-start(bf16[2048,256]{1,0:T(8,128)(2,1)S(1)} %broadcast_select_fusion.6.refs_2_), channel_id=1, source_target_pairs={{0,4},{4,0},{1,5},{5,1},{2,6},{6,2},{3,7},{7,3},{8,12},{12,8},{9,1... | collective-permute-start | bytes 3145736 | tf_op jit(solution)/shard_map/ppermute | solution.py:362
  718.6 43.1 %collective-permute-start.87 = (bf16[256,2048]{1,0:T(8,128)(2,1)S(1)}, bf16[256,2048]{1,0:T(8,128)(2,1)S(1)}, u32[]{:S(2)}, u32[]{:S(2)}) collective-permute-start(bf16[256,2048]{1,0:T(8,128)(2,1)S(1)} %add_convert_fusion.9.refs_2_), channel_id=1, source_target_pairs={{0,4},{4,0},{1,5},{5,1},{2,6},{6,2},{3,7},{7,3},{8,12},{12,8},{9,1... | collective-permute-start | bytes 3145736 | tf_op jit(solution)/shard_map/ppermute | solution.py:362
  724.7 38.2 %collective-permute-start.85 = (bf16[256,2048]{1,0:T(8,128)(2,1)S(1)}, bf16[256,2048]{1,0:T(8,128)(2,1)S(1)}, u32[]{:S(2)}, u32[]{:S(2)}) collective-permute-start(bf16[256,2048]{1,0:T(8,128)(2,1)S(1)} %get-tuple-element.174), channel_id=1, source_target_pairs={{0,1},{1,0},{2,3},{3,2},{4,5},{5,4},{6,7},{7,6},{8,9},{9,8},{10,11... | collective-permute-start | bytes 3145736 | tf_op jit(solution)/shard_map/ppermute | solution.py:354
  (245 other events, 2611.5 us)
